TPU v7x, 256 devices: a whole 4x4x8 slice. The times are simulated.
256 devices in a mesh: gx: 8 (over z_lo, core), gy: 32 (over z_hi, y, x).
Axes of the slice: x: 4, y: 4, z: 8 (z_hi: 2, z_lo: 4; z = z_hi * 4 + z_lo), core: 2. Of those that a mesh axis runs over, the one named last changes fastest.
Arguments:
- conductivity: float32 [32, 512, 16], P('gx', 'gy'), may hold values from 0.1 to 10
- storage: float32 [32, 512, 16], P('gx', 'gy'), may hold values from 0.05 to 0.5
- head_term: float32 [32, 512, 16], P('gx', 'gy'), may hold values from -6 to 6
- zone_id: int32 [32, 512, 16], P('gx', 'gy'), may hold values from 0 to 63
- layer_count: int32 [8, 32], P('gx', 'gy'), may hold values from 4 to 16, as said below
- well_cell: int32 [8, 32, 32, 8], P('gx', 'gy'), may hold values from 0 to 1023
- well_count: int32 [8, 32, 32], P('gx', 'gy'), may hold values from 0 to 8, as said below
Outputs:
- tangent: float32 [32, 512, 1024], P('gx', 'gy')
- wells: float32 [65536, 64], P(('gx', 'gy'))
Inputs may be any that keep to these rules, and one draw needn't show every extreme that they name: `layer_count`: some subdomain has all 16 layers. `well_count`: in each subdomain row one owner receives 8 rows from every subdomain of that row.
All inputs are finite; a program needn't handle non-finite values.
Results may differ from a plain program's by a relative error of at most 0.0003.
Values sent between devices are 32-bit elements; how exact they have to be, the bound alone decides.
No kernel may reach another device: no remote copies, remote signals or barrier semaphores. Data moves between devices by JAX's collectives and lax.ppermute only.
A program may use at most 64 MiB of HBM per device.

v0:
```python
import jax
import jax.numpy as jnp
from jax import lax
from jax.sharding import PartitionSpec as P

ZONES = 64
ITERS = 3
PASSES = 4


relax_factor = 0.8


def with_halo(array, sides, width):
    for axis, dim in sides:
        devices, length = (lax.axis_size(axis), array.shape[dim])
        up = [(i, (i + 1) % devices) for i in range(devices - 1)]
        down = [(j, i) for i, j in up]
        last = lax.slice_in_dim(array, length - width, length, axis=dim)
        first = lax.slice_in_dim(array, 0, width, axis=dim)
        before = lax.ppermute(last, axis, up)
        after = lax.ppermute(first, axis, down)
        array = jnp.concatenate([before, array, after], axis=dim)
    return array


def vertical(field, stride):
    zeros = jnp.zeros_like(field[..., :stride])
    return jnp.concatenate([field[..., stride:], zeros], axis=-1) + jnp.concatenate(
        [zeros, field[..., :-stride]], axis=-1
    )


def faces_sum(grid):
    return grid[:-2, 1:-1] + grid[2:, 1:-1] + grid[1:-1, :-2] + grid[1:-1, 2:]


def corner_sum(grid):
    return grid[:-2, :-2] + grid[:-2, 2:] + grid[2:, :-2] + grid[2:, 2:]


def neighbours(padded, stride):
    paired = vertical(padded, stride)
    return (
        paired[1:-1, 1:-1]
        + faces_sum(padded)
        + 0.5 * faces_sum(paired)
        + 0.5 * corner_sum(padded)
        + 0.25 * corner_sum(paired)
    )


def cycle_pad(field, width):
    return jnp.pad(field, ((width, width), (width, width), (0, 0)))


def spread(field, count):
    return jnp.repeat(field, count, axis=-1)


def dim_weights(length, has_lower, has_upper):
    places = jnp.arange(length)
    edge = jnp.where((places == 0) | (places == length - 1), 0.5, 1.0)
    edge = jnp.where(places == 1, jnp.where(has_lower, 0.5, 1.0), edge)
    edge = jnp.where(places == length - 2, jnp.where(has_upper, 0.5, 1.0), edge)
    return edge.astype(jnp.float32)


def prepare(cond_wide, store_ext):
    cond_ext = cond_wide[1:-1, 1:-1]
    diag_ext = store_ext + cond_ext * neighbours(cond_wide, 1)
    active = (cond_ext > 0.0).astype(jnp.float32)
    inverse = active / (diag_ext + 1.0 - active)
    return (spread(cond_ext, ZONES), spread(diag_ext, ZONES), spread(inverse, ZONES))


def sweeps(residual_ext, prepared):
    cond_full, diag_full, inverse_full = prepared
    correction = jnp.zeros_like(residual_ext)
    for sweep in range(PASSES):
        applied = diag_full * correction - cond_full * neighbours(
            cycle_pad(cond_full * correction, 1), ZONES
        )
        correction = correction + relax_factor * inverse_full * (residual_ext - applied)
    return correction


def make_source(weighted, zone_float, layers):
    onehot = (zone_float[..., None] == jnp.arange(ZONES, dtype=jnp.float32)).astype(jnp.float32)
    return (onehot * weighted[..., None]).reshape(
        weighted.shape[0], weighted.shape[1], layers * ZONES
    )


def shards(conductivity, storage, head_term, zone_id, layer_count, well_cell, well_count):
    rows, cols, layers = conductivity.shape
    depth = jnp.arange(layers, dtype=jnp.int32)
    active = (depth[None, None, :] < layer_count[0, 0]).astype(jnp.float32)
    cond = jnp.sqrt(conductivity) * active
    weighted = cond * head_term
    zone_float = zone_id.astype(jnp.float32)
    coef = jnp.concatenate([cond, storage], axis=2)
    coef_wide = with_halo(coef, (("gx", 0), ("gy", 1)), 2)
    cond_wide = coef_wide[..., :layers]
    store_ext = coef_wide[1:-1, 1:-1, layers : 2 * layers]
    prepared = prepare(cond_wide, store_ext)
    cond_own = prepared[0][1:-1, 1:-1]
    diag_own = prepared[1][1:-1, 1:-1]
    source = make_source(weighted, zone_float, layers)
    row_index = lax.axis_index("gx")
    col_index = lax.axis_index("gy")
    weights = (
        dim_weights(rows + 2, row_index > 0, row_index < lax.axis_size("gx") - 1)[:, None, None]
        * dim_weights(cols + 2, col_index > 0, col_index < lax.axis_size("gy") - 1)[None, :, None]
    )
    tangent = jnp.zeros((rows, cols, layers * ZONES), jnp.float32)
    for outer in range(ITERS):
        field_ext = with_halo(tangent, (("gx", 0), ("gy", 1)), 1)
        residual = source - (
            diag_own * tangent - cond_own * neighbours(prepared[0] * field_ext, ZONES)
        )
        residual_ext = with_halo(residual, (("gx", 0), ("gy", 1)), 1)
        correction = sweeps(residual_ext, prepared) * weights
        row_edges = jnp.stack([correction[0], correction[-1]], axis=0)
        row_got = with_halo(row_edges, (("gx", 0),), 1)
        correction = correction.at[1].add(row_got[0]).at[-2].add(row_got[3])
        inner = correction[1:-1]
        col_edges = jnp.stack([inner[:, 0], inner[:, -1]], axis=1)
        col_got = with_halo(col_edges, (("gy", 1),), 1)
        update = inner[:, 1:-1].at[:, 0].add(col_got[:, 0]).at[:, -1].add(col_got[:, 3])
        tangent = tangent + update
    flat = tangent.reshape(rows * cols * layers, ZONES)
    owners = well_cell.shape[2]
    slots = well_cell.shape[3]
    cells = well_cell[0, 0].reshape(owners * slots)
    picked = jnp.take(flat, cells, axis=0).reshape(owners, slots, ZONES)
    live = (jnp.arange(slots, dtype=jnp.int32)[None, :] < well_count[0, 0][:, None]).astype(
        jnp.float32
    )
    picked = picked * live[..., None]
    arrived = lax.all_to_all(picked, "gy", split_axis=0, concat_axis=0, tiled=True)
    return (tangent, arrived.reshape(owners * slots, ZONES))


def solution(mesh):
    placed = (
        P("gx", "gy", None),
        P("gx", "gy", None),
        P("gx", "gy", None),
        P("gx", "gy", None),
        P("gx", "gy"),
        P("gx", "gy", None, None),
        P("gx", "gy", None),
    )
    return jax.shard_map(
        shards,
        mesh=mesh,
        in_specs=placed,
        out_specs=(P("gx", "gy", None), P(("gx", "gy"), None)),
        check_vma=False,
    )
```

profile of v0, /device:TPU:1, one launch (start us, length us, event | category | flops | bytes accessed | tf_op | source)
XLA Modules:
  0.0 306.6 jit_solution(10907610840047886494)
XLA Ops:
  0.7 4.9 %collective-permute-start.4 = (f32[1,16,1024]{2,1,0:T(8,128)S(1)}, f32[1,16,1024]{2,1,0:T(8,128)S(1)}, u32[]{:S(2)}, u32[]{:S(2)}) collective-permute-start(f32[1,16,1024]{2,1,0:T(8,128)S(1)} %broadcast.424), channel_id=1, source_target_pairs={{0,32},{32,64},{64,96},{96,128},{128,160},{160,192},{192,224},{1,3... | collective-permute-start | bytes 196616 | tf_op jit(solution)/shard_map/ppermute | solution.py:21
  9.1 3.6 %collective-permute-start = (f32[2,16,32]{2,1,0:T(8,128)S(1)}, f32[2,16,32]{2,1,0:T(8,128)S(1)}, u32[]{:S(2)}, u32[]{:S(2)}) collective-permute-start(f32[2,16,32]{2,1,0:T(8,128)S(1)} %get-tuple-element.237), channel_id=1, source_target_pairs={{0,32},{32,64},{64,96},{96,128},{128,160},{160,192},{192,224},{1,3... | collective-permute-start | bytes 12296 | tf_op jit(solution)/shard_map/ppermute | solution.py:21
  14.7 3.1 %collective-permute-done.1 = f32[2,16,32]{2,1,0:T(8,128)S(1)} collective-permute-done((f32[2,16,32]{2,1,0:T(8,128)S(1)}, f32[2,16,32]{2,1,0:T(8,128)S(1)}, u32[]{:S(2)}, u32[]{:S(2)}) %collective-permute-start.1) | collective-permute-done | bytes 4128 | tf_op jit(solution)/shard_map/ppermute | solution.py:22
  17.8 3.1 %collective-permute-start.2 = (f32[8,2,32]{2,1,0:T(2,128)S(1)}, f32[8,2,32]{2,1,0:T(2,128)S(1)}, u32[]{:S(2)}, u32[]{:S(2)}) collective-permute-start(f32[8,2,32]{2,1,0:T(2,128)S(1)} %get-tuple-element.235), channel_id=1, source_target_pairs={{0,1},{1,2},{2,3},{3,4},{4,5},{5,6},{6,7},{7,8},{8,9},{9,10},{10,1... | collective-permute-start | bytes 6152 | tf_op jit(solution)/shard_map/ppermute | solution.py:21
  25.7 3.2 %collective-permute-start.6 = (f32[6,1,1024]{2,1,0:T(1,128)S(1)}, f32[6,1,1024]{2,1,0:T(1,128)S(1)}, u32[]{:S(2)}, u32[]{:S(2)}) collective-permute-start(f32[6,1,1024]{2,1,0:T(1,128)S(1)} %get-tuple-element.218), channel_id=1, source_target_pairs={{0,1},{1,2},{2,3},{3,4},{4,5},{5,6},{6,7},{7,8},{8,9},{9,10},{10,1... | collective-permute-start | bytes 73736 | tf_op jit(solution)/shard_map/ppermute | solution.py:21
  35.9 4.3 %collective-permute-start.8 = (f32[1,16,1024]{2,1,0:T(8,128)S(1)}, f32[1,16,1024]{2,1,0:T(8,128)S(1)}, u32[]{:S(2)}, u32[]{:S(2)}) collective-permute-start(f32[1,16,1024]{2,1,0:T(8,128)S(1)} %get-tuple-element.228), channel_id=1, source_target_pairs={{0,32},{32,64},{64,96},{96,128},{128,160},{160,192},{192,224},{1,3... | collective-permute-start | bytes 196616 | tf_op jit(solution)/shard_map/ppermute | solution.py:21
  46.4 4.4 %collective-permute-start.10 = (f32[6,1,1024]{2,1,0:T(1,128)S(1)}, f32[6,1,1024]{2,1,0:T(1,128)S(1)}, u32[]{:S(2)}, u32[]{:S(2)}) collective-permute-start(f32[6,1,1024]{2,1,0:T(1,128)S(1)} %get-tuple-element.216), channel_id=1, source_target_pairs={{0,1},{1,2},{2,3},{3,4},{4,5},{5,6},{6,7},{7,8},{8,9},{9,10},{10,1... | collective-permute-start | bytes 73736 | tf_op jit(solution)/shard_map/ppermute | solution.py:21
  52.4 3.3 %collective-permute-done.11 = f32[6,1,1024]{2,1,0:T(1,128)S(1)} collective-permute-done((f32[6,1,1024]{2,1,0:T(1,128)S(1)}, f32[6,1,1024]{2,1,0:T(1,128)S(1)}, u32[]{:S(2)}, u32[]{:S(2)}) %collective-permute-start.11) | collective-permute-done | bytes 24608 | tf_op jit(solution)/shard_map/ppermute | solution.py:22
  67.1 4.0 %collective-permute-start.12 = (f32[1,18,1024]{2,1,0:T(8,128)S(1)}, f32[1,18,1024]{2,1,0:T(8,128)S(1)}, u32[]{:S(2)}, u32[]{:S(2)}) collective-permute-start(f32[1,18,1024]{2,1,0:T(8,128)S(1)} %slice.1718), channel_id=1, source_target_pairs={{0,32},{32,64},{64,96},{96,128},{128,160},{160,192},{192,224},{1,3... | collective-permute-start | bytes 221192 | tf_op jit(solution)/shard_map/ppermute | solution.py:21
  74.6 4.7 %collective-permute-done.13 = f32[1,18,1024]{2,1,0:T(8,128)S(1)} collective-permute-done((f32[1,18,1024]{2,1,0:T(8,128)S(1)}, f32[1,18,1024]{2,1,0:T(8,128)S(1)}, u32[]{:S(2)}, u32[]{:S(2)}) %collective-permute-start.13) | collective-permute-done | bytes 73760 | tf_op jit(solution)/shard_map/ppermute | solution.py:22
  79.4 4.5 %collective-permute-start.14 = (f32[4,1,1024]{2,1,0:T(1,128)S(1)}, f32[4,1,1024]{2,1,0:T(1,128)S(1)}, u32[]{:S(2)}, u32[]{:S(2)}) collective-permute-start(f32[4,1,1024]{2,1,0:T(1,128)S(1)} %get-tuple-element.193), channel_id=1, source_target_pairs={{0,1},{1,2},{2,3},{3,4},{4,5},{5,6},{6,7},{7,8},{8,9},{9,10},{10,1... | collective-permute-start | bytes 49160 | tf_op jit(solution)/shard_map/ppermute | solution.py:21
  85.4 3.4 %collective-permute-done.15 = f32[4,1,1024]{2,1,0:T(1,128)S(1)} collective-permute-done((f32[4,1,1024]{2,1,0:T(1,128)S(1)}, f32[4,1,1024]{2,1,0:T(1,128)S(1)}, u32[]{:S(2)}, u32[]{:S(2)}) %collective-permute-start.15) | collective-permute-done | bytes 16416 | tf_op jit(solution)/shard_map/ppermute | solution.py:22
  93.9 3.6 %collective-permute-done.17 = f32[1,16,1024]{2,1,0:T(8,128)S(1)} collective-permute-done((f32[1,16,1024]{2,1,0:T(8,128)S(1)}, f32[1,16,1024]{2,1,0:T(8,128)S(1)}, u32[]{:S(2)}, u32[]{:S(2)}) %collective-permute-start.17) | collective-permute-done | bytes 65568 | tf_op jit(solution)/shard_map/ppermute | solution.py:22
  97.6 4.0 %collective-permute-start.18 = (f32[6,1,1024]{2,1,0:T(1,128)S(1)}, f32[6,1,1024]{2,1,0:T(1,128)S(1)}, u32[]{:S(2)}, u32[]{:S(2)}) collective-permute-start(f32[6,1,1024]{2,1,0:T(1,128)S(1)} %get-tuple-element.214), channel_id=1, source_target_pairs={{0,1},{1,2},{2,3},{3,4},{4,5},{5,6},{6,7},{7,8},{8,9},{9,10},{10,1... | collective-permute-start | bytes 73736 | tf_op jit(solution)/shard_map/ppermute | solution.py:21
  103.1 3.4 %collective-permute-done.19 = f32[6,1,1024]{2,1,0:T(1,128)S(1)} collective-permute-done((f32[6,1,1024]{2,1,0:T(1,128)S(1)}, f32[6,1,1024]{2,1,0:T(1,128)S(1)}, u32[]{:S(2)}, u32[]{:S(2)}) %collective-permute-start.19) | collective-permute-done | bytes 24608 | tf_op jit(solution)/shard_map/ppermute | solution.py:22
  107.6 3.0 collective-permute-start.20
  112.6 3.6 %collective-permute-done.21 = f32[1,16,1024]{2,1,0:T(8,128)S(1)} collective-permute-done((f32[1,16,1024]{2,1,0:T(8,128)S(1)}, f32[1,16,1024]{2,1,0:T(8,128)S(1)}, u32[]{:S(2)}, u32[]{:S(2)}) %collective-permute-start.21) | collective-permute-done | bytes 65568 | tf_op jit(solution)/shard_map/ppermute | solution.py:22
  116.2 3.7 %collective-permute-start.22 = (f32[6,1,1024]{2,1,0:T(1,128)S(1)}, f32[6,1,1024]{2,1,0:T(1,128)S(1)}, u32[]{:S(2)}, u32[]{:S(2)}) collective-permute-start(f32[6,1,1024]{2,1,0:T(1,128)S(1)} %get-tuple-element.212), channel_id=1, source_target_pairs={{0,1},{1,2},{2,3},{3,4},{4,5},{5,6},{6,7},{7,8},{8,9},{9,10},{10,1... | collective-permute-start | bytes 73736 | tf_op jit(solution)/shard_map/ppermute | solution.py:21
  121.3 3.5 %collective-permute-done.23 = f32[6,1,1024]{2,1,0:T(1,128)S(1)} collective-permute-done((f32[6,1,1024]{2,1,0:T(1,128)S(1)}, f32[6,1,1024]{2,1,0:T(1,128)S(1)}, u32[]{:S(2)}, u32[]{:S(2)}) %collective-permute-start.23) | collective-permute-done | bytes 24608 | tf_op jit(solution)/shard_map/ppermute | solution.py:22
  140.5 4.7 %collective-permute-done.25 = f32[1,18,1024]{2,1,0:T(8,128)S(1)} collective-permute-done((f32[1,18,1024]{2,1,0:T(8,128)S(1)}, f32[1,18,1024]{2,1,0:T(8,128)S(1)}, u32[]{:S(2)}, u32[]{:S(2)}) %collective-permute-start.25) | collective-permute-done | bytes 73760 | tf_op jit(solution)/shard_map/ppermute | solution.py:22
  145.2 3.7 %collective-permute-start.26 = (f32[4,1,1024]{2,1,0:T(1,128)S(1)}, f32[4,1,1024]{2,1,0:T(1,128)S(1)}, u32[]{:S(2)}, u32[]{:S(2)}) collective-permute-start(f32[4,1,1024]{2,1,0:T(1,128)S(1)} %get-tuple-element.181), channel_id=1, source_target_pairs={{0,1},{1,2},{2,3},{3,4},{4,5},{5,6},{6,7},{7,8},{8,9},{9,10},{10,1... | collective-permute-start | bytes 49160 | tf_op jit(solution)/shard_map/ppermute | solution.py:21
  150.5 3.3 %collective-permute-done.27 = f32[4,1,1024]{2,1,0:T(1,128)S(1)} collective-permute-done((f32[4,1,1024]{2,1,0:T(1,128)S(1)}, f32[4,1,1024]{2,1,0:T(1,128)S(1)}, u32[]{:S(2)}, u32[]{:S(2)}) %collective-permute-start.27) | collective-permute-done | bytes 16416 | tf_op jit(solution)/shard_map/ppermute | solution.py:22
  158.9 3.6 %collective-permute-done.29 = f32[1,16,1024]{2,1,0:T(8,128)S(1)} collective-permute-done((f32[1,16,1024]{2,1,0:T(8,128)S(1)}, f32[1,16,1024]{2,1,0:T(8,128)S(1)}, u32[]{:S(2)}, u32[]{:S(2)}) %collective-permute-start.29) | collective-permute-done | bytes 65568 | tf_op jit(solution)/shard_map/ppermute | solution.py:22
  162.6 3.7 %collective-permute-start.30 = (f32[6,1,1024]{2,1,0:T(1,128)S(1)}, f32[6,1,1024]{2,1,0:T(1,128)S(1)}, u32[]{:S(2)}, u32[]{:S(2)}) collective-permute-start(f32[6,1,1024]{2,1,0:T(1,128)S(1)} %get-tuple-element.210), channel_id=1, source_target_pairs={{0,1},{1,2},{2,3},{3,4},{4,5},{5,6},{6,7},{7,8},{8,9},{9,10},{10,1... | collective-permute-start | bytes 73736 | tf_op jit(solution)/shard_map/ppermute | solution.py:21
  167.7 3.5 %collective-permute-done.31 = f32[6,1,1024]{2,1,0:T(1,128)S(1)} collective-permute-done((f32[6,1,1024]{2,1,0:T(1,128)S(1)}, f32[6,1,1024]{2,1,0:T(1,128)S(1)}, u32[]{:S(2)}, u32[]{:S(2)}) %collective-permute-start.31) | collective-permute-done | bytes 24608 | tf_op jit(solution)/shard_map/ppermute | solution.py:22
  177.3 3.6 %collective-permute-done.33 = f32[1,16,1024]{2,1,0:T(8,128)S(1)} collective-permute-done((f32[1,16,1024]{2,1,0:T(8,128)S(1)}, f32[1,16,1024]{2,1,0:T(8,128)S(1)}, u32[]{:S(2)}, u32[]{:S(2)}) %collective-permute-start.33) | collective-permute-done | bytes 65568 | tf_op jit(solution)/shard_map/ppermute | solution.py:22
  181.0 4.9 %collective-permute-start.34 = (f32[6,1,1024]{2,1,0:T(1,128)S(1)}, f32[6,1,1024]{2,1,0:T(1,128)S(1)}, u32[]{:S(2)}, u32[]{:S(2)}) collective-permute-start(f32[6,1,1024]{2,1,0:T(1,128)S(1)} %get-tuple-element.208), channel_id=1, source_target_pairs={{0,1},{1,2},{2,3},{3,4},{4,5},{5,6},{6,7},{7,8},{8,9},{9,10},{10,1... | collective-permute-start | bytes 73736 | tf_op jit(solution)/shard_map/ppermute | solution.py:21
  187.5 3.2 %collective-permute-done.35 = f32[6,1,1024]{2,1,0:T(1,128)S(1)} collective-permute-done((f32[6,1,1024]{2,1,0:T(1,128)S(1)}, f32[6,1,1024]{2,1,0:T(1,128)S(1)}, u32[]{:S(2)}, u32[]{:S(2)}) %collective-permute-start.35) | collective-permute-done | bytes 24608 | tf_op jit(solution)/shard_map/ppermute | solution.py:22
  206.5 4.7 %collective-permute-done.37 = f32[1,18,1024]{2,1,0:T(8,128)S(1)} collective-permute-done((f32[1,18,1024]{2,1,0:T(8,128)S(1)}, f32[1,18,1024]{2,1,0:T(8,128)S(1)}, u32[]{:S(2)}, u32[]{:S(2)}) %collective-permute-start.37) | collective-permute-done | bytes 73760 | tf_op jit(solution)/shard_map/ppermute | solution.py:22
  211.2 10.3 %collective-permute-start.38 = (f32[4,1,1024]{2,1,0:T(1,128)S(1)}, f32[4,1,1024]{2,1,0:T(1,128)S(1)}, u32[]{:S(2)}, u32[]{:S(2)}) collective-permute-start(f32[4,1,1024]{2,1,0:T(1,128)S(1)} %get-tuple-element.169), channel_id=1, source_target_pairs={{0,1},{1,2},{2,3},{3,4},{4,5},{5,6},{6,7},{7,8},{8,9},{9,10},{10,1... | collective-permute-start | bytes 49160 | tf_op jit(solution)/shard_map/ppermute | solution.py:21
  223.2 3.3 %collective-permute-done.39 = f32[4,1,1024]{2,1,0:T(1,128)S(1)} collective-permute-done((f32[4,1,1024]{2,1,0:T(1,128)S(1)}, f32[4,1,1024]{2,1,0:T(1,128)S(1)}, u32[]{:S(2)}, u32[]{:S(2)}) %collective-permute-start.39) | collective-permute-done | bytes 16416 | tf_op jit(solution)/shard_map/ppermute | solution.py:22
  228.4 76.1 %all_to_all.5 = f32[32,1,512]{2,1,0:T(1,128)S(1)} all-to-all(f32[32,1,512]{2,1,0:T(1,128)S(1)} %reshape.498), channel_id=1, replica_groups=mesh['gx'=8,'gy'=32] {'gy'}, dimensions={0} | all-to-all | bytes 131072 | tf_op jit(solution)/shard_map/all_to_all | solution.py:141
  (185 shorter events, 103.9 us)
Async XLA Ops:
  0.7 25.0 %collective-permute-start.4 = (f32[1,16,1024]{2,1,0:T(8,128)S(1)}, f32[1,16,1024]{2,1,0:T(8,128)S(1)}, u32[]{:S(2)}, u32[]{:S(2)}) collective-permute-start(f32[1,16,1024]{2,1,0:T(8,128)S(1)} %broadcast.424), channel_id=1, source_target_pairs={{0,32},{32,64},{64,96},{96,128},{128,160},{160,192},{192,224},{1,3... | collective-permute-start | bytes 196616 | tf_op jit(solution)/shard_map/ppermute | solution.py:21
  5.6 20.0 %collective-permute-start.5 = (f32[1,16,1024]{2,1,0:T(8,128)S(1)}, f32[1,16,1024]{2,1,0:T(8,128)S(1)}, u32[]{:S(2)}, u32[]{:S(2)}) collective-permute-start(f32[1,16,1024]{2,1,0:T(8,128)S(1)} %broadcast.424), channel_id=1, source_target_pairs={{32,0},{64,32},{96,64},{128,96},{160,128},{192,160},{224,192},{33,... | collective-permute-start | bytes 196616 | tf_op jit(solution)/shard_map/ppermute | solution.py:22
  9.1 5.6 %collective-permute-start = (f32[2,16,32]{2,1,0:T(8,128)S(1)}, f32[2,16,32]{2,1,0:T(8,128)S(1)}, u32[]{:S(2)}, u32[]{:S(2)}) collective-permute-start(f32[2,16,32]{2,1,0:T(8,128)S(1)} %get-tuple-element.237), channel_id=1, source_target_pairs={{0,32},{32,64},{64,96},{96,128},{128,160},{160,192},{192,224},{1,3... | collective-permute-start | bytes 12296 | tf_op jit(solution)/shard_map/ppermute | solution.py:21
  12.7 5.1 %collective-permute-start.1 = (f32[2,16,32]{2,1,0:T(8,128)S(1)}, f32[2,16,32]{2,1,0:T(8,128)S(1)}, u32[]{:S(2)}, u32[]{:S(2)}) collective-permute-start(f32[2,16,32]{2,1,0:T(8,128)S(1)} %get-tuple-element.238), channel_id=1, source_target_pairs={{32,0},{64,32},{96,64},{128,96},{160,128},{192,160},{224,192},{33,... | collective-permute-start | bytes 12296 | tf_op jit(solution)/shard_map/ppermute | solution.py:22
  17.8 6.7 %collective-permute-start.2 = (f32[8,2,32]{2,1,0:T(2,128)S(1)}, f32[8,2,32]{2,1,0:T(2,128)S(1)}, u32[]{:S(2)}, u32[]{:S(2)}) collective-permute-start(f32[8,2,32]{2,1,0:T(2,128)S(1)} %get-tuple-element.235), channel_id=1, source_target_pairs={{0,1},{1,2},{2,3},{3,4},{4,5},{5,6},{6,7},{7,8},{8,9},{9,10},{10,1... | collective-permute-start | bytes 6152 | tf_op jit(solution)/shard_map/ppermute | solution.py:21
  25.7 6.6 %collective-permute-start.6 = (f32[6,1,1024]{2,1,0:T(1,128)S(1)}, f32[6,1,1024]{2,1,0:T(1,128)S(1)}, u32[]{:S(2)}, u32[]{:S(2)}) collective-permute-start(f32[6,1,1024]{2,1,0:T(1,128)S(1)} %get-tuple-element.218), channel_id=1, source_target_pairs={{0,1},{1,2},{2,3},{3,4},{4,5},{5,6},{6,7},{7,8},{8,9},{9,10},{10,1... | collective-permute-start | bytes 73736 | tf_op jit(solution)/shard_map/ppermute | solution.py:21
  28.9 5.0 %collective-permute-start.7 = (f32[6,1,1024]{2,1,0:T(1,128)S(1)}, f32[6,1,1024]{2,1,0:T(1,128)S(1)}, u32[]{:S(2)}, u32[]{:S(2)}) collective-permute-start(f32[6,1,1024]{2,1,0:T(1,128)S(1)} %get-tuple-element.219), channel_id=1, source_target_pairs={{1,0},{2,1},{3,2},{4,3},{5,4},{6,5},{7,6},{8,7},{9,8},{10,9},{11,1... | collective-permute-start | bytes 73736 | tf_op jit(solution)/shard_map/ppermute | solution.py:22
  35.9 9.0 %collective-permute-start.8 = (f32[1,16,1024]{2,1,0:T(8,128)S(1)}, f32[1,16,1024]{2,1,0:T(8,128)S(1)}, u32[]{:S(2)}, u32[]{:S(2)}) collective-permute-start(f32[1,16,1024]{2,1,0:T(8,128)S(1)} %get-tuple-element.228), channel_id=1, source_target_pairs={{0,32},{32,64},{64,96},{96,128},{128,160},{160,192},{192,224},{1,3... | collective-permute-start | bytes 196616 | tf_op jit(solution)/shard_map/ppermute | solution.py:21
  40.2 5.6 %collective-permute-start.9 = (f32[1,16,1024]{2,1,0:T(8,128)S(1)}, f32[1,16,1024]{2,1,0:T(8,128)S(1)}, u32[]{:S(2)}, u32[]{:S(2)}) collective-permute-start(f32[1,16,1024]{2,1,0:T(8,128)S(1)} %get-tuple-element.229), channel_id=1, source_target_pairs={{32,0},{64,32},{96,64},{128,96},{160,128},{192,160},{224,192},{33,... | collective-permute-start | bytes 196616 | tf_op jit(solution)/shard_map/ppermute | solution.py:22
  46.4 6.0 %collective-permute-start.10 = (f32[6,1,1024]{2,1,0:T(1,128)S(1)}, f32[6,1,1024]{2,1,0:T(1,128)S(1)}, u32[]{:S(2)}, u32[]{:S(2)}) collective-permute-start(f32[6,1,1024]{2,1,0:T(1,128)S(1)} %get-tuple-element.216), channel_id=1, source_target_pairs={{0,1},{1,2},{2,3},{3,4},{4,5},{5,6},{6,7},{7,8},{8,9},{9,10},{10,1... | collective-permute-start | bytes 73736 | tf_op jit(solution)/shard_map/ppermute | solution.py:21
  50.8 4.9 %collective-permute-start.11 = (f32[6,1,1024]{2,1,0:T(1,128)S(1)}, f32[6,1,1024]{2,1,0:T(1,128)S(1)}, u32[]{:S(2)}, u32[]{:S(2)}) collective-permute-start(f32[6,1,1024]{2,1,0:T(1,128)S(1)} %get-tuple-element.217), channel_id=1, source_target_pairs={{1,0},{2,1},{3,2},{4,3},{5,4},{6,5},{7,6},{8,7},{9,8},{10,9},{11,1... | collective-permute-start | bytes 73736 | tf_op jit(solution)/shard_map/ppermute | solution.py:22
  67.1 5.6 %collective-permute-start.12 = (f32[1,18,1024]{2,1,0:T(8,128)S(1)}, f32[1,18,1024]{2,1,0:T(8,128)S(1)}, u32[]{:S(2)}, u32[]{:S(2)}) collective-permute-start(f32[1,18,1024]{2,1,0:T(8,128)S(1)} %slice.1718), channel_id=1, source_target_pairs={{0,32},{32,64},{64,96},{96,128},{128,160},{160,192},{192,224},{1,3... | collective-permute-start | bytes 221192 | tf_op jit(solution)/shard_map/ppermute | solution.py:21
  72.7 6.6 %collective-permute-start.13 = (f32[1,18,1024]{2,1,0:T(8,128)S(1)}, f32[1,18,1024]{2,1,0:T(8,128)S(1)}, u32[]{:S(2)}, u32[]{:S(2)}) collective-permute-start(f32[1,18,1024]{2,1,0:T(8,128)S(1)} %get-tuple-element.194), channel_id=1, source_target_pairs={{32,0},{64,32},{96,64},{128,96},{160,128},{192,160},{224,192},{33,... | collective-permute-start | bytes 221192 | tf_op jit(solution)/shard_map/ppermute | solution.py:22
  79.4 5.8 %collective-permute-start.14 = (f32[4,1,1024]{2,1,0:T(1,128)S(1)}, f32[4,1,1024]{2,1,0:T(1,128)S(1)}, u32[]{:S(2)}, u32[]{:S(2)}) collective-permute-start(f32[4,1,1024]{2,1,0:T(1,128)S(1)} %get-tuple-element.193), channel_id=1, source_target_pairs={{0,1},{1,2},{2,3},{3,4},{4,5},{5,6},{6,7},{7,8},{8,9},{9,10},{10,1... | collective-permute-start | bytes 49160 | tf_op jit(solution)/shard_map/ppermute | solution.py:21
  83.9 4.9 %collective-permute-start.15 = (f32[4,1,1024]{2,1,0:T(1,128)S(1)}, f32[4,1,1024]{2,1,0:T(1,128)S(1)}, u32[]{:S(2)}, u32[]{:S(2)}) collective-permute-start(f32[4,1,1024]{2,1,0:T(1,128)S(1)} %get-tuple-element.192), channel_id=1, source_target_pairs={{1,0},{2,1},{3,2},{4,3},{5,4},{6,5},{7,6},{8,7},{9,8},{10,9},{11,1... | collective-permute-start | bytes 49160 | tf_op jit(solution)/shard_map/ppermute | solution.py:22
  89.0 4.9 %collective-permute-start.16 = (f32[1,16,1024]{2,1,0:T(8,128)S(1)}, f32[1,16,1024]{2,1,0:T(8,128)S(1)}, u32[]{:S(2)}, u32[]{:S(2)}) collective-permute-start(f32[1,16,1024]{2,1,0:T(8,128)S(1)} %get-tuple-element.226), channel_id=1, source_target_pairs={{0,32},{32,64},{64,96},{96,128},{128,160},{160,192},{192,224},{1,3... | collective-permute-start | bytes 196616 | tf_op jit(solution)/shard_map/ppermute | solution.py:21
  92.0 5.6 %collective-permute-start.17 = (f32[1,16,1024]{2,1,0:T(8,128)S(1)}, f32[1,16,1024]{2,1,0:T(8,128)S(1)}, u32[]{:S(2)}, u32[]{:S(2)}) collective-permute-start(f32[1,16,1024]{2,1,0:T(8,128)S(1)} %get-tuple-element.227), channel_id=1, source_target_pairs={{32,0},{64,32},{96,64},{128,96},{160,128},{192,160},{224,192},{33,... | collective-permute-start | bytes 196616 | tf_op jit(solution)/shard_map/ppermute | solution.py:22
  97.6 5.5 %collective-permute-start.18 = (f32[6,1,1024]{2,1,0:T(1,128)S(1)}, f32[6,1,1024]{2,1,0:T(1,128)S(1)}, u32[]{:S(2)}, u32[]{:S(2)}) collective-permute-start(f32[6,1,1024]{2,1,0:T(1,128)S(1)} %get-tuple-element.214), channel_id=1, source_target_pairs={{0,1},{1,2},{2,3},{3,4},{4,5},{5,6},{6,7},{7,8},{8,9},{9,10},{10,1... | collective-permute-start | bytes 73736 | tf_op jit(solution)/shard_map/ppermute | solution.py:21
  101.6 4.9 %collective-permute-start.19 = (f32[6,1,1024]{2,1,0:T(1,128)S(1)}, f32[6,1,1024]{2,1,0:T(1,128)S(1)}, u32[]{:S(2)}, u32[]{:S(2)}) collective-permute-start(f32[6,1,1024]{2,1,0:T(1,128)S(1)} %get-tuple-element.215), channel_id=1, source_target_pairs={{1,0},{2,1},{3,2},{4,3},{5,4},{6,5},{7,6},{8,7},{9,8},{10,9},{11,1... | collective-permute-start | bytes 73736 | tf_op jit(solution)/shard_map/ppermute | solution.py:22
  107.6 5.0 %collective-permute-start.20 = (f32[1,16,1024]{2,1,0:T(8,128)S(1)}, f32[1,16,1024]{2,1,0:T(8,128)S(1)}, u32[]{:S(2)}, u32[]{:S(2)}) collective-permute-start(f32[1,16,1024]{2,1,0:T(8,128)S(1)} %get-tuple-element.224), channel_id=1, source_target_pairs={{0,32},{32,64},{64,96},{96,128},{128,160},{160,192},{192,224},{1,3... | collective-permute-start | bytes 196616 | tf_op jit(solution)/shard_map/ppermute | solution.py:21
  110.6 5.6 %collective-permute-start.21 = (f32[1,16,1024]{2,1,0:T(8,128)S(1)}, f32[1,16,1024]{2,1,0:T(8,128)S(1)}, u32[]{:S(2)}, u32[]{:S(2)}) collective-permute-start(f32[1,16,1024]{2,1,0:T(8,128)S(1)} %get-tuple-element.225), channel_id=1, source_target_pairs={{32,0},{64,32},{96,64},{128,96},{160,128},{192,160},{224,192},{33,... | collective-permute-start | bytes 196616 | tf_op jit(solution)/shard_map/ppermute | solution.py:22
  116.2 5.1 %collective-permute-start.22 = (f32[6,1,1024]{2,1,0:T(1,128)S(1)}, f32[6,1,1024]{2,1,0:T(1,128)S(1)}, u32[]{:S(2)}, u32[]{:S(2)}) collective-permute-start(f32[6,1,1024]{2,1,0:T(1,128)S(1)} %get-tuple-element.212), channel_id=1, source_target_pairs={{0,1},{1,2},{2,3},{3,4},{4,5},{5,6},{6,7},{7,8},{8,9},{9,10},{10,1... | collective-permute-start | bytes 73736 | tf_op jit(solution)/shard_map/ppermute | solution.py:21
  138.6 6.6 %collective-permute-start.25 = (f32[1,18,1024]{2,1,0:T(8,128)S(1)}, f32[1,18,1024]{2,1,0:T(8,128)S(1)}, u32[]{:S(2)}, u32[]{:S(2)}) collective-permute-start(f32[1,18,1024]{2,1,0:T(8,128)S(1)} %get-tuple-element.182), channel_id=1, source_target_pairs={{32,0},{64,32},{96,64},{128,96},{160,128},{192,160},{224,192},{33,... | collective-permute-start | bytes 221192 | tf_op jit(solution)/shard_map/ppermute | solution.py:22
  145.2 5.1 %collective-permute-start.26 = (f32[4,1,1024]{2,1,0:T(1,128)S(1)}, f32[4,1,1024]{2,1,0:T(1,128)S(1)}, u32[]{:S(2)}, u32[]{:S(2)}) collective-permute-start(f32[4,1,1024]{2,1,0:T(1,128)S(1)} %get-tuple-element.181), channel_id=1, source_target_pairs={{0,1},{1,2},{2,3},{3,4},{4,5},{5,6},{6,7},{7,8},{8,9},{9,10},{10,1... | collective-permute-start | bytes 49160 | tf_op jit(solution)/shard_map/ppermute | solution.py:21
  154.0 4.9 %collective-permute-start.28 = (f32[1,16,1024]{2,1,0:T(8,128)S(1)}, f32[1,16,1024]{2,1,0:T(8,128)S(1)}, u32[]{:S(2)}, u32[]{:S(2)}) collective-permute-start(f32[1,16,1024]{2,1,0:T(8,128)S(1)} %get-tuple-element.222), channel_id=1, source_target_pairs={{0,32},{32,64},{64,96},{96,128},{128,160},{160,192},{192,224},{1,3... | collective-permute-start | bytes 196616 | tf_op jit(solution)/shard_map/ppermute | solution.py:21
  157.0 5.6 %collective-permute-start.29 = (f32[1,16,1024]{2,1,0:T(8,128)S(1)}, f32[1,16,1024]{2,1,0:T(8,128)S(1)}, u32[]{:S(2)}, u32[]{:S(2)}) collective-permute-start(f32[1,16,1024]{2,1,0:T(8,128)S(1)} %get-tuple-element.223), channel_id=1, source_target_pairs={{32,0},{64,32},{96,64},{128,96},{160,128},{192,160},{224,192},{33,... | collective-permute-start | bytes 196616 | tf_op jit(solution)/shard_map/ppermute | solution.py:22
  162.6 5.1 %collective-permute-start.30 = (f32[6,1,1024]{2,1,0:T(1,128)S(1)}, f32[6,1,1024]{2,1,0:T(1,128)S(1)}, u32[]{:S(2)}, u32[]{:S(2)}) collective-permute-start(f32[6,1,1024]{2,1,0:T(1,128)S(1)} %get-tuple-element.210), channel_id=1, source_target_pairs={{0,1},{1,2},{2,3},{3,4},{4,5},{5,6},{6,7},{7,8},{8,9},{9,10},{10,1... | collective-permute-start | bytes 73736 | tf_op jit(solution)/shard_map/ppermute | solution.py:21
  172.3 5.0 %collective-permute-start.32 = (f32[1,16,1024]{2,1,0:T(8,128)S(1)}, f32[1,16,1024]{2,1,0:T(8,128)S(1)}, u32[]{:S(2)}, u32[]{:S(2)}) collective-permute-start(f32[1,16,1024]{2,1,0:T(8,128)S(1)} %get-tuple-element.220), channel_id=1, source_target_pairs={{0,32},{32,64},{64,96},{96,128},{128,160},{160,192},{192,224},{1,3... | collective-permute-start | bytes 196616 | tf_op jit(solution)/shard_map/ppermute | solution.py:21
  175.4 5.6 %collective-permute-start.33 = (f32[1,16,1024]{2,1,0:T(8,128)S(1)}, f32[1,16,1024]{2,1,0:T(8,128)S(1)}, u32[]{:S(2)}, u32[]{:S(2)}) collective-permute-start(f32[1,16,1024]{2,1,0:T(8,128)S(1)} %get-tuple-element.221), channel_id=1, source_target_pairs={{32,0},{64,32},{96,64},{128,96},{160,128},{192,160},{224,192},{33,... | collective-permute-start | bytes 196616 | tf_op jit(solution)/shard_map/ppermute | solution.py:22
  181.0 6.6 %collective-permute-start.34 = (f32[6,1,1024]{2,1,0:T(1,128)S(1)}, f32[6,1,1024]{2,1,0:T(1,128)S(1)}, u32[]{:S(2)}, u32[]{:S(2)}) collective-permute-start(f32[6,1,1024]{2,1,0:T(1,128)S(1)} %get-tuple-element.208), channel_id=1, source_target_pairs={{0,1},{1,2},{2,3},{3,4},{4,5},{5,6},{6,7},{7,8},{8,9},{9,10},{10,1... | collective-permute-start | bytes 73736 | tf_op jit(solution)/shard_map/ppermute | solution.py:21
  204.5 6.6 %collective-permute-start.37 = (f32[1,18,1024]{2,1,0:T(8,128)S(1)}, f32[1,18,1024]{2,1,0:T(8,128)S(1)}, u32[]{:S(2)}, u32[]{:S(2)}) collective-permute-start(f32[1,18,1024]{2,1,0:T(8,128)S(1)} %get-tuple-element.170), channel_id=1, source_target_pairs={{32,0},{64,32},{96,64},{128,96},{160,128},{192,160},{224,192},{33,... | collective-permute-start | bytes 221192 | tf_op jit(solution)/shard_map/ppermute | solution.py:22
  211.2 11.8 %collective-permute-start.38 = (f32[4,1,1024]{2,1,0:T(1,128)S(1)}, f32[4,1,1024]{2,1,0:T(1,128)S(1)}, u32[]{:S(2)}, u32[]{:S(2)}) collective-permute-start(f32[4,1,1024]{2,1,0:T(1,128)S(1)} %get-tuple-element.169), channel_id=1, source_target_pairs={{0,1},{1,2},{2,3},{3,4},{4,5},{5,6},{6,7},{7,8},{8,9},{9,10},{10,1... | collective-permute-start | bytes 49160 | tf_op jit(solution)/shard_map/ppermute | solution.py:21
  (20 other events, 72.4 us)
where the time goes:
time: 308 us; the launch traced here: 307 us
  starting transfers between devices  113 us (37%)
  blocking collectives  76.1 us (25%)
  waiting for transfers between devices  66.6 us (22%)
  other arithmetic  32.4 us (11%)
  local copies, waits for them, and re-layouts  15.9 us (5%)
    ppermute x20, starting transfers between devices, with_halo(): before = lax.ppermute(last, axis, up)  80.6 us
    all_to_all x1, blocking collectives, shards(): lax.all_to_all(picked, 'gy', split_axis=0, concat_axis=0, tiled=True)  76.1 us
    ppermute x20, waiting for transfers between devices, with_halo(): after = lax.ppermute(first, axis, down)  61.9 us
    ppermute x20, starting transfers between devices, with_halo(): after = lax.ppermute(first, axis, down)  32.5 us
    mul x10, other arithmetic, sweeps(): cond_full * correction  19.1 us
    mul x3, other arithmetic, shards(): correction = sweeps(residual_ext, prepared) * weights  7.96 us
  transfers between devices with their start and end apart: 40, of which 22 were waited for; matrix products, arithmetic and copies ran while one was open for 3% of the time, Pallas kernels for 0%

commit v1 on v0

v1 whole, which is shorter than its diff:
```python
import jax
import jax.numpy as jnp
from jax import lax
from jax.experimental import pallas as pl
from jax.experimental.pallas import tpu as pltpu
from jax.sharding import PartitionSpec as P

ROWS, COLS, LAYERS, ZONES = 4, 16, 16, 64
HALO = 12
WIDE = COLS + 2 * HALO
PAIRS = WIDE // 2
SUBX, SUBY = 8, 32
GROUP = ZONES // SUBX
TILE = (SUBX, LAYERS * GROUP)
STEP = 3
RELAX = 0.8


def total(first, second):
    return first if second is None else second if first is None else first + second


def lane_places():
    return lax.broadcasted_iota(jnp.int32, TILE, 1)


def sub_places():
    return lax.broadcasted_iota(jnp.int32, TILE, 0)


def up_sub(field):
    return jnp.where(sub_places() == 0, 0.0, pltpu.roll(field, 1, 0))


def down_sub(field):
    return jnp.where(sub_places() == SUBX - 1, 0.0, pltpu.roll(field, SUBX - 1, 0))


def layers_sum(field):
    lanes = lane_places()
    above = jnp.where(lanes >= TILE[1] - GROUP, 0.0, pltpu.roll(field, TILE[1] - GROUP, 1))
    below = jnp.where(lanes < GROUP, 0.0, pltpu.roll(field, GROUP, 1))
    return (field + above) + (field + below)


def rows_sum(cells):
    pairs = [total(a, b) for a, b in zip(cells[:-1], cells[1:])]
    return [total(a, b) for a, b in zip(pairs[:-1], pairs[1:])]


def column_loop(first, last, column, emit):
    before = column(first - 1)
    here = column(first)
    pair = [a + b for a, b in zip(before, here)]

    def one(col, here, pair):
        after = column(col + 1)
        next_pair = [a + b for a, b in zip(here, after)]
        emit(col, [a + b for a, b in zip(pair, next_pair)])
        return after, next_pair

    count = last + 1 - first
    groups = count // STEP

    def body(index, carry):
        here, pair = carry
        for inner in range(STEP):
            here, pair = one(first + index * STEP + inner, here, pair)
        return here, pair

    if groups > 1:
        here, pair = lax.fori_loop(0, groups, body, (here, pair))
        first = first + groups * STEP
    for col in range(first, last + 1):
        here, pair = one(col, here, pair)


def expand(raw, cond, store, head, zone):
    lanes = lane_places()
    picks = [[side * 64 + part * LAYERS + lanes // GROUP for part in range(4)] for side in range(2)]

    def body(index, carry):
        for side in range(2):
            col = 2 * index + side
            conds = []
            for row in range(ROWS):
                packed = raw[pl.ds(row * PAIRS + index, SUBX, stride=ROWS * PAIRS), :]
                parts = [
                    jnp.take_along_axis(packed, places, axis=1, mode="promise_in_bounds")
                    for places in picks[side]
                ]
                conds.append(parts[0])
                store[col, row] = parts[1]
                head[col, row] = parts[2]
                zone[col, row] = parts[3]
            for row, field in enumerate([up_sub(conds[-1])] + conds + [down_sub(conds[0])]):
                cond[col, row] = field
        return carry

    lax.fori_loop(0, PAIRS, body, 0)


def coefficients(zone_base, cond, store, head, zone, keep, gain, source):
    wanted = (zone_base + lane_places() % GROUP).astype(jnp.float32)

    def column(col):
        sums = rows_sum([cond[col, row] for row in range(ROWS + 2)])
        return [layers_sum(field) for field in sums]

    def emit(col, around):
        keeps, gains, sources = [], [], []
        for row in range(ROWS):
            here = cond[col, row + 1]
            near = here * (0.25 * around[row])
            diag = store[col, row] + (near - 2.0 * here * here)
            active = jnp.where(here > 0.0, 1.0, 0.0)
            step = RELAX * (active / (diag + 1.0 - active))
            scaled = step * here * here
            keeps.append(1.0 - step * (store[col, row] + near))
            gains.append(0.25 * scaled)
            sources.append(jnp.where(zone[col, row] == wanted, scaled * head[col, row], 0.0))
        for target, fields in ((keep, keeps), (gain, gains), (source, sources)):
            for row, field in enumerate([up_sub(fields[-1])] + fields + [down_sub(fields[0])]):
                target[col, row] = field

    column_loop(1, WIDE - 2, column, emit)


def main_kernel(info, raw, out, cond, store, head, zone, keep, gain, source, state, *buffers):
    expand(raw, cond, store, head, zone)
    coefficients(info[0], cond, store, head, zone, keep, gain, source)
    has_left, has_right = info[1] > 0, info[2] > 0
    left_own = jnp.where(has_left, 0.5, 1.0)
    right_own = jnp.where(has_right, 0.5, 1.0)
    subs = sub_places()
    low_own = jnp.where(subs == 0, 1.0, 0.5)
    high_own = jnp.where(subs == SUBX - 1, 1.0, 0.5)
    high = HALO + COLS
    bases = (0, HALO - 2, high - 2)
    ends = (HALO + 1, high + 1, WIDE - 1)
    rims = ((HALO + 1,), (HALO - 2, high + 1), (high - 2,))
    fields = tuple((buffers[2 * k], buffers[2 * k + 1]) for k in range(3))
    zeros = jnp.zeros(TILE, jnp.float32)

    for outer in range(3):
        reach = 4 * (2 - outer)
        for part in range(3):
            for buffer in fields[part]:
                for col in rims[part]:
                    for row in range(6):
                        buffer[col - bases[part], row] = zeros if outer == 0 else state[col, row + 1]
        for sweep in range(4):
            more = reach + 3 - sweep
            ranges = (
                (HALO - more, HALO),
                (HALO - 1, high) if more > 0 else (HALO, high - 1),
                (high - 1, high - 1 + more),
            )
            for part in range(3):
                base = bases[part]
                old, new = fields[part][(sweep + 1) % 2], fields[part][sweep % 2]
                first, last = ranges[part]
                if outer == 0 and sweep == 0:
                    def copy(col, carry, new=new, base=base):
                        for row in range(6):
                            new[col - base, row] = source[col, row]
                        return carry
                    lax.fori_loop(first, last + 1, copy, 0)
                    continue

                def column(col, old=old, base=base, sweep=sweep, outer=outer):
                    if sweep == 0:
                        cells = [state[col, row] for row in range(8)]
                    else:
                        cells = [old[col - base, row] for row in range(6)]
                        if outer == 0:
                            cells = [None] + cells + [None]
                        else:
                            cells = [state[col, 0]] + cells + [state[col, 7]]
                    return [layers_sum(field) for field in rows_sum(cells)]

                def emit(col, around, old=old, new=new, base=base, sweep=sweep):
                    for row in range(6):
                        here = state[col, row + 1] if sweep == 0 else old[col - base, row]
                        new[col - base, row] = (
                            source[col, row] + keep[col, row] * here + gain[col, row] * around[row]
                        )

                column_loop(first, last, column, emit)

        done = tuple(fields[part][1] for part in range(3))

        def merge(col, cells, final):
            mine = [
                low_own * cells[1] + (1.0 - low_own) * pltpu.roll(cells[5], 1, 0),
                cells[2],
                cells[3],
                high_own * cells[4] + (1.0 - high_own) * pltpu.roll(cells[0], SUBX - 1, 0),
            ]
            if final:
                for row in range(ROWS):
                    here = cond[col, row + 1]
                    inside = here > 0.0
                    value = jnp.where(inside, mine[row] / jnp.where(inside, here, 1.0), 0.0)
                    out[pl.ds(row * COLS + col - HALO, SUBX, stride=ROWS * COLS), :] = value
            else:
                for row in range(ROWS):
                    state[col, row + 2] = mine[row]
                state[col, 0] = up_sub(mine[2])
                state[col, 1] = up_sub(mine[3])
                state[col, 6] = down_sub(mine[0])
                state[col, 7] = down_sub(mine[1])

        def merge_range(first, last, part):
            def body(col, carry):
                merge(col, [done[part][col - bases[part], row] for row in range(6)], outer == 2)
                return carry
            lax.fori_loop(first, last + 1, body, 0)

        def merge_mixed(col, part, own):
            cells = [
                own * done[1][col - bases[1], row] + (1.0 - own) * done[part][col - bases[part], row]
                for row in range(6)
            ]
            merge(col, cells, outer == 2)

        lefts = (HALO - 1, HALO) if outer < 2 else (HALO,)
        rights = (high - 1, high) if outer < 2 else (high - 1,)
        for col in lefts:
            merge_mixed(col, 0, left_own)
        for col in rights:
            merge_mixed(col, 2, right_own)
        merge_range(HALO + 1, high - 2, 1)
        if outer < 2:
            merge_range(HALO - reach, HALO - 2, 0)
            merge_range(high + 1, high - 1 + reach, 2)


def run_main(info, raw):
    def cells(cols, rows):
        return pltpu.VMEM((cols, rows) + TILE, jnp.float32)

    scratch = [cells(WIDE, 6)] + [cells(WIDE, ROWS)] * 3 + [cells(WIDE, 6)] * 3 + [cells(WIDE, 8)]
    scratch += [cells(HALO + 2, 6)] * 2 + [cells(COLS + 4, 6)] * 2 + [cells(HALO + 2, 6)] * 2
    return pl.pallas_call(
        main_kernel,
        out_shape=jax.ShapeDtypeStruct((SUBX * ROWS * COLS, TILE[1]), jnp.float32),
        in_specs=[pl.BlockSpec(memory_space=pltpu.SMEM), pl.BlockSpec(memory_space=pltpu.VMEM)],
        out_specs=pl.BlockSpec(memory_space=pltpu.VMEM),
        scratch_shapes=scratch,
        compiler_params=pltpu.CompilerParams(vmem_limit_bytes=40 * 1024 * 1024),
        name="schwarz",
    )(info, raw)


def place_kernel(parts, tangent):
    lanes = lane_places()
    rows = ROWS * COLS

    def body(index, carry):
        start = pl.multiple_of(index * 8, 8)
        blocks = [parts[pl.ds(pl.multiple_of(a * rows + index * 8, 8), 8), :] for a in range(SUBX)]
        for pair in range(LAYERS // 2):
            places = (2 * pair + lanes // ZONES) * GROUP + lanes % GROUP
            whole = jnp.zeros(TILE, jnp.float32)
            for a in range(SUBX):
                moved = jnp.take_along_axis(blocks[a], places, axis=1, mode="promise_in_bounds")
                whole = jnp.where((lanes % ZONES) // GROUP == a, moved, whole)
            tangent[pl.ds(start, 8), pair * 128 : (pair + 1) * 128] = whole
        return carry

    lax.fori_loop(0, rows // 8, body, 0)


def run_place(parts):
    return pl.pallas_call(
        place_kernel,
        out_shape=jax.ShapeDtypeStruct((ROWS * COLS, LAYERS * ZONES), jnp.float32),
        in_specs=[pl.BlockSpec(memory_space=pltpu.VMEM)],
        out_specs=pl.BlockSpec(memory_space=pltpu.VMEM),
        name="place",
    )(parts)


def gather_inputs(conductivity, storage, head_term, zone_id, layer_count):
    depth = jnp.arange(LAYERS, dtype=jnp.int32)
    active = (depth[None, None, :] < layer_count[0, 0]).astype(jnp.float32)
    cond = jnp.sqrt(conductivity) * active
    fields = jnp.concatenate([cond, storage, head_term, zone_id.astype(jnp.float32)], axis=2)
    even = lax.axis_index("gy") % 2 == 0
    inner = [(i, i ^ 1) for i in range(SUBY)]
    outer = [(i, i + 1) for i in range(1, SUBY - 1, 2)]
    outer = outer + [(j, i) for i, j in outer]
    first, last = fields[:, :HALO], fields[:, COLS - HALO :]
    got_inner = lax.ppermute(jnp.where(even, last, first), "gy", inner)
    got_outer = lax.ppermute(jnp.where(even, first, last), "gy", outer)
    left = jnp.where(even, got_outer, got_inner)
    right = jnp.where(even, got_inner, got_outer)
    wide = jnp.concatenate([left, fields, right], axis=1).reshape(ROWS * PAIRS, 128)
    copies = jnp.broadcast_to(wide[None], (SUBX,) + wide.shape)
    gathered = lax.all_to_all(copies, "gx", 0, 0, tiled=True)
    return gathered.reshape(SUBX * ROWS * PAIRS, 128)


def shards(conductivity, storage, head_term, zone_id, layer_count, well_cell, well_count):
    raw = gather_inputs(conductivity, storage, head_term, zone_id, layer_count)
    row, col = lax.axis_index("gx"), lax.axis_index("gy")
    info = jnp.stack([row * GROUP, col, SUBY - 1 - col]).astype(jnp.int32)
    parts = run_main(info, raw).reshape(SUBX, ROWS * COLS, 128)
    parts = lax.all_to_all(parts, "gx", 0, 0, tiled=True)
    tangent = run_place(parts.reshape(SUBX * ROWS * COLS, 128)).reshape(ROWS, COLS, LAYERS * ZONES)
    flat = tangent.reshape(ROWS * COLS * LAYERS, ZONES)
    owners, slots = well_cell.shape[2:]
    cells = well_cell[0, 0].reshape(owners * slots)
    picked = jnp.take(flat, cells, axis=0).reshape(owners, slots, ZONES)
    live = jnp.arange(slots, dtype=jnp.int32)[None, :] < well_count[0, 0][:, None]
    picked = jnp.where(live[..., None], picked, 0.0)
    arrived = lax.all_to_all(picked, "gy", split_axis=0, concat_axis=0, tiled=True)
    return (tangent, arrived.reshape(owners * slots, ZONES))


def solution(mesh):
    placed = (
        P("gx", "gy", None),
        P("gx", "gy", None),
        P("gx", "gy", None),
        P("gx", "gy", None),
        P("gx", "gy"),
        P("gx", "gy", None, None),
        P("gx", "gy", None),
    )
    return jax.shard_map(
        shards,
        mesh=mesh,
        in_specs=placed,
        out_specs=(P("gx", "gy", None), P(("gx", "gy"), None)),
        check_vma=False,
    )
```

time: 308 us -> 95.7 us (0.31)
  starting transfers between devices: 113 us -> 17.4 us
  blocking collectives: 76.1 us -> 24.5 us
  waiting for transfers between devices: 66.6 us -> 18.3 us
  other arithmetic: 32.4 us -> 1.33 us
  Pallas kernels: 0 us -> 24.1 us
  local copies, waits for them, and re-layouts: 15.9 us -> 7.97 us
    ppermute x40 -> x2, starting transfers between devices: 113 us -> 5.25 us  [the longest x1 4.58 us: gather_inputs(): got_inner = lax.ppermute(jnp.where(even, last, first), 'gy', inner)]
    ppermute x40 -> x2, waiting for transfers between devices: 66.6 us -> 1.3 us  [the longest x1 1.3 us: gather_inputs(): got_inner = lax.ppermute(jnp.where(even, last, first), 'gy', inner)]
    all_to_all x1, blocking collectives: 76.1 us -> 24.5 us  [shards(): lax.all_to_all(picked, 'gy', split_axis=0, concat_axis=0, tiled=True)]
    mul x19 -> x1, other arithmetic: 28.4 us -> 0.01 us  [gather_inputs(): cond = jnp.sqrt(conductivity) * active]
    pallas_call x0 -> x2, Pallas kernels: none -> 24.1 us  [the longest x1 21 us: run_main(): pl.pallas_call(main_kernel, out_shape=jax.ShapeDtypeStruct((SUBX * ROWS *...]
    all_to_all x0 -> x2, waiting for transfers between devices: none -> 17 us  [the longest x1 8.99 us: gather_inputs(): gathered = lax.all_to_all(copies, 'gx', 0, 0, tiled=True)]
    all_to_all x0 -> x2, starting transfers between devices: none -> 12.2 us  [the longest x1 7.72 us: gather_inputs(): gathered = lax.all_to_all(copies, 'gx', 0, 0, tiled=True)]
    slice x28 -> x0, local copies, waits for them, and re-layouts: 3.64 us -> none  [the longest x11 2.73 us: vertical(): field[..., stride:]]
  transfers between devices with their start and end apart: 40 -> 4, of which waited for: 22 -> 3; matrix products, arithmetic and copies ran while one was open for 3% -> 0% of each run, Pallas kernels for 0% -> 0%
where the time goes in v1:
time: 95.7 us; the launch traced here: 95 us
  blocking collectives  24.5 us (26%)
  Pallas kernels  24.1 us (25%)
  waiting for transfers between devices  18.3 us (19%)
  starting transfers between devices  17.4 us (18%)
  local copies, waits for them, and re-layouts  7.97 us (8%)
  between operations  1.4 us (1%)
  other arithmetic  1.33 us (1%)
    all_to_all x1, blocking collectives, shards(): lax.all_to_all(picked, 'gy', split_axis=0, concat_axis=0, tiled=True)  24.5 us
    pallas_call x1, Pallas kernels, run_main(): pl.pallas_call(main_kernel, out_shape=jax.ShapeDtypeStruct((SUBX * ROWS *...  21 us
    all_to_all x1, waiting for transfers between devices, gather_inputs(): gathered = lax.all_to_all(copies, 'gx', 0, 0, tiled=True)  8.99 us
    all_to_all x1, waiting for transfers between devices, shards(): parts = lax.all_to_all(parts, 'gx', 0, 0, tiled=True)  7.98 us
    all_to_all x1, starting transfers between devices, gather_inputs(): gathered = lax.all_to_all(copies, 'gx', 0, 0, tiled=True)  7.72 us
    unnamed x18, local copies, waits for them, and re-layouts  4.63 us
    ppermute x1, starting transfers between devices, gather_inputs(): got_inner = lax.ppermute(jnp.where(even, last, first), 'gy', inner)  4.58 us
    all_to_all x1, starting transfers between devices, shards(): parts = lax.all_to_all(parts, 'gx', 0, 0, tiled=True)  4.44 us
  transfers between devices with their start and end apart: 4, of which 3 were waited for; matrix products, arithmetic and copies ran while one was open for 0% of the time, Pallas kernels for 0%

profile of v1, /device:TPU:1, one launch (start us, length us, event | category | flops | bytes accessed | tf_op | source)
XLA Modules:
  0.0 95.0 jit_solution(2827915356127902366)
XLA Ops:
  1.3 0.1 copy-done.3
  1.4 0.8 copy-done.4
  2.2 0.7 copy-done.1
  2.9 0.1 pad_maximum_fusion.1
  3.0 0.7 collective-permute-start
  3.7 4.6 %collective-permute-start.1 = (f32[4,12,64]{2,1,0:T(8,128)S(1)}, f32[4,12,64]{2,1,0:T(8,128)S(1)}, u32[]{:S(2)}, u32[]{:S(2)}) collective-permute-start(f32[4,12,64]{2,1,0:T(8,128)S(1)} %get-tuple-element.7), channel_id=1, source_target_pairs={{0,1},{1,0},{2,3},{3,2},{4,5},{5,4},{6,7},{7,6},{8,9},{9,8},{10,11... | collective-permute-start | bytes 36872 | tf_op jit(solution)/shard_map/ppermute | solution.py:295
  8.3 1.3 %collective-permute-done.1 = f32[4,12,64]{2,1,0:T(8,128)S(1)} collective-permute-done((f32[4,12,64]{2,1,0:T(8,128)S(1)}, f32[4,12,64]{2,1,0:T(8,128)S(1)}, u32[]{:S(2)}, u32[]{:S(2)}) %collective-permute-start.1) | collective-permute-done | bytes 12320 | tf_op jit(solution)/shard_map/ppermute | solution.py:295
  9.6 0.1 pad_maximum_fusion
  9.7 0.1 broadcast_in_dim.32
  9.8 0.8 broadcast_in_dim.33
  10.5 7.7 %all-to-all-start = ((f32[8,80,128]{2,1,0:T(8,128)}), f32[8,80,128]{2,1,0:T(8,128)S(1)}, u32[]{:S(2)}, u32[]{:S(2)}) async-start(f32[8,80,128]{2,1,0:T(8,128)} %broadcast_in_dim.33), calls=%async_computation | async-start | bytes 655360 | tf_op jit(solution)/shard_map/all_to_all | solution.py:301
  18.3 0.7 copy-done.5
  19.0 0.1 copy.12
  19.0 0.1 reshape_squeeze.6
  19.1 0.1 copy.11
  19.2 0.1 pad_add_fusion.info
  19.3 9.0 %all-to-all-done = f32[8,80,128]{2,1,0:T(8,128)S(1)} async-done(((f32[8,80,128]{2,1,0:T(8,128)}), f32[8,80,128]{2,1,0:T(8,128)S(1)}, u32[]{:S(2)}, u32[]{:S(2)}) %all-to-all-start) | async-done | bytes 327712 | tf_op jit(solution)/shard_map/all_to_all | solution.py:301
  28.3 21.0 %schwarz.1 = f32[512,128]{1,0:T(8,128)} custom-call(s32[3]{0:T(128)S(1)} %pad_add_fusion.info, f32[640,128]{1,0:T(8,128)S(1)} %bitcast.22), custom_call_target="tpu_custom_call" | custom-call | tf_op jit(solution)/shard_map/schwarz/pallas_call | solution.py:245
  49.3 4.4 %all-to-all-start.1 = ((f32[8,64,128]{2,1,0:T(8,128)}), f32[8,64,128]{2,1,0:T(8,128)S(1)}, u32[]{:S(2)}, u32[]{:S(2)}) async-start(f32[8,64,128]{2,1,0:T(8,128)} %bitcast.5), calls=%async_computation.1 | async-start | bytes 524288 | tf_op jit(solution)/shard_map/all_to_all | solution.py:310
  53.7 0.6 copy-done.6
  54.5 8.0 %all-to-all-done.1 = f32[8,64,128]{2,1,0:T(8,128)S(1)} async-done(((f32[8,64,128]{2,1,0:T(8,128)}), f32[8,64,128]{2,1,0:T(8,128)S(1)}, u32[]{:S(2)}, u32[]{:S(2)}) %all-to-all-start.1) | async-done | bytes 262176 | tf_op jit(solution)/shard_map/all_to_all | solution.py:310
  62.4 0.7 copy-done
  63.1 3.1 %place.1 = f32[64,1024]{1,0:T(8,128)} custom-call(f32[512,128]{1,0:T(8,128)} %bitcast.24), custom_call_target="tpu_custom_call" | custom-call | tf_op jit(solution)/shard_map/place/pallas_call | solution.py:276
  66.2 1.1 %reshape_reshape.3 = f32[1024,64]{1,0:T(8,128)S(1)} reshape(f32[64,1024]{1,0:T(8,128)} %place.1) | data formatting | bytes 524288 | tf_op jit(solution)/shard_map/reshape;reshape | solution.py:312
  67.3 0.7 gather_fusion
  68.1 0.1 fusion
  68.2 0.1 reshape.105
  68.3 24.5 %all_to_all.15 = f32[32,1,512]{2,1,0:T(1,128)S(1)} all-to-all(f32[32,1,512]{2,1,0:T(1,128)S(1)} %reshape.105), channel_id=1, replica_groups=mesh['gx'=8,'gy'=32] {'gy'}, dimensions={0} | all-to-all | bytes 131072 | tf_op jit(solution)/shard_map/all_to_all | solution.py:318
  92.9 0.5 broadcast.54
  93.4 0.8 reduce
  94.2 0.1 reshape.106
  94.3 0.7 copy.13
  (18 shorter events, 0.2 us)
Async XLA Ops:
  0.6 0.8 copy-start.3
  1.4 0.8 copy-start.4
  2.1 0.8 copy-start.1
  2.1 0.8 copy-start.2
  3.0 5.3 %collective-permute-start = (f32[4,12,64]{2,1,0:T(8,128)S(1)}, f32[4,12,64]{2,1,0:T(8,128)S(1)}, u32[]{:S(2)}, u32[]{:S(2)}) collective-permute-start(f32[4,12,64]{2,1,0:T(8,128)S(1)} %get-tuple-element.6), channel_id=1, source_target_pairs={{1,2},{3,4},{5,6},{7,8},{9,10},{11,12},{13,14},{15,16},{17,18},{19... | collective-permute-start | bytes 36872 | tf_op jit(solution)/shard_map/ppermute | solution.py:296
  3.7 5.9 %collective-permute-start.1 = (f32[4,12,64]{2,1,0:T(8,128)S(1)}, f32[4,12,64]{2,1,0:T(8,128)S(1)}, u32[]{:S(2)}, u32[]{:S(2)}) collective-permute-start(f32[4,12,64]{2,1,0:T(8,128)S(1)} %get-tuple-element.7), channel_id=1, source_target_pairs={{0,1},{1,0},{2,3},{3,2},{4,5},{5,4},{6,7},{7,6},{8,9},{9,8},{10,11... | collective-permute-start | bytes 36872 | tf_op jit(solution)/shard_map/ppermute | solution.py:295
  10.5 17.7 %all-to-all-start = ((f32[8,80,128]{2,1,0:T(8,128)}), f32[8,80,128]{2,1,0:T(8,128)S(1)}, u32[]{:S(2)}, u32[]{:S(2)}) async-start(f32[8,80,128]{2,1,0:T(8,128)} %broadcast_in_dim.33), calls=%async_computation | async-start | bytes 655360 | tf_op jit(solution)/shard_map/all_to_all | solution.py:301
  18.3 0.7 copy-start.5
  49.3 13.2 %all-to-all-start.1 = ((f32[8,64,128]{2,1,0:T(8,128)}), f32[8,64,128]{2,1,0:T(8,128)S(1)}, u32[]{:S(2)}, u32[]{:S(2)}) async-start(f32[8,64,128]{2,1,0:T(8,128)} %bitcast.5), calls=%async_computation.1 | async-start | bytes 524288 | tf_op jit(solution)/shard_map/all_to_all | solution.py:310
  53.7 0.7 copy-start.6
  62.4 0.7 copy-start

commit v2 on v1

--- a/solution.py
+++ b/solution.py
@@ -10,9 +10,9 @@
 WIDE = COLS + 2 * HALO
 PAIRS = WIDE // 2
 SUBX, SUBY = 8, 32
+CAP = 8
 GROUP = ZONES // SUBX
 TILE = (SUBX, LAYERS * GROUP)
-STEP = 3
 RELAX = 0.8
 
 
@@ -59,18 +59,6 @@
         emit(col, [a + b for a, b in zip(pair, next_pair)])
         return after, next_pair
 
-    count = last + 1 - first
-    groups = count // STEP
-
-    def body(index, carry):
-        here, pair = carry
-        for inner in range(STEP):
-            here, pair = one(first + index * STEP + inner, here, pair)
-        return here, pair
-
-    if groups > 1:
-        here, pair = lax.fori_loop(0, groups, body, (here, pair))
-        first = first + groups * STEP
     for col in range(first, last + 1):
         here, pair = one(col, here, pair)
 
@@ -97,7 +85,7 @@
                 cond[col, row] = field
         return carry
 
-    lax.fori_loop(0, PAIRS, body, 0)
+    lax.fori_loop(0, PAIRS, body, 0, unroll=True)
 
 
 def coefficients(zone_base, cond, store, head, zone, keep, gain, source):
@@ -126,9 +114,17 @@
     column_loop(1, WIDE - 2, column, emit)
 
 
-def main_kernel(info, raw, out, cond, store, head, zone, keep, gain, source, state, *buffers):
+def collect(me, mine, other, raw):
+    block = ROWS * PAIRS
+    for place in range(SUBX):
+        piece = (mine if place % 2 == 0 else other)[pl.ds((place // 2) * block, block), :]
+        raw[pl.ds(pl.multiple_of((me ^ place) * block, 8), block), :] = piece
+
+
+def main_kernel(info, mine, other, out, raw, cond, store, head, zone, keep, gain, source, state, *buffers):
+    collect(info[0], mine, other, raw)
     expand(raw, cond, store, head, zone)
-    coefficients(info[0], cond, store, head, zone, keep, gain, source)
+    coefficients(info[0] * GROUP, cond, store, head, zone, keep, gain, source)
     has_left, has_right = info[1] > 0, info[2] > 0
     left_own = jnp.where(has_left, 0.5, 1.0)
     right_own = jnp.where(has_right, 0.5, 1.0)
@@ -165,7 +161,7 @@
                         for row in range(6):
                             new[col - base, row] = source[col, row]
                         return carry
-                    lax.fori_loop(first, last + 1, copy, 0)
+                    lax.fori_loop(first, last + 1, copy, 0, unroll=True)
                     continue
 
                 def column(col, old=old, base=base, sweep=sweep, outer=outer):
@@ -215,7 +211,7 @@
             def body(col, carry):
                 merge(col, [done[part][col - bases[part], row] for row in range(6)], outer == 2)
                 return carry
-            lax.fori_loop(first, last + 1, body, 0)
+            lax.fori_loop(first, last + 1, body, 0, unroll=True)
 
         def merge_mixed(col, part, own):
             cells = [
@@ -236,24 +232,24 @@
             merge_range(high + 1, high - 1 + reach, 2)
 
 
-def run_main(info, raw):
+def run_main(info, mine, other):
     def cells(cols, rows):
         return pltpu.VMEM((cols, rows) + TILE, jnp.float32)
 
-    scratch = [cells(WIDE, 6)] + [cells(WIDE, ROWS)] * 3 + [cells(WIDE, 6)] * 3 + [cells(WIDE, 8)]
+    scratch = [pltpu.VMEM((SUBX * ROWS * PAIRS, 128), jnp.float32), cells(WIDE, 6)] + [cells(WIDE, ROWS)] * 3 + [cells(WIDE, 6)] * 3 + [cells(WIDE, 8)]
     scratch += [cells(HALO + 2, 6)] * 2 + [cells(COLS + 4, 6)] * 2 + [cells(HALO + 2, 6)] * 2
     return pl.pallas_call(
         main_kernel,
         out_shape=jax.ShapeDtypeStruct((SUBX * ROWS * COLS, TILE[1]), jnp.float32),
-        in_specs=[pl.BlockSpec(memory_space=pltpu.SMEM), pl.BlockSpec(memory_space=pltpu.VMEM)],
+        in_specs=[pl.BlockSpec(memory_space=pltpu.SMEM)] + [pl.BlockSpec(memory_space=pltpu.VMEM)] * 2,
         out_specs=pl.BlockSpec(memory_space=pltpu.VMEM),
         scratch_shapes=scratch,
         compiler_params=pltpu.CompilerParams(vmem_limit_bytes=40 * 1024 * 1024),
         name="schwarz",
-    )(info, raw)
-
-
-def place_kernel(parts, tangent):
+    )(info, mine, other)
+
+
+def place_kernel(cells, counts, parts, tangent, picks, table):
     lanes = lane_places()
     rows = ROWS * COLS
 
@@ -267,19 +263,67 @@
                 moved = jnp.take_along_axis(blocks[a], places, axis=1, mode="promise_in_bounds")
                 whole = jnp.where((lanes % ZONES) // GROUP == a, moved, whole)
             tangent[pl.ds(start, 8), pair * 128 : (pair + 1) * 128] = whole
+            table[pl.ds(pl.multiple_of(pair * rows + index * 8, 8), 8), :] = whole
         return carry
 
-    lax.fori_loop(0, rows // 8, body, 0)
-
-
-def run_place(parts):
+    lax.fori_loop(0, rows // 8, body, 0, unroll=2)
+    upper = lax.broadcasted_iota(jnp.int32, (1, 128), 1) >= ZONES
+
+    def fetch(owner, slot, want):
+        cell = cells[slot, owner]
+        layer = cell % LAYERS
+        line = table[pl.ds((layer // 2) * rows + cell // LAYERS, 1), :]
+        line = jnp.where(layer % 2 == want, line, pltpu.roll(line, ZONES, 1))
+        return jnp.where(slot < counts[owner], line, 0.0)
+
+    def pick(owner, carry):
+        lines = []
+        for slot in range(CAP // 2):
+            lines.append(jnp.where(upper, fetch(owner, slot + CAP // 2, 1), fetch(owner, slot, 0)))
+        for slot, line in enumerate(lines):
+            picks[pl.ds(owner * (CAP // 2) + slot, 1), :] = line
+        return carry
+
+    lax.fori_loop(0, SUBY, pick, 0, unroll=4)
+
+
+def run_place(cells, counts, parts):
     return pl.pallas_call(
         place_kernel,
-        out_shape=jax.ShapeDtypeStruct((ROWS * COLS, LAYERS * ZONES), jnp.float32),
+        out_shape=(
+            jax.ShapeDtypeStruct((ROWS * COLS, LAYERS * ZONES), jnp.float32),
+            jax.ShapeDtypeStruct((SUBY * CAP // 2, 128), jnp.float32),
+        ),
+        in_specs=[pl.BlockSpec(memory_space=pltpu.SMEM)] * 2 + [pl.BlockSpec(memory_space=pltpu.VMEM)],
+        out_specs=(pl.BlockSpec(memory_space=pltpu.VMEM),) * 2,
+        scratch_shapes=[pltpu.VMEM((ROWS * COLS * LAYERS // 2, 128), jnp.float32)],
+        name="place",
+    )(cells, counts, parts)
+
+
+def finish_kernel(arrived, wells):
+    across = arrived[...].T
+    lanes = lane_places()
+    for start in range(0, ZONES, 8):
+        low, high = across[start : start + 8], across[ZONES + start : ZONES + start + 8]
+        for half in range(2):
+            places = (half * 16 + lanes // CAP) * (CAP // 2) + lanes % (CAP // 2)
+            both = [
+                jnp.take_along_axis(part, places, axis=1, mode="promise_in_bounds") for part in (low, high)
+            ]
+            wells[start : start + 8, half * 128 : (half + 1) * 128] = jnp.where(
+                lanes % CAP < CAP // 2, both[0], both[1]
+            )
+
+
+def run_finish(arrived):
+    return pl.pallas_call(
+        finish_kernel,
+        out_shape=jax.ShapeDtypeStruct((ZONES, SUBY * CAP), jnp.float32),
         in_specs=[pl.BlockSpec(memory_space=pltpu.VMEM)],
         out_specs=pl.BlockSpec(memory_space=pltpu.VMEM),
-        name="place",
-    )(parts)
+        name="finish",
+    )(arrived)
 
 
 def gather_inputs(conductivity, storage, head_term, zone_id, layer_count):
@@ -297,26 +341,27 @@
     left = jnp.where(even, got_outer, got_inner)
     right = jnp.where(even, got_inner, got_outer)
     wide = jnp.concatenate([left, fields, right], axis=1).reshape(ROWS * PAIRS, 128)
-    copies = jnp.broadcast_to(wide[None], (SUBX,) + wide.shape)
-    gathered = lax.all_to_all(copies, "gx", 0, 0, tiled=True)
-    return gathered.reshape(SUBX * ROWS * PAIRS, 128)
+    blocks = [wide]
+    for shift in (2, 4, 6):
+        blocks.append(lax.ppermute(wide, "gx", [(i, i ^ shift) for i in range(SUBX)]))
+    mine = jnp.concatenate(blocks, axis=0)
+    other = lax.ppermute(mine, "gx", [(i, i ^ 1) for i in range(SUBX)])
+    return mine, other
 
 
 def shards(conductivity, storage, head_term, zone_id, layer_count, well_cell, well_count):
-    raw = gather_inputs(conductivity, storage, head_term, zone_id, layer_count)
+    mine, other = gather_inputs(conductivity, storage, head_term, zone_id, layer_count)
     row, col = lax.axis_index("gx"), lax.axis_index("gy")
-    info = jnp.stack([row * GROUP, col, SUBY - 1 - col]).astype(jnp.int32)
-    parts = run_main(info, raw).reshape(SUBX, ROWS * COLS, 128)
+    info = jnp.stack([row, col, SUBY - 1 - col]).astype(jnp.int32)
+    parts = run_main(info, mine, other).reshape(SUBX, ROWS * COLS, 128)
     parts = lax.all_to_all(parts, "gx", 0, 0, tiled=True)
-    tangent = run_place(parts.reshape(SUBX * ROWS * COLS, 128)).reshape(ROWS, COLS, LAYERS * ZONES)
-    flat = tangent.reshape(ROWS * COLS * LAYERS, ZONES)
-    owners, slots = well_cell.shape[2:]
-    cells = well_cell[0, 0].reshape(owners * slots)
-    picked = jnp.take(flat, cells, axis=0).reshape(owners, slots, ZONES)
-    live = jnp.arange(slots, dtype=jnp.int32)[None, :] < well_count[0, 0][:, None]
-    picked = jnp.where(live[..., None], picked, 0.0)
-    arrived = lax.all_to_all(picked, "gy", split_axis=0, concat_axis=0, tiled=True)
-    return (tangent, arrived.reshape(owners * slots, ZONES))
+    tangent, picks = run_place(
+        well_cell[0, 0].T, well_count[0, 0], parts.reshape(SUBX * ROWS * COLS, 128)
+    )
+    picks = picks.reshape(SUBY, CAP // 2, 128)
+    arrived = lax.all_to_all(picks, "gy", split_axis=0, concat_axis=0, tiled=True)
+    wells = run_finish(arrived.reshape(SUBY * CAP // 2, 128)).T
+    return (tangent.reshape(ROWS, COLS, LAYERS * ZONES), wells)
 
 
 def solution(mesh):

time: 95.7 us -> 76.4 us (0.80)
  blocking collectives: 24.5 us -> 37.1 us
  waiting for transfers between devices: 18.3 us -> 5.7 us
  Pallas kernels: 24.1 us -> 16.4 us
  local copies, waits for them, and re-layouts: 7.97 us -> 1.68 us
  starting transfers between devices: 17.4 us -> 13.3 us
  other arithmetic: 1.33 us -> 0.31 us
    all_to_all x2 -> x0, waiting for transfers between devices: 17 us -> none  [the longest x1 8.99 us: gather_inputs(): gathered = lax.all_to_all(copies, 'gx', 0, 0, tiled=True)]
    pallas_call x1, Pallas kernels: 21 us -> 8.16 us  [run_main(): pl.pallas_call(main_kernel, out_shape=jax.ShapeDtypeStruct((SUBX * ROWS *...]
    all_to_all x1 -> x2, blocking collectives: 24.5 us -> 37.1 us  [the longest x1 24.8 us: shards(): lax.all_to_all(picks, 'gy', split_axis=0, concat_axis=0, tiled=True)]
    all_to_all x2 -> x0, starting transfers between devices: 12.2 us -> none  [the longest x1 7.72 us: gather_inputs(): gathered = lax.all_to_all(copies, 'gx', 0, 0, tiled=True)]
    ppermute x0 -> x4, starting transfers between devices: none -> 8.03 us  [the longest x3 4.77 us: gather_inputs(): lax.ppermute(wide, 'gx', [(i, i ^ shift) for i in range(SUBX)])]
    pallas_call x1 -> x2, Pallas kernels: 3.1 us -> 8.23 us  [the longest x1 6.51 us: run_place(): pl.pallas_call(place_kernel, out_shape=(jax.ShapeDtypeStruct((ROWS * COLS...]
    ppermute x0 -> x4, waiting for transfers between devices: none -> 4.4 us  [the longest x3 3.44 us: gather_inputs(): lax.ppermute(wide, 'gx', [(i, i ^ shift) for i in range(SUBX)])]
    unnamed x18 -> x11, local copies, waits for them, and re-layouts: 4.63 us -> 1.6 us
  transfers between devices with their start and end apart: 4 -> 6, of which waited for: 3 -> 4; matrix products, arithmetic and copies ran while one was open for 0% -> 0% of each run, Pallas kernels for 0% -> 0%
where the time goes in v2:
time: 76.4 us; the launch traced here: 75.9 us
  blocking collectives  37.1 us (49%)
  Pallas kernels  16.4 us (21%)
  starting transfers between devices  13.3 us (17%)
  waiting for transfers between devices  5.7 us (7%)
  local copies, waits for them, and re-layouts  1.68 us (2%)
  between operations  1.37 us (2%)
    all_to_all x1, blocking collectives, shards(): lax.all_to_all(picks, 'gy', split_axis=0, concat_axis=0, tiled=True)  24.8 us
    all_to_all x1, blocking collectives, shards(): parts = lax.all_to_all(parts, 'gx', 0, 0, tiled=True)  12.3 us
    pallas_call x1, Pallas kernels, run_main(): pl.pallas_call(main_kernel, out_shape=jax.ShapeDtypeStruct((SUBX * ROWS *...  8.16 us
    pallas_call x1, Pallas kernels, run_place(): pl.pallas_call(place_kernel, out_shape=(jax.ShapeDtypeStruct((ROWS * COLS...  6.51 us
    ppermute x3, starting transfers between devices, gather_inputs(): lax.ppermute(wide, 'gx', [(i, i ^ shift) for i in range(SUBX)])  4.77 us
    ppermute x1, starting transfers between devices, gather_inputs(): got_inner = lax.ppermute(jnp.where(even, last, first), 'gy', inner)  4.58 us
    ppermute x3, waiting for transfers between devices, gather_inputs(): lax.ppermute(wide, 'gx', [(i, i ^ shift) for i in range(SUBX)])  3.44 us
    ppermute x1, starting transfers between devices, gather_inputs(): other = lax.ppermute(mine, 'gx', [(i, i ^ 1) for i in range(SUBX)])  3.26 us
  transfers between devices with their start and end apart: 6, of which 4 were waited for; matrix products, arithmetic and copies ran while one was open for 0% of the time, Pallas kernels for 0%

profile of v2, /device:TPU:1, one launch (start us, length us, event | category | flops | bytes accessed | tf_op | source)
XLA Modules:
  0.0 75.9 jit_solution(13816590834960720013)
XLA Ops:
  0.6 0.0 copy-start.2
  1.3 0.1 copy-done.2
  1.4 0.0 copy-start.3
  1.4 0.8 copy-done.3
  2.1 0.0 copy-start
  2.1 0.0 copy-start.1
  2.2 0.7 copy-done
  2.9 0.0 copy-done.1
  2.9 0.1 pad_maximum_fusion.1
  3.0 0.7 collective-permute-start
  3.7 4.6 %collective-permute-start.1 = (f32[4,12,64]{2,1,0:T(8,128)S(1)}, f32[4,12,64]{2,1,0:T(8,128)S(1)}, u32[]{:S(2)}, u32[]{:S(2)}) collective-permute-start(f32[4,12,64]{2,1,0:T(8,128)S(1)} %get-tuple-element.9), channel_id=1, source_target_pairs={{0,1},{1,0},{2,3},{3,2},{4,5},{5,4},{6,7},{7,6},{8,9},{9,8},{10,11... | collective-permute-start | bytes 36872 | tf_op jit(solution)/shard_map/ppermute | solution.py:339
  8.3 0.0 collective-permute-done
  8.3 1.3 %collective-permute-done.1 = f32[4,12,64]{2,1,0:T(8,128)S(1)} collective-permute-done((f32[4,12,64]{2,1,0:T(8,128)S(1)}, f32[4,12,64]{2,1,0:T(8,128)S(1)}, u32[]{:S(2)}, u32[]{:S(2)}) %collective-permute-start.1) | collective-permute-done | bytes 12320 | tf_op jit(solution)/shard_map/ppermute | solution.py:339
  9.6 0.1 pad_maximum_fusion
  9.7 0.1 reshape.29
  9.8 4.4 %collective-permute-start.4 = (f32[80,128]{1,0:T(8,128)S(1)}, f32[80,128]{1,0:T(8,128)S(1)}, u32[]{:S(2)}, u32[]{:S(2)}) collective-permute-start(f32[80,128]{1,0:T(8,128)S(1)} %reshape.29), channel_id=1, source_target_pairs={{0,192},{32,224},{64,128},{96,160},{128,64},{160,96},{192,0},{224,... | collective-permute-start | bytes 122888 | tf_op jit(solution)/shard_map/ppermute | solution.py:346
  14.2 0.0 collective-permute-start.3
  14.2 0.4 collective-permute-start.2
  14.6 2.8 %collective-permute-done.2 = f32[80,128]{1,0:T(8,128)S(1)} collective-permute-done((f32[80,128]{1,0:T(8,128)S(1)}, f32[80,128]{1,0:T(8,128)S(1)}, u32[]{:S(2)}, u32[]{:S(2)}) %collective-permute-start.2) | collective-permute-done | bytes 40992 | tf_op jit(solution)/shard_map/ppermute | solution.py:346
  17.3 0.7 collective-permute-done.3
  18.0 0.0 collective-permute-done.4
  18.0 3.3 %collective-permute-start.5 = (f32[320,128]{1,0:T(8,128)S(1)}, f32[320,128]{1,0:T(8,128)S(1)}, u32[]{:S(2)}, u32[]{:S(2)}) collective-permute-start(f32[320,128]{1,0:T(8,128)S(1)} %constant_dynamic-update-slice_fusion.mine), channel_id=1, source_target_pairs={{0,32},{32,0},{64,96},{96,64},{128,160},{160,128},{192,224},{224,1... | collective-permute-start | bytes 491528 | tf_op jit(solution)/shard_map/ppermute | solution.py:348
  21.3 0.1 pad_add_fusion.info
  21.4 1.0 %collective-permute-done.5.other = f32[320,128]{1,0:T(8,128)S(1)} collective-permute-done((f32[320,128]{1,0:T(8,128)S(1)}, f32[320,128]{1,0:T(8,128)S(1)}, u32[]{:S(2)}, u32[]{:S(2)}) %collective-permute-start.5) | collective-permute-done | bytes 163872 | tf_op jit(solution)/shard_map/ppermute | solution.py:348
  22.3 8.2 %schwarz.1 = f32[512,128]{1,0:T(8,128)S(1)} custom-call(s32[3]{0:T(128)S(1)} %pad_add_fusion.info, f32[320,128]{1,0:T(8,128)S(1)} %constant_dynamic-update-slice_fusion.mine, f32[320,128]{1,0:T(8,128)S(1)} %collective-permute-done.5.other), custom_call_target="tpu_custom_call" | custom-call | tf_op jit(solution)/shard_map/schwarz/pallas_call | solution.py:241
  30.5 12.3 %all_to_all.10 = f32[8,64,128]{2,1,0:T(8,128)} all-to-all(f32[8,64,128]{2,1,0:T(8,128)S(1)} %bitcast.15), channel_id=1, replica_groups=mesh['gx'=8,'gy'=32] {'gx'}, dimensions={0} | all-to-all | bytes 524288 | tf_op jit(solution)/shard_map/all_to_all | solution.py:357
  42.8 6.5 %place.1 = (f32[64,1024]{1,0:T(8,128)}, f32[128,128]{1,0:T(8,128)}) custom-call(s32[8,32]{1,0:T(8,128)} %bitcast.20, s32[32]{0:T(128)} %bitcast.21, f32[512,128]{1,0:T(8,128)} %bitcast.16), custom_call_target="tpu_custom_call" | custom-call | tf_op jit(solution)/shard_map/place/pallas_call | solution.py:291
  49.3 24.8 %all_to_all.11 = f32[32,4,128]{2,1,0:T(4,128)} all-to-all(f32[32,4,128]{2,1,0:T(4,128)} %bitcast.19), channel_id=1, replica_groups=mesh['gx'=8,'gy'=32] {'gy'}, dimensions={0} | all-to-all | bytes 131072 | tf_op jit(solution)/shard_map/all_to_all | solution.py:362
  74.2 1.7 %finish.1 = f32[64,256]{1,0:T(8,128)} custom-call(f32[128,128]{1,0:T(8,128)} %bitcast.17), custom_call_target="tpu_custom_call" | custom-call | tf_op jit(solution)/shard_map/finish/pallas_call | solution.py:320
  (9 shorter events, 0.1 us)
Async XLA Ops:
  0.6 0.8 %copy-start.2 = (s32[4,16,16]{2,1,0:T(8,128)S(1)}, s32[4,16,16]{2,1,0:T(8,128)}, u32[]{:S(2)}) copy-start(s32[4,16,16]{2,1,0:T(8,128)} %param.10) | copy-start | bytes 12292
  1.4 0.8 copy-start.3
  2.1 0.8 copy-start
  2.1 0.8 %copy-start.1 = (f32[4,16,16]{2,1,0:T(8,128)S(1)}, f32[4,16,16]{2,1,0:T(8,128)}, u32[]{:S(2)}) copy-start(f32[4,16,16]{2,1,0:T(8,128)} %param.8) | copy-start | bytes 12292
  3.0 5.3 %collective-permute-start = (f32[4,12,64]{2,1,0:T(8,128)S(1)}, f32[4,12,64]{2,1,0:T(8,128)S(1)}, u32[]{:S(2)}, u32[]{:S(2)}) collective-permute-start(f32[4,12,64]{2,1,0:T(8,128)S(1)} %get-tuple-element.8), channel_id=1, source_target_pairs={{1,2},{3,4},{5,6},{7,8},{9,10},{11,12},{13,14},{15,16},{17,18},{19... | collective-permute-start | bytes 36872 | tf_op jit(solution)/shard_map/ppermute | solution.py:340
  3.7 5.9 %collective-permute-start.1 = (f32[4,12,64]{2,1,0:T(8,128)S(1)}, f32[4,12,64]{2,1,0:T(8,128)S(1)}, u32[]{:S(2)}, u32[]{:S(2)}) collective-permute-start(f32[4,12,64]{2,1,0:T(8,128)S(1)} %get-tuple-element.9), channel_id=1, source_target_pairs={{0,1},{1,0},{2,3},{3,2},{4,5},{5,4},{6,7},{7,6},{8,9},{9,8},{10,11... | collective-permute-start | bytes 36872 | tf_op jit(solution)/shard_map/ppermute | solution.py:339
  9.8 8.2 %collective-permute-start.4 = (f32[80,128]{1,0:T(8,128)S(1)}, f32[80,128]{1,0:T(8,128)S(1)}, u32[]{:S(2)}, u32[]{:S(2)}) collective-permute-start(f32[80,128]{1,0:T(8,128)S(1)} %reshape.29), channel_id=1, source_target_pairs={{0,192},{32,224},{64,128},{96,160},{128,64},{160,96},{192,0},{224,... | collective-permute-start | bytes 122888 | tf_op jit(solution)/shard_map/ppermute | solution.py:346
  14.2 3.8 %collective-permute-start.3 = (f32[80,128]{1,0:T(8,128)S(1)}, f32[80,128]{1,0:T(8,128)S(1)}, u32[]{:S(2)}, u32[]{:S(2)}) collective-permute-start(f32[80,128]{1,0:T(8,128)S(1)} %reshape.29), channel_id=1, source_target_pairs={{0,128},{32,160},{64,192},{96,224},{128,0},{160,32},{192,64},{224,... | collective-permute-start | bytes 122888 | tf_op jit(solution)/shard_map/ppermute | solution.py:346
  14.2 3.1 %collective-permute-start.2 = (f32[80,128]{1,0:T(8,128)S(1)}, f32[80,128]{1,0:T(8,128)S(1)}, u32[]{:S(2)}, u32[]{:S(2)}) collective-permute-start(f32[80,128]{1,0:T(8,128)S(1)} %reshape.29), channel_id=1, source_target_pairs={{0,64},{32,96},{64,0},{96,32},{128,192},{160,224},{192,128},{224,1... | collective-permute-start | bytes 122888 | tf_op jit(solution)/shard_map/ppermute | solution.py:346
  18.0 4.3 %collective-permute-start.5 = (f32[320,128]{1,0:T(8,128)S(1)}, f32[320,128]{1,0:T(8,128)S(1)}, u32[]{:S(2)}, u32[]{:S(2)}) collective-permute-start(f32[320,128]{1,0:T(8,128)S(1)} %constant_dynamic-update-slice_fusion.mine), channel_id=1, source_target_pairs={{0,32},{32,0},{64,96},{96,64},{128,160},{160,128},{192,224},{224,1... | collective-permute-start | bytes 491528 | tf_op jit(solution)/shard_map/ppermute | solution.py:348

commit v3 on v2

--- a/solution.py
+++ b/solution.py
@@ -8,7 +8,10 @@
 ROWS, COLS, LAYERS, ZONES = 4, 16, 16, 64
 HALO = 12
 WIDE = COLS + 2 * HALO
-PAIRS = WIDE // 2
+HALF = COLS // 2
+OWN = ROWS * HALF
+BLOCK = 3 * OWN
+PLACES = ROWS * COLS
 SUBX, SUBY = 8, 32
 CAP = 8
 GROUP = ZONES // SUBX
@@ -63,29 +66,49 @@
         here, pair = one(col, here, pair)
 
 
-def expand(raw, cond, store, head, zone):
+def pack_kernel(layers, conductivity, storage, head, zone, own):
+    live = lax.broadcasted_iota(jnp.int32, (HALF, LAYERS), 1) < layers[0, 0]
+    for row in range(ROWS):
+        parts = []
+        for half in range(2):
+            cols = slice(half * HALF, (half + 1) * HALF)
+            parts.append(jnp.where(live, jnp.sqrt(conductivity[row, cols, :]), 0.0))
+            parts.append(storage[row, cols, :])
+            parts.append(head[row, cols, :])
+            parts.append(zone[row, cols, :].astype(jnp.float32))
+        own[row * HALF : (row + 1) * HALF, :] = jnp.concatenate(parts, axis=1)
+
+
+def run_pack(layers, conductivity, storage, head, zone):
+    return pl.pallas_call(
+        pack_kernel,
+        out_shape=jax.ShapeDtypeStruct((OWN, 128), jnp.float32),
+        in_specs=[pl.BlockSpec(memory_space=pltpu.SMEM)] + [pl.BlockSpec(memory_space=pltpu.VMEM)] * 4,
+        out_specs=pl.BlockSpec(memory_space=pltpu.VMEM),
+        name="pack",
+    )(layers, conductivity, storage, head, zone)
+
+
+def expand(odd, raw, cond, store, head, zone):
     lanes = lane_places()
-    picks = [[side * 64 + part * LAYERS + lanes // GROUP for part in range(4)] for side in range(2)]
-
-    def body(index, carry):
-        for side in range(2):
-            col = 2 * index + side
-            conds = []
-            for row in range(ROWS):
-                packed = raw[pl.ds(row * PAIRS + index, SUBX, stride=ROWS * PAIRS), :]
-                parts = [
-                    jnp.take_along_axis(packed, places, axis=1, mode="promise_in_bounds")
-                    for places in picks[side]
-                ]
-                conds.append(parts[0])
-                store[col, row] = parts[1]
-                head[col, row] = parts[2]
-                zone[col, row] = parts[3]
-            for row, field in enumerate([up_sub(conds[-1])] + conds + [down_sub(conds[0])]):
-                cond[col, row] = field
-        return carry
-
-    lax.fori_loop(0, PAIRS, body, 0, unroll=True)
+    picks = [[half * 64 + part * LAYERS + lanes // GROUP for part in range(4)] for half in range(2)]
+    bases = (2 * OWN - odd * OWN, 0, OWN + odd * OWN)
+
+    for col in range(WIDE):
+        block, place = divmod(col - HALO + COLS, COLS)
+        conds = []
+        for row in range(ROWS):
+            packed = raw[pl.ds(bases[block] + row * HALF + place % HALF, SUBX, stride=BLOCK), :]
+            parts = [
+                jnp.take_along_axis(packed, places, axis=1, mode="promise_in_bounds")
+                for places in picks[place // HALF]
+            ]
+            conds.append(parts[0])
+            store[col, row] = parts[1]
+            head[col, row] = parts[2]
+            zone[col, row] = parts[3]
+        for row, field in enumerate([up_sub(conds[-1])] + conds + [down_sub(conds[0])]):
+            cond[col, row] = field
 
 
 def coefficients(zone_base, cond, store, head, zone, keep, gain, source):
@@ -115,15 +138,14 @@
 
 
 def collect(me, mine, other, raw):
-    block = ROWS * PAIRS
     for place in range(SUBX):
-        piece = (mine if place % 2 == 0 else other)[pl.ds((place // 2) * block, block), :]
-        raw[pl.ds(pl.multiple_of((me ^ place) * block, 8), block), :] = piece
-
-
-def main_kernel(info, mine, other, out, raw, cond, store, head, zone, keep, gain, source, state, *buffers):
+        piece = (mine if place % 2 == 0 else other)[pl.ds((place // 2) * BLOCK, BLOCK), :]
+        raw[pl.ds(pl.multiple_of((me ^ place) * BLOCK, 8), BLOCK), :] = piece
+
+
+def main_kernel(info, mine, other, out0, out2, out4, out6, out, raw, cond, store, head, zone, keep, gain, source, state, *buffers):
     collect(info[0], mine, other, raw)
-    expand(raw, cond, store, head, zone)
+    expand(info[1] & 1, raw, cond, store, head, zone)
     coefficients(info[0] * GROUP, cond, store, head, zone, keep, gain, source)
     has_left, has_right = info[1] > 0, info[2] > 0
     left_own = jnp.where(has_left, 0.5, 1.0)
@@ -231,74 +253,89 @@
             merge_range(HALO - reach, HALO - 2, 0)
             merge_range(high + 1, high - 1 + reach, 2)
 
+    for place in range(SUBX):
+        target = (out0, out2, out4, out6)[place // 2]
+        chunk = out[pl.ds(pl.multiple_of((info[0] ^ place) * PLACES, 8), PLACES), :]
+        target[(place % 2) * PLACES : (place % 2 + 1) * PLACES, :] = chunk
+
 
 def run_main(info, mine, other):
     def cells(cols, rows):
         return pltpu.VMEM((cols, rows) + TILE, jnp.float32)
 
-    scratch = [pltpu.VMEM((SUBX * ROWS * PAIRS, 128), jnp.float32), cells(WIDE, 6)] + [cells(WIDE, ROWS)] * 3 + [cells(WIDE, 6)] * 3 + [cells(WIDE, 8)]
+    scratch = [pltpu.VMEM((SUBX * rows, 128), jnp.float32) for rows in (PLACES, BLOCK)] + [cells(WIDE, 6)] + [cells(WIDE, ROWS)] * 3 + [cells(WIDE, 6)] * 3 + [cells(WIDE, 8)]
     scratch += [cells(HALO + 2, 6)] * 2 + [cells(COLS + 4, 6)] * 2 + [cells(HALO + 2, 6)] * 2
     return pl.pallas_call(
         main_kernel,
-        out_shape=jax.ShapeDtypeStruct((SUBX * ROWS * COLS, TILE[1]), jnp.float32),
+        out_shape=(jax.ShapeDtypeStruct((2 * PLACES, TILE[1]), jnp.float32),) * 4,
         in_specs=[pl.BlockSpec(memory_space=pltpu.SMEM)] + [pl.BlockSpec(memory_space=pltpu.VMEM)] * 2,
-        out_specs=pl.BlockSpec(memory_space=pltpu.VMEM),
+        out_specs=(pl.BlockSpec(memory_space=pltpu.VMEM),) * 4,
         scratch_shapes=scratch,
         compiler_params=pltpu.CompilerParams(vmem_limit_bytes=40 * 1024 * 1024),
         name="schwarz",
     )(info, mine, other)
 
 
-def place_kernel(cells, counts, parts, tangent, picks, table):
+def swap_blocks(fields):
     lanes = lane_places()
-    rows = ROWS * COLS
-
-    def body(index, carry):
-        start = pl.multiple_of(index * 8, 8)
-        blocks = [parts[pl.ds(pl.multiple_of(a * rows + index * 8, 8), 8), :] for a in range(SUBX)]
-        for pair in range(LAYERS // 2):
-            places = (2 * pair + lanes // ZONES) * GROUP + lanes % GROUP
-            whole = jnp.zeros(TILE, jnp.float32)
-            for a in range(SUBX):
-                moved = jnp.take_along_axis(blocks[a], places, axis=1, mode="promise_in_bounds")
-                whole = jnp.where((lanes % ZONES) // GROUP == a, moved, whole)
-            tangent[pl.ds(start, 8), pair * 128 : (pair + 1) * 128] = whole
-            table[pl.ds(pl.multiple_of(pair * rows + index * 8, 8), 8), :] = whole
-        return carry
-
-    lax.fori_loop(0, rows // 8, body, 0, unroll=2)
+    width = 128 // SUBX
+    fields = list(fields)
+    for step in (1, 2, 4):
+        late = (lanes // width) & step != 0
+        for low in range(SUBX):
+            if low & step:
+                continue
+            a, b = fields[low], fields[low | step]
+            fields[low] = jnp.where(late, pltpu.roll(b, step * width, 1), a)
+            fields[low | step] = jnp.where(late, b, pltpu.roll(a, 128 - step * width, 1))
+    return fields
+
+
+def place_kernel(info, index, own, got2, got4, got6, other, tangent, picks, parts, table):
+    lanes = lane_places()
+    for place in range(SUBX):
+        near = (own, got2, got4, got6)[place // 2]
+        if place % 2 == 0:
+            chunk = near[0:PLACES, :]
+        else:
+            chunk = other[(place // 2) * PLACES : (place // 2 + 1) * PLACES, :]
+        parts[pl.ds(pl.multiple_of((info[0] ^ place) * PLACES, 8), PLACES), :] = chunk
+    order = (lanes % ZONES) // GROUP * 16 + lanes // ZONES * GROUP + lanes % GROUP
+    entries = PLACES * LAYERS // 2
+    for start in range(0, PLACES, 8):
+        blocks = swap_blocks([parts[a * PLACES + start : a * PLACES + start + 8, :] for a in range(SUBX)])
+        for pair in range(SUBX):
+            whole = jnp.take_along_axis(blocks[pair], order, axis=1, mode="promise_in_bounds")
+            tangent[start : start + 8, pair * 128 : (pair + 1) * 128] = whole
+            line = pair * PLACES + start
+            table[line : line + 8, :] = whole
+            table[entries + line : entries + line + 8, :] = pltpu.roll(whole, ZONES, 1)
+    table[2 * entries : 2 * entries + 8, :] = jnp.zeros(TILE, jnp.float32)
     upper = lax.broadcasted_iota(jnp.int32, (1, 128), 1) >= ZONES
-
-    def fetch(owner, slot, want):
-        cell = cells[slot, owner]
-        layer = cell % LAYERS
-        line = table[pl.ds((layer // 2) * rows + cell // LAYERS, 1), :]
-        line = jnp.where(layer % 2 == want, line, pltpu.roll(line, ZONES, 1))
-        return jnp.where(slot < counts[owner], line, 0.0)
-
-    def pick(owner, carry):
-        lines = []
+    for owner in range(SUBY):
         for slot in range(CAP // 2):
-            lines.append(jnp.where(upper, fetch(owner, slot + CAP // 2, 1), fetch(owner, slot, 0)))
-        for slot, line in enumerate(lines):
-            picks[pl.ds(owner * (CAP // 2) + slot, 1), :] = line
-        return carry
-
-    lax.fori_loop(0, SUBY, pick, 0, unroll=4)
-
-
-def run_place(cells, counts, parts):
+            low = table[pl.ds(index[slot, owner], 1), :]
+            high = table[pl.ds(index[slot + CAP // 2, owner], 1), :]
+            line = owner * (CAP // 2) + slot
+            picks[line : line + 1, :] = jnp.where(upper, high, low)
+
+
+def run_place(info, index, *pieces):
+    entries = PLACES * LAYERS // 2
     return pl.pallas_call(
         place_kernel,
         out_shape=(
-            jax.ShapeDtypeStruct((ROWS * COLS, LAYERS * ZONES), jnp.float32),
+            jax.ShapeDtypeStruct((PLACES, LAYERS * ZONES), jnp.float32),
             jax.ShapeDtypeStruct((SUBY * CAP // 2, 128), jnp.float32),
         ),
-        in_specs=[pl.BlockSpec(memory_space=pltpu.SMEM)] * 2 + [pl.BlockSpec(memory_space=pltpu.VMEM)],
+        in_specs=[pl.BlockSpec(memory_space=pltpu.SMEM)] * 2 + [pl.BlockSpec(memory_space=pltpu.VMEM)] * 5,
         out_specs=(pl.BlockSpec(memory_space=pltpu.VMEM),) * 2,
-        scratch_shapes=[pltpu.VMEM((ROWS * COLS * LAYERS // 2, 128), jnp.float32)],
+        scratch_shapes=[
+            pltpu.VMEM((SUBX * PLACES, 128), jnp.float32),
+            pltpu.VMEM((2 * entries + 8, 128), jnp.float32),
+        ],
         name="place",
-    )(cells, counts, parts)
+    )(info, index, *pieces)
 
 
 def finish_kernel(arrived, wells):
@@ -326,38 +363,43 @@
     )(arrived)
 
 
+def swap(array, axis, pairs):
+    return lax.ppermute(array, axis, pairs)
+
+
+def partners(shift):
+    return [(i, i ^ shift) for i in range(SUBX)]
+
+
 def gather_inputs(conductivity, storage, head_term, zone_id, layer_count):
-    depth = jnp.arange(LAYERS, dtype=jnp.int32)
-    active = (depth[None, None, :] < layer_count[0, 0]).astype(jnp.float32)
-    cond = jnp.sqrt(conductivity) * active
-    fields = jnp.concatenate([cond, storage, head_term, zone_id.astype(jnp.float32)], axis=2)
-    even = lax.axis_index("gy") % 2 == 0
+    own = run_pack(layer_count, conductivity, storage, head_term, zone_id)
     inner = [(i, i ^ 1) for i in range(SUBY)]
     outer = [(i, i + 1) for i in range(1, SUBY - 1, 2)]
     outer = outer + [(j, i) for i, j in outer]
-    first, last = fields[:, :HALO], fields[:, COLS - HALO :]
-    got_inner = lax.ppermute(jnp.where(even, last, first), "gy", inner)
-    got_outer = lax.ppermute(jnp.where(even, first, last), "gy", outer)
-    left = jnp.where(even, got_outer, got_inner)
-    right = jnp.where(even, got_inner, got_outer)
-    wide = jnp.concatenate([left, fields, right], axis=1).reshape(ROWS * PAIRS, 128)
-    blocks = [wide]
-    for shift in (2, 4, 6):
-        blocks.append(lax.ppermute(wide, "gx", [(i, i ^ shift) for i in range(SUBX)]))
-    mine = jnp.concatenate(blocks, axis=0)
-    other = lax.ppermute(mine, "gx", [(i, i ^ 1) for i in range(SUBX)])
-    return mine, other
+    wide = jnp.concatenate([own, swap(own, "gy", inner), swap(own, "gy", outer)], axis=0)
+    mine = jnp.concatenate([wide] + [swap(wide, "gx", partners(shift)) for shift in (2, 4, 6)], axis=0)
+    return mine, swap(mine, "gx", partners(1))
+
+
+def line_index(well_cell, well_count):
+    cells = well_cell.T
+    slots = jnp.arange(CAP, dtype=jnp.int32)[:, None]
+    layer = cells & (LAYERS - 1)
+    entries = PLACES * LAYERS // 2
+    turned = (layer & 1) != (slots >= CAP // 2).astype(jnp.int32)
+    lines = (layer >> 1) * PLACES + (cells >> 4) + jnp.where(turned, entries, 0)
+    return jnp.where(slots < well_count[None, :], lines, 2 * entries)
 
 
 def shards(conductivity, storage, head_term, zone_id, layer_count, well_cell, well_count):
     mine, other = gather_inputs(conductivity, storage, head_term, zone_id, layer_count)
     row, col = lax.axis_index("gx"), lax.axis_index("gy")
     info = jnp.stack([row, col, SUBY - 1 - col]).astype(jnp.int32)
-    parts = run_main(info, mine, other).reshape(SUBX, ROWS * COLS, 128)
-    parts = lax.all_to_all(parts, "gx", 0, 0, tiled=True)
-    tangent, picks = run_place(
-        well_cell[0, 0].T, well_count[0, 0], parts.reshape(SUBX * ROWS * COLS, 128)
-    )
+    index = line_index(well_cell[0, 0], well_count[0, 0])
+    sends = run_main(info, mine, other)
+    near = [sends[0]] + [swap(sends[k], "gx", partners(2 * k)) for k in (1, 2, 3)]
+    far = swap(jnp.concatenate([part[PLACES:] for part in near], axis=0), "gx", partners(1))
+    tangent, picks = run_place(info, index, *near, far)
     picks = picks.reshape(SUBY, CAP // 2, 128)
     arrived = lax.all_to_all(picks, "gy", split_axis=0, concat_axis=0, tiled=True)
     wells = run_finish(arrived.reshape(SUBY * CAP // 2, 128)).T

time: 76.4 us -> 72.8 us (0.953)
  blocking collectives: 37.1 us -> 25.2 us
  starting transfers between devices: 13.3 us -> 19.1 us
  waiting for transfers between devices: 5.7 us -> 8.54 us
  Pallas kernels: 16.4 us -> 13.9 us
  local copies, waits for them, and re-layouts: 1.68 us -> 3.42 us
    all_to_all x1 -> x0, blocking collectives: 12.3 us -> none  [shards(): parts = lax.all_to_all(parts, 'gx', 0, 0, tiled=True)]
    ppermute x6 -> x10, starting transfers between devices: 13.3 us -> 19.1 us  [swap(): return lax.ppermute(array, axis, pairs)]
    ppermute x6 -> x10, waiting for transfers between devices: 5.7 us -> 8.54 us  [swap(): return lax.ppermute(array, axis, pairs)]
    pallas_call x2 -> x3, Pallas kernels: 14.7 us -> 12.2 us  [the longest x1 8.24 us: run_main(): pl.pallas_call(main_kernel, out_shape=(jax.ShapeDtypeStruct((2 * PLACES,...]
    unnamed x11 -> x23, local copies, waits for them, and re-layouts: 1.6 us -> 2.66 us
  transfers between devices with their start and end apart: 6 -> 10, of which waited for: 4 -> 7; matrix products, arithmetic and copies ran while one was open for 0% -> 2% of each run, Pallas kernels for 0% -> 0%
where the time goes in v3:
time: 72.8 us; the launch traced here: 72.3 us
  blocking collectives  25.2 us (35%)
  starting transfers between devices  19.1 us (26%)
  Pallas kernels  13.9 us (19%)
  waiting for transfers between devices  8.54 us (12%)
  local copies, waits for them, and re-layouts  3.42 us (5%)
  between operations  1.39 us (2%)
  other arithmetic  0.75 us (1%)
    all_to_all x1, blocking collectives, shards(): lax.all_to_all(picks, 'gy', split_axis=0, concat_axis=0, tiled=True)  25.2 us
    ppermute x10, starting transfers between devices, swap(): return lax.ppermute(array, axis, pairs)  19.1 us
    ppermute x10, waiting for transfers between devices, swap(): return lax.ppermute(array, axis, pairs)  8.54 us
    pallas_call x1, Pallas kernels, run_main(): pl.pallas_call(main_kernel, out_shape=(jax.ShapeDtypeStruct((2 * PLACES,...  8.24 us
    unnamed x23, local copies, waits for them, and re-layouts  2.66 us
    pallas_call x1, Pallas kernels, run_place(): pl.pallas_call(place_kernel, out_shape=(jax.ShapeDtypeStruct((PLACES, LAY...  2.47 us
    pallas_call x1, Pallas kernels, run_finish(): pl.pallas_call(finish_kernel, out_shape=jax.ShapeDtypeStruct((ZONES, SUBY...  1.72 us
    pallas_call x1, Pallas kernels, run_pack(): pl.pallas_call(pack_kernel, out_shape=jax.ShapeDtypeStruct((OWN, 128), jn...  1.51 us
  transfers between devices with their start and end apart: 10, of which 7 were waited for; matrix products, arithmetic and copies ran while one was open for 2% of the time, Pallas kernels for 0%

profile of v3, /device:TPU:1, one launch (start us, length us, event | category | flops | bytes accessed | tf_op | source)
XLA Modules:
  0.0 72.3 jit_solution(6546012680608351755)
XLA Ops:
  1.3 1.5 %pack.1 = f32[32,128]{1,0:T(8,128)} custom-call(s32[1,1]{1,0:T(1,128)S(6)} %copy.14.layers, f32[4,16,16]{2,1,0:T(8,128)} %conductivity.1, f32[4,16,16]{2,1,0:T(8,128)} %storage.1, f32[4,16,16]{2,1,0:T(8,128)} %head.1, s32[4,16,16]{2,1,0:T(8,128)} %zone.1), custom_call_target="tpu_custom_call" | custom-call | tf_op jit(solution)/shard_map/pack/pallas_call | solution.py:83
  2.8 0.8 %collective-permute-start.1 = (f32[32,128]{1,0:T(8,128)}, f32[32,128]{1,0:T(8,128)S(1)}, u32[]{:S(2)}, u32[]{:S(2)}) collective-permute-start(f32[32,128]{1,0:T(8,128)} %pack.1), channel_id=1, source_target_pairs={{1,2},{3,4},{5,6},{7,8},{9,10},{11,12},{13,14},{15,16},{17,18},{19... | collective-permute-start | bytes 49160 | tf_op jit(solution)/shard_map/ppermute | solution.py:367
  3.6 4.6 %collective-permute-start = (f32[32,128]{1,0:T(8,128)}, f32[32,128]{1,0:T(8,128)S(1)}, u32[]{:S(2)}, u32[]{:S(2)}) collective-permute-start(f32[32,128]{1,0:T(8,128)} %pack.1), channel_id=1, source_target_pairs={{0,1},{1,0},{2,3},{3,2},{4,5},{5,4},{6,7},{7,6},{8,9},{9,8},{10,11... | collective-permute-start | bytes 49160 | tf_op jit(solution)/shard_map/ppermute | solution.py:367
  8.2 0.8 %constant_dynamic-update-slice_fusion.5 = f32[384,128]{1,0:T(8,128)S(1)} fusion(f32[32,128]{1,0:T(8,128)} %pack.1), kind=kLoop, calls=%fused_computation.7 | loop fusion | bytes 32768
  8.9 0.0 collective-permute-done.1
  8.9 0.6 collective-permute-done
  9.5 4.4 %collective-permute-start.4 = (f32[96,128]{1,0:T(8,128)S(1)}, f32[96,128]{1,0:T(8,128)S(1)}, u32[]{:S(2)}, u32[]{:S(2)}) collective-permute-start(f32[96,128]{1,0:T(8,128)S(1)} %pad_maximum_fusion.1), channel_id=1, source_target_pairs={{0,192},{32,224},{64,128},{96,160},{128,64},{160,96},{192,0},{224,... | collective-permute-start | bytes 147464 | tf_op jit(solution)/shard_map/ppermute | solution.py:367
  13.9 0.0 collective-permute-start.3
  13.9 0.4 collective-permute-start.2
  14.3 2.8 %collective-permute-done.2 = f32[96,128]{1,0:T(8,128)S(1)} collective-permute-done((f32[96,128]{1,0:T(8,128)S(1)}, f32[96,128]{1,0:T(8,128)S(1)}, u32[]{:S(2)}, u32[]{:S(2)}) %collective-permute-start.2) | collective-permute-done | bytes 49184 | tf_op jit(solution)/shard_map/ppermute | solution.py:367
  17.2 0.8 %collective-permute-done.3 = f32[96,128]{1,0:T(8,128)S(1)} collective-permute-done((f32[96,128]{1,0:T(8,128)S(1)}, f32[96,128]{1,0:T(8,128)S(1)}, u32[]{:S(2)}, u32[]{:S(2)}) %collective-permute-start.3) | collective-permute-done | bytes 49184 | tf_op jit(solution)/shard_map/ppermute | solution.py:367
  18.0 3.2 %collective-permute-start.5 = (f32[384,128]{1,0:T(8,128)S(1)}, f32[384,128]{1,0:T(8,128)S(1)}, u32[]{:S(2)}, u32[]{:S(2)}) collective-permute-start(f32[384,128]{1,0:T(8,128)S(1)} %constant_dynamic-update-slice_fusion.mine), channel_id=1, source_target_pairs={{0,32},{32,0},{64,96},{96,64},{128,160},{160,128},{192,224},{224,1... | collective-permute-start | bytes 589832 | tf_op jit(solution)/shard_map/ppermute | solution.py:367
  21.1 0.1 pad_add_fusion.info
  21.2 1.0 %collective-permute-done.5.other = f32[384,128]{1,0:T(8,128)S(1)} collective-permute-done((f32[384,128]{1,0:T(8,128)S(1)}, f32[384,128]{1,0:T(8,128)S(1)}, u32[]{:S(2)}, u32[]{:S(2)}) %collective-permute-start.5) | collective-permute-done | bytes 196640 | tf_op jit(solution)/shard_map/ppermute | solution.py:367
  22.2 8.2 %schwarz.1 = (f32[128,128]{1,0:T(8,128)S(1)}, f32[128,128]{1,0:T(8,128)S(1)}, f32[128,128]{1,0:T(8,128)S(1)}, f32[128,128]{1,0:T(8,128)S(1)}) custom-call(s32[3]{0:T(128)S(1)} %pad_add_fusion.info, f32[384,128]{1,0:T(8,128)S(1)} %constant_dynamic-update-slice_fusion.mine, f32[384,128]{1,0:T(8,128)S(1)} %collective-permute-done.5.other), custom_call_target="tpu_custom_call" | custom-call | tf_op jit(solution)/shard_map/schwarz/pallas_call | solution.py:268
  30.5 0.0 copy-start
  30.5 0.3 collective-permute-start.6
  30.8 1.6 %collective-permute-start.7 = (f32[128,128]{1,0:T(8,128)S(1)}, f32[128,128]{1,0:T(8,128)S(1)}, u32[]{:S(2)}, u32[]{:S(2)}) collective-permute-start(f32[128,128]{1,0:T(8,128)S(1)} %get-tuple-element.10), channel_id=1, source_target_pairs={{0,128},{32,160},{64,192},{96,224},{128,0},{160,32},{192,64},{224,... | collective-permute-start | bytes 196616 | tf_op jit(solution)/shard_map/ppermute | solution.py:367
  32.5 1.7 %collective-permute-start.8 = (f32[128,128]{1,0:T(8,128)S(1)}, f32[128,128]{1,0:T(8,128)S(1)}, u32[]{:S(2)}, u32[]{:S(2)}) collective-permute-start(f32[128,128]{1,0:T(8,128)S(1)} %get-tuple-element.11), channel_id=1, source_target_pairs={{0,192},{32,224},{64,128},{96,160},{128,64},{160,96},{192,0},{224,... | collective-permute-start | bytes 196616 | tf_op jit(solution)/shard_map/ppermute | solution.py:367
  34.2 0.6 copy-done.2
  34.8 0.2 collective-permute-done.7.got4
  35.0 0.6 copy-done.3
  35.6 2.8 %collective-permute-done.8.got6 = f32[128,128]{1,0:T(8,128)S(1)} collective-permute-done((f32[128,128]{1,0:T(8,128)S(1)}, f32[128,128]{1,0:T(8,128)S(1)}, u32[]{:S(2)}, u32[]{:S(2)}) %collective-permute-start.8) | collective-permute-done | bytes 65568 | tf_op jit(solution)/shard_map/ppermute | solution.py:367
  38.4 0.7 %slice-done.1 = f32[64,128]{1,0:T(8,128)S(1)} async-done(((f32[128,128]{1,0:T(8,128)}), f32[64,128]{1,0:T(8,128)S(1)}, s32[]{:S(2)}) %slice-start.1) | async-done | bytes 32792 | tf_op jit(solution)/shard_map/slice | solution.py:401
  39.2 0.0 copy-start.8
  39.2 2.1 %collective-permute-start.9 = (f32[256,128]{1,0:T(8,128)S(1)}, f32[256,128]{1,0:T(8,128)S(1)}, u32[]{:S(2)}, u32[]{:S(2)}) collective-permute-start(f32[256,128]{1,0:T(8,128)S(1)} %pad_maximum_fusion), channel_id=1, source_target_pairs={{0,32},{32,0},{64,96},{96,64},{128,160},{160,128},{192,224},{224,1... | collective-permute-start | bytes 393224 | tf_op jit(solution)/shard_map/ppermute | solution.py:367
  41.3 0.7 bitcast_select_fusion.index
  42.0 0.3 collective-permute-done.9.other
  42.3 0.6 copy-done.6
  42.9 2.5 %place.1 = (f32[64,1024]{1,0:T(8,128)}, f32[128,128]{1,0:T(8,128)}) custom-call(s32[3]{0:T(128)} %copy-done.1, s32[8,32]{1,0:T(8,128)} %bitcast_select_fusion.index, f32[128,128]{1,0:T(8,128)} %copy-done, f32[128,128]{1,0:T(8,128)} %copy-done.2, f32[128,128]{1,0:T(8,128)} %copy-done.3, f32[128,128]{1,0:T(8,128)} %copy-done.4, f32[256,128]{1,0:T(8,128)} %copy-done.6), custom_call_target="tpu_custom_call" | custom-call | tf_op jit(solution)/shard_map/place/pallas_call | solution.py:325
  45.4 25.2 %all_to_all.5 = f32[32,4,128]{2,1,0:T(4,128)} all-to-all(f32[32,4,128]{2,1,0:T(4,128)} %bitcast.20), channel_id=1, replica_groups=mesh['gx'=8,'gy'=32] {'gy'}, dimensions={0} | all-to-all | bytes 131072 | tf_op jit(solution)/shard_map/all_to_all | solution.py:404
  70.6 1.7 %finish.1 = f32[64,256]{1,0:T(8,128)} custom-call(f32[128,128]{1,0:T(8,128)} %bitcast.18), custom_call_target="tpu_custom_call" | custom-call | tf_op jit(solution)/shard_map/finish/pallas_call | solution.py:357
  (28 shorter events, 0.1 us)
Async XLA Ops:
  2.8 6.7 %copy-start.5 = (f32[32,128]{1,0:T(8,128)S(1)}, f32[32,128]{1,0:T(8,128)}, u32[]{:S(2)}) copy-start(f32[32,128]{1,0:T(8,128)} %pack.1) | copy-start | bytes 49156
  2.8 6.1 %collective-permute-start.1 = (f32[32,128]{1,0:T(8,128)}, f32[32,128]{1,0:T(8,128)S(1)}, u32[]{:S(2)}, u32[]{:S(2)}) collective-permute-start(f32[32,128]{1,0:T(8,128)} %pack.1), channel_id=1, source_target_pairs={{1,2},{3,4},{5,6},{7,8},{9,10},{11,12},{13,14},{15,16},{17,18},{19... | collective-permute-start | bytes 49160 | tf_op jit(solution)/shard_map/ppermute | solution.py:367
  3.6 5.9 %collective-permute-start = (f32[32,128]{1,0:T(8,128)}, f32[32,128]{1,0:T(8,128)S(1)}, u32[]{:S(2)}, u32[]{:S(2)}) collective-permute-start(f32[32,128]{1,0:T(8,128)} %pack.1), channel_id=1, source_target_pairs={{0,1},{1,0},{2,3},{3,2},{4,5},{5,4},{6,7},{7,6},{8,9},{9,8},{10,11... | collective-permute-start | bytes 49160 | tf_op jit(solution)/shard_map/ppermute | solution.py:367
  9.5 8.4 %collective-permute-start.4 = (f32[96,128]{1,0:T(8,128)S(1)}, f32[96,128]{1,0:T(8,128)S(1)}, u32[]{:S(2)}, u32[]{:S(2)}) collective-permute-start(f32[96,128]{1,0:T(8,128)S(1)} %pad_maximum_fusion.1), channel_id=1, source_target_pairs={{0,192},{32,224},{64,128},{96,160},{128,64},{160,96},{192,0},{224,... | collective-permute-start | bytes 147464 | tf_op jit(solution)/shard_map/ppermute | solution.py:367
  13.9 4.0 %collective-permute-start.3 = (f32[96,128]{1,0:T(8,128)S(1)}, f32[96,128]{1,0:T(8,128)S(1)}, u32[]{:S(2)}, u32[]{:S(2)}) collective-permute-start(f32[96,128]{1,0:T(8,128)S(1)} %pad_maximum_fusion.1), channel_id=1, source_target_pairs={{0,128},{32,160},{64,192},{96,224},{128,0},{160,32},{192,64},{224,... | collective-permute-start | bytes 147464 | tf_op jit(solution)/shard_map/ppermute | solution.py:367
  13.9 3.2 %collective-permute-start.2 = (f32[96,128]{1,0:T(8,128)S(1)}, f32[96,128]{1,0:T(8,128)S(1)}, u32[]{:S(2)}, u32[]{:S(2)}) collective-permute-start(f32[96,128]{1,0:T(8,128)S(1)} %pad_maximum_fusion.1), channel_id=1, source_target_pairs={{0,64},{32,96},{64,0},{96,32},{128,192},{160,224},{192,128},{224,1... | collective-permute-start | bytes 147464 | tf_op jit(solution)/shard_map/ppermute | solution.py:367
  18.0 4.2 %collective-permute-start.5 = (f32[384,128]{1,0:T(8,128)S(1)}, f32[384,128]{1,0:T(8,128)S(1)}, u32[]{:S(2)}, u32[]{:S(2)}) collective-permute-start(f32[384,128]{1,0:T(8,128)S(1)} %constant_dynamic-update-slice_fusion.mine), channel_id=1, source_target_pairs={{0,32},{32,0},{64,96},{96,64},{128,160},{160,128},{192,224},{224,1... | collective-permute-start | bytes 589832 | tf_op jit(solution)/shard_map/ppermute | solution.py:367
  21.2 9.2 %copy-start.1 = (s32[3]{0:T(128)}, s32[3]{0:T(128)S(1)}, u32[]{:S(2)}) copy-start(s32[3]{0:T(128)S(1)} %pad_add_fusion.info) | copy-start | bytes 40
  30.5 3.7 %copy-start = (f32[128,128]{1,0:T(8,128)}, f32[128,128]{1,0:T(8,128)S(1)}, u32[]{:S(2)}) copy-start(f32[128,128]{1,0:T(8,128)S(1)} %get-tuple-element.8.own) | copy-start | bytes 196612
  30.5 3.6 %collective-permute-start.6 = (f32[128,128]{1,0:T(8,128)S(1)}, f32[128,128]{1,0:T(8,128)S(1)}, u32[]{:S(2)}, u32[]{:S(2)}) collective-permute-start(f32[128,128]{1,0:T(8,128)S(1)} %get-tuple-element.9), channel_id=1, source_target_pairs={{0,64},{32,96},{64,0},{96,32},{128,192},{160,224},{192,128},{224,1... | collective-permute-start | bytes 196616 | tf_op jit(solution)/shard_map/ppermute | solution.py:367
  30.8 4.1 %collective-permute-start.7 = (f32[128,128]{1,0:T(8,128)S(1)}, f32[128,128]{1,0:T(8,128)S(1)}, u32[]{:S(2)}, u32[]{:S(2)}) collective-permute-start(f32[128,128]{1,0:T(8,128)S(1)} %get-tuple-element.10), channel_id=1, source_target_pairs={{0,128},{32,160},{64,192},{96,224},{128,0},{160,32},{192,64},{224,... | collective-permute-start | bytes 196616 | tf_op jit(solution)/shard_map/ppermute | solution.py:367
  32.5 6.0 %collective-permute-start.8 = (f32[128,128]{1,0:T(8,128)S(1)}, f32[128,128]{1,0:T(8,128)S(1)}, u32[]{:S(2)}, u32[]{:S(2)}) collective-permute-start(f32[128,128]{1,0:T(8,128)S(1)} %get-tuple-element.11), channel_id=1, source_target_pairs={{0,192},{32,224},{64,128},{96,160},{128,64},{160,96},{192,0},{224,... | collective-permute-start | bytes 196616 | tf_op jit(solution)/shard_map/ppermute | solution.py:367
  34.1 0.6 copy-start.2
  35.0 0.6 copy-start.3
  35.6 2.9 %slice-start = ((f32[128,128]{1,0:T(8,128)}), f32[64,128]{1,0:T(8,128)S(1)}, s32[]{:S(2)}) async-start(f32[128,128]{1,0:T(8,128)} %copy-done.2), calls=%async_computation.1 | async-start | bytes 65536 | tf_op jit(solution)/shard_map/slice | solution.py:401
  38.4 0.8 %copy-start.4 = (f32[128,128]{1,0:T(8,128)}, f32[128,128]{1,0:T(8,128)S(1)}, u32[]{:S(2)}) copy-start(f32[128,128]{1,0:T(8,128)S(1)} %collective-permute-done.8.got6) | copy-start | bytes 196612
  38.4 0.8 %slice-start.1 = ((f32[128,128]{1,0:T(8,128)}), f32[64,128]{1,0:T(8,128)S(1)}, s32[]{:S(2)}) async-start(f32[128,128]{1,0:T(8,128)} %copy-done.3), calls=%async_computation.2 | async-start | bytes 65536 | tf_op jit(solution)/shard_map/slice | solution.py:401
  39.2 2.1 %copy-start.7 = (s32[1,1,32,8]{2,3,1,0:T(8,128)S(1)}, s32[1,1,32,8]{2,3,1,0:T(8,128)}, u32[]{:S(2)}) copy-start(s32[1,1,32,8]{2,3,1,0:T(8,128)} %param.12) | copy-start | bytes 3076
  39.2 2.1 %copy-start.8 = (s32[1,1,32]{2,1,0:T(1,128)S(1)}, s32[1,1,32]{2,1,0:T(1,128)}, u32[]{:S(2)}) copy-start(s32[1,1,32]{2,1,0:T(1,128)} %param.13) | copy-start | bytes 388
  39.2 3.1 %collective-permute-start.9 = (f32[256,128]{1,0:T(8,128)S(1)}, f32[256,128]{1,0:T(8,128)S(1)}, u32[]{:S(2)}, u32[]{:S(2)}) collective-permute-start(f32[256,128]{1,0:T(8,128)S(1)} %pad_maximum_fusion), channel_id=1, source_target_pairs={{0,32},{32,0},{64,96},{96,64},{128,160},{160,128},{192,224},{224,1... | collective-permute-start | bytes 393224 | tf_op jit(solution)/shard_map/ppermute | solution.py:367
  42.3 0.6 copy-start.6

commit v4 on v3

--- a/solution.py
+++ b/solution.py
@@ -85,6 +85,7 @@
         out_shape=jax.ShapeDtypeStruct((OWN, 128), jnp.float32),
         in_specs=[pl.BlockSpec(memory_space=pltpu.SMEM)] + [pl.BlockSpec(memory_space=pltpu.VMEM)] * 4,
         out_specs=pl.BlockSpec(memory_space=pltpu.VMEM),
+        compiler_params=pltpu.CompilerParams(vmem_limit_bytes=4 * 1024 * 1024),
         name="pack",
     )(layers, conductivity, storage, head, zone)
 
@@ -291,14 +292,12 @@
     return fields
 
 
-def place_kernel(info, index, own, got2, got4, got6, other, tangent, picks, parts, table):
+def place_kernel(info, index, *refs):
+    pieces, (tangent, picks, parts, table) = refs[:SUBX], refs[SUBX:]
     lanes = lane_places()
     for place in range(SUBX):
-        near = (own, got2, got4, got6)[place // 2]
-        if place % 2 == 0:
-            chunk = near[0:PLACES, :]
-        else:
-            chunk = other[(place // 2) * PLACES : (place // 2 + 1) * PLACES, :]
+        side = place % 2
+        chunk = pieces[side * 4 + place // 2][side * PLACES : (side + 1) * PLACES, :]
         parts[pl.ds(pl.multiple_of((info[0] ^ place) * PLACES, 8), PLACES), :] = chunk
     order = (lanes % ZONES) // GROUP * 16 + lanes // ZONES * GROUP + lanes % GROUP
     entries = PLACES * LAYERS // 2
@@ -320,7 +319,7 @@
             picks[line : line + 1, :] = jnp.where(upper, high, low)
 
 
-def run_place(info, index, *pieces):
+def run_place(info, index, pieces):
     entries = PLACES * LAYERS // 2
     return pl.pallas_call(
         place_kernel,
@@ -328,12 +327,13 @@
             jax.ShapeDtypeStruct((PLACES, LAYERS * ZONES), jnp.float32),
             jax.ShapeDtypeStruct((SUBY * CAP // 2, 128), jnp.float32),
         ),
-        in_specs=[pl.BlockSpec(memory_space=pltpu.SMEM)] * 2 + [pl.BlockSpec(memory_space=pltpu.VMEM)] * 5,
+        in_specs=[pl.BlockSpec(memory_space=pltpu.SMEM)] * 2 + [pl.BlockSpec(memory_space=pltpu.VMEM)] * 8,
         out_specs=(pl.BlockSpec(memory_space=pltpu.VMEM),) * 2,
         scratch_shapes=[
             pltpu.VMEM((SUBX * PLACES, 128), jnp.float32),
             pltpu.VMEM((2 * entries + 8, 128), jnp.float32),
         ],
+        compiler_params=pltpu.CompilerParams(vmem_limit_bytes=8 * 1024 * 1024),
         name="place",
     )(info, index, *pieces)
 
@@ -359,6 +359,7 @@
         out_shape=jax.ShapeDtypeStruct((ZONES, SUBY * CAP), jnp.float32),
         in_specs=[pl.BlockSpec(memory_space=pltpu.VMEM)],
         out_specs=pl.BlockSpec(memory_space=pltpu.VMEM),
+        compiler_params=pltpu.CompilerParams(vmem_limit_bytes=4 * 1024 * 1024),
         name="finish",
     )(arrived)
 
@@ -371,14 +372,15 @@
     return [(i, i ^ shift) for i in range(SUBX)]
 
 
-def gather_inputs(conductivity, storage, head_term, zone_id, layer_count):
+def gather_inputs(conductivity, storage, head_term, zone_id, layer_count, others):
     own = run_pack(layer_count, conductivity, storage, head_term, zone_id)
     inner = [(i, i ^ 1) for i in range(SUBY)]
     outer = [(i, i + 1) for i in range(1, SUBY - 1, 2)]
     outer = outer + [(j, i) for i, j in outer]
     wide = jnp.concatenate([own, swap(own, "gy", inner), swap(own, "gy", outer)], axis=0)
+    wide, others = lax.optimization_barrier((wide, others))
     mine = jnp.concatenate([wide] + [swap(wide, "gx", partners(shift)) for shift in (2, 4, 6)], axis=0)
-    return mine, swap(mine, "gx", partners(1))
+    return mine, swap(mine, "gx", partners(1)), others
 
 
 def line_index(well_cell, well_count):
@@ -392,14 +394,16 @@
 
 
 def shards(conductivity, storage, head_term, zone_id, layer_count, well_cell, well_count):
-    mine, other = gather_inputs(conductivity, storage, head_term, zone_id, layer_count)
     row, col = lax.axis_index("gx"), lax.axis_index("gy")
     info = jnp.stack([row, col, SUBY - 1 - col]).astype(jnp.int32)
     index = line_index(well_cell[0, 0], well_count[0, 0])
+    mine, other, (info, index) = gather_inputs(
+        conductivity, storage, head_term, zone_id, layer_count, (info, index)
+    )
     sends = run_main(info, mine, other)
     near = [sends[0]] + [swap(sends[k], "gx", partners(2 * k)) for k in (1, 2, 3)]
-    far = swap(jnp.concatenate([part[PLACES:] for part in near], axis=0), "gx", partners(1))
-    tangent, picks = run_place(info, index, *near, far)
+    far = [swap(part, "gx", partners(1)) for part in near]
+    tangent, picks = run_place(info, index, near + far)
     picks = picks.reshape(SUBY, CAP // 2, 128)
     arrived = lax.all_to_all(picks, "gy", split_axis=0, concat_axis=0, tiled=True)
     wells = run_finish(arrived.reshape(SUBY * CAP // 2, 128)).T

time: 72.8 us -> 70.6 us (0.970)
  starting transfers between devices: 19.1 us -> 22.4 us
  Pallas kernels: 13.9 us -> 11.4 us
  waiting for transfers between devices: 8.54 us -> 6.23 us
    ppermute x10 -> x13, starting transfers between devices: 19.1 us -> 22.4 us  [swap(): return lax.ppermute(array, axis, pairs)]
    ppermute x10 -> x13, waiting for transfers between devices: 8.54 us -> 6.23 us  [swap(): return lax.ppermute(array, axis, pairs)]
    pallas_call x1, Pallas kernels: 1.51 us -> 0.09 us  [run_pack(): pl.pallas_call(pack_kernel, out_shape=jax.ShapeDtypeStruct((OWN, 128), jn...]
    unnamed x23 -> x15, local copies, waits for them, and re-layouts: 2.66 us -> 3.72 us
    pallas_call x1, Pallas kernels: 1.72 us -> 0.88 us  [run_finish(): pl.pallas_call(finish_kernel, out_shape=jax.ShapeDtypeStruct((ZONES, SUBY...]
    slice x6 -> x0, local copies, waits for them, and re-layouts: 0.75 us -> none  [shards(): part[PLACES:]]
  transfers between devices with their start and end apart: 10 -> 13, of which waited for: 7 -> 6; matrix products, arithmetic and copies ran while one was open for 2% -> 0% of each run, Pallas kernels for 0% -> 0%
where the time goes in v4:
time: 70.6 us; the launch traced here: 70.1 us
  blocking collectives  24.9 us (35%)
  starting transfers between devices  22.4 us (32%)
  Pallas kernels  11.4 us (16%)
  waiting for transfers between devices  6.23 us (9%)
  local copies, waits for them, and re-layouts  3.73 us (5%)
  between operations  1.35 us (2%)
    all_to_all x1, blocking collectives, shards(): lax.all_to_all(picks, 'gy', split_axis=0, concat_axis=0, tiled=True)  24.9 us
    ppermute x13, starting transfers between devices, swap(): return lax.ppermute(array, axis, pairs)  22.4 us
    pallas_call x1, Pallas kernels, run_main(): pl.pallas_call(main_kernel, out_shape=(jax.ShapeDtypeStruct((2 * PLACES,...  8.24 us
    ppermute x13, waiting for transfers between devices, swap(): return lax.ppermute(array, axis, pairs)  6.23 us
    unnamed x15, local copies, waits for them, and re-layouts  3.72 us
    pallas_call x1, Pallas kernels, run_place(): pl.pallas_call(place_kernel, out_shape=(jax.ShapeDtypeStruct((PLACES, LAY...  2.16 us
  transfers between devices with their start and end apart: 13, of which 6 were waited for; matrix products, arithmetic and copies ran while one was open for 0% of the time, Pallas kernels for 0%

profile of v4, /device:TPU:1, one launch (start us, length us, event | category | flops | bytes accessed | tf_op | source)
XLA Modules:
  0.0 70.1 jit_solution(16936918657099829580)
XLA Ops:
  1.3 0.7 %copy-done = f32[4,16,16]{2,1,0:T(8,128)S(1)} copy-done((f32[4,16,16]{2,1,0:T(8,128)S(1)}, f32[4,16,16]{2,1,0:T(8,128)}, u32[]{:S(2)}) %copy-start) | copy-done | bytes 4120
  2.0 0.8 %copy-done.1 = f32[4,16,16]{2,1,0:T(8,128)S(1)} copy-done((f32[4,16,16]{2,1,0:T(8,128)S(1)}, f32[4,16,16]{2,1,0:T(8,128)}, u32[]{:S(2)}) %copy-start.1) | copy-done | bytes 4120
  2.8 0.8 %copy-done.2 = f32[4,16,16]{2,1,0:T(8,128)S(1)} copy-done((f32[4,16,16]{2,1,0:T(8,128)S(1)}, f32[4,16,16]{2,1,0:T(8,128)}, u32[]{:S(2)}) %copy-start.2) | copy-done | bytes 4120
  3.6 0.8 %copy-done.3 = s32[4,16,16]{2,1,0:T(8,128)S(1)} copy-done((s32[4,16,16]{2,1,0:T(8,128)S(1)}, s32[4,16,16]{2,1,0:T(8,128)}, u32[]{:S(2)}) %copy-start.3) | copy-done | bytes 4120
  4.3 0.1 pack.1
  4.4 0.7 collective-permute-start.1
  5.1 4.6 %collective-permute-start = (f32[32,128]{1,0:T(8,128)S(1)}, f32[32,128]{1,0:T(8,128)S(1)}, u32[]{:S(2)}, u32[]{:S(2)}) collective-permute-start(f32[32,128]{1,0:T(8,128)S(1)} %pack.1), channel_id=1, source_target_pairs={{0,1},{1,0},{2,3},{3,2},{4,5},{5,4},{6,7},{7,6},{8,9},{9,8},{10,11... | collective-permute-start | bytes 49160 | tf_op jit(solution)/shard_map/ppermute | solution.py:368
  9.7 0.7 copy-done.4
  10.4 0.1 bitcast_select_fusion.index
  10.4 0.1 pad_add_fusion.info
  10.5 0.3 collective-permute-done
  10.8 4.3 %collective-permute-start.4 = (f32[96,128]{1,0:T(8,128)S(1)}, f32[96,128]{1,0:T(8,128)S(1)}, u32[]{:S(2)}, u32[]{:S(2)}) collective-permute-start(f32[96,128]{1,0:T(8,128)S(1)} %pad_maximum_fusion), channel_id=1, source_target_pairs={{0,192},{32,224},{64,128},{96,160},{128,64},{160,96},{192,0},{224,... | collective-permute-start | bytes 147464 | tf_op jit(solution)/shard_map/ppermute | solution.py:368
  15.1 0.4 collective-permute-start.2
  15.5 2.9 %collective-permute-done.2 = f32[96,128]{1,0:T(8,128)S(1)} collective-permute-done((f32[96,128]{1,0:T(8,128)S(1)}, f32[96,128]{1,0:T(8,128)S(1)}, u32[]{:S(2)}, u32[]{:S(2)}) %collective-permute-start.2) | collective-permute-done | bytes 49184 | tf_op jit(solution)/shard_map/ppermute | solution.py:368
  18.4 0.8 %collective-permute-done.3 = f32[96,128]{1,0:T(8,128)S(1)} collective-permute-done((f32[96,128]{1,0:T(8,128)S(1)}, f32[96,128]{1,0:T(8,128)S(1)}, u32[]{:S(2)}, u32[]{:S(2)}) %collective-permute-start.3) | collective-permute-done | bytes 49184 | tf_op jit(solution)/shard_map/ppermute | solution.py:368
  19.2 0.0 collective-permute-done.4
  19.2 3.2 %collective-permute-start.5 = (f32[384,128]{1,0:T(8,128)S(1)}, f32[384,128]{1,0:T(8,128)S(1)}, u32[]{:S(2)}, u32[]{:S(2)}) collective-permute-start(f32[384,128]{1,0:T(8,128)S(1)} %constant_dynamic-update-slice_fusion.mine), channel_id=1, source_target_pairs={{0,32},{32,0},{64,96},{96,64},{128,160},{160,128},{192,224},{224,1... | collective-permute-start | bytes 589832 | tf_op jit(solution)/shard_map/ppermute | solution.py:368
  22.4 1.1 %collective-permute-done.5.other = f32[384,128]{1,0:T(8,128)S(1)} collective-permute-done((f32[384,128]{1,0:T(8,128)S(1)}, f32[384,128]{1,0:T(8,128)S(1)}, u32[]{:S(2)}, u32[]{:S(2)}) %collective-permute-start.5) | collective-permute-done | bytes 196640 | tf_op jit(solution)/shard_map/ppermute | solution.py:368
  23.4 8.2 %schwarz.1 = (f32[128,128]{1,0:T(8,128)S(1)}, f32[128,128]{1,0:T(8,128)S(1)}, f32[128,128]{1,0:T(8,128)S(1)}, f32[128,128]{1,0:T(8,128)S(1)}) custom-call(s32[3]{0:T(128)S(1)} %pad_add_fusion.info, f32[384,128]{1,0:T(8,128)S(1)} %constant_dynamic-update-slice_fusion.mine, f32[384,128]{1,0:T(8,128)S(1)} %collective-permute-done.5.other), custom_call_target="tpu_custom_call" | custom-call | tf_op jit(solution)/shard_map/schwarz/pallas_call | solution.py:269
  31.7 0.3 collective-permute-start.6
  32.0 1.6 %collective-permute-start.7 = (f32[128,128]{1,0:T(8,128)S(1)}, f32[128,128]{1,0:T(8,128)S(1)}, u32[]{:S(2)}, u32[]{:S(2)}) collective-permute-start(f32[128,128]{1,0:T(8,128)S(1)} %get-tuple-element.16), channel_id=1, source_target_pairs={{0,128},{32,160},{64,192},{96,224},{128,0},{160,32},{192,64},{224,... | collective-permute-start | bytes 196616 | tf_op jit(solution)/shard_map/ppermute | solution.py:368
  33.6 1.7 %collective-permute-start.8 = (f32[128,128]{1,0:T(8,128)S(1)}, f32[128,128]{1,0:T(8,128)S(1)}, u32[]{:S(2)}, u32[]{:S(2)}) collective-permute-start(f32[128,128]{1,0:T(8,128)S(1)} %get-tuple-element.17), channel_id=1, source_target_pairs={{0,192},{32,224},{64,128},{96,160},{128,64},{160,96},{192,0},{224,... | collective-permute-start | bytes 196616 | tf_op jit(solution)/shard_map/ppermute | solution.py:368
  35.3 1.2 %collective-permute-start.9 = (f32[128,128]{1,0:T(8,128)S(1)}, f32[128,128]{1,0:T(8,128)S(1)}, u32[]{:S(2)}, u32[]{:S(2)}) collective-permute-start(f32[128,128]{1,0:T(8,128)S(1)} %get-tuple-element.14.refs_0_), channel_id=1, source_target_pairs={{0,32},{32,0},{64,96},{96,64},{128,160},{160,128},{192,224},{224,1... | collective-permute-start | bytes 196616 | tf_op jit(solution)/shard_map/ppermute | solution.py:368
  36.5 0.6 collective-permute-start.10
  37.1 0.0 collective-permute-done.7.refs_2_
  37.1 3.8 %collective-permute-start.11 = (f32[128,128]{1,0:T(8,128)S(1)}, f32[128,128]{1,0:T(8,128)S(1)}, u32[]{:S(2)}, u32[]{:S(2)}) collective-permute-start(f32[128,128]{1,0:T(8,128)S(1)} %collective-permute-done.7.refs_2_), channel_id=1, source_target_pairs={{0,32},{32,0},{64,96},{96,64},{128,160},{160,128},{192,224},{224,1... | collective-permute-start | bytes 196616 | tf_op jit(solution)/shard_map/ppermute | solution.py:368
  40.9 0.0 collective-permute-start.12
  41.0 0.9 %collective-permute-done.11.refs_6_ = f32[128,128]{1,0:T(8,128)S(1)} collective-permute-done((f32[128,128]{1,0:T(8,128)S(1)}, f32[128,128]{1,0:T(8,128)S(1)}, u32[]{:S(2)}, u32[]{:S(2)}) %collective-permute-start.11) | collective-permute-done | bytes 65568 | tf_op jit(solution)/shard_map/ppermute | solution.py:368
  41.8 0.4 collective-permute-done.12.refs_7_
  42.2 2.2 %place.1 = (f32[64,1024]{1,0:T(8,128)}, f32[128,128]{1,0:T(8,128)S(1)}) custom-call(s32[3]{0:T(128)S(1)} %pad_add_fusion.info, s32[8,32]{1,0:T(8,128)S(1)} %bitcast_select_fusion.index, f32[128,128]{1,0:T(8,128)S(1)} %get-tuple-element.14.refs_0_, f32[128,128]{1,0:T(8,128)S(1)} %collective-permute-done.6.refs_1_, ...), custom_call_target="tpu_custom_call" | custom-call | tf_op jit(solution)/shard_map/place/pallas_call | solution.py:324
  44.4 24.9 %all_to_all.5 = f32[32,4,128]{2,1,0:T(4,128)S(1)} all-to-all(f32[32,4,128]{2,1,0:T(4,128)S(1)} %bitcast.19), channel_id=1, replica_groups=mesh['gx'=8,'gy'=32] {'gy'}, dimensions={0} | all-to-all | bytes 131072 | tf_op jit(solution)/shard_map/all_to_all | solution.py:408
  69.2 0.9 %finish.1 = f32[64,256]{1,0:T(8,128)} custom-call(f32[128,128]{1,0:T(8,128)S(1)} %bitcast.18), custom_call_target="tpu_custom_call" | custom-call | tf_op jit(solution)/shard_map/finish/pallas_call | solution.py:357
  (19 shorter events, 0.1 us)
Async XLA Ops:
  1.3 0.8 %copy-start = (f32[4,16,16]{2,1,0:T(8,128)S(1)}, f32[4,16,16]{2,1,0:T(8,128)}, u32[]{:S(2)}) copy-start(f32[4,16,16]{2,1,0:T(8,128)} %conductivity.1) | copy-start | bytes 12292
  2.0 0.8 %copy-start.1 = (f32[4,16,16]{2,1,0:T(8,128)S(1)}, f32[4,16,16]{2,1,0:T(8,128)}, u32[]{:S(2)}) copy-start(f32[4,16,16]{2,1,0:T(8,128)} %storage.1) | copy-start | bytes 12292
  2.8 0.8 %copy-start.2 = (f32[4,16,16]{2,1,0:T(8,128)S(1)}, f32[4,16,16]{2,1,0:T(8,128)}, u32[]{:S(2)}) copy-start(f32[4,16,16]{2,1,0:T(8,128)} %head.1) | copy-start | bytes 12292
  3.6 0.8 %copy-start.3 = (s32[4,16,16]{2,1,0:T(8,128)S(1)}, s32[4,16,16]{2,1,0:T(8,128)}, u32[]{:S(2)}) copy-start(s32[4,16,16]{2,1,0:T(8,128)} %zone.1) | copy-start | bytes 12292
  4.4 6.1 %collective-permute-start.1 = (f32[32,128]{1,0:T(8,128)S(1)}, f32[32,128]{1,0:T(8,128)S(1)}, u32[]{:S(2)}, u32[]{:S(2)}) collective-permute-start(f32[32,128]{1,0:T(8,128)S(1)} %pack.1), channel_id=1, source_target_pairs={{1,2},{3,4},{5,6},{7,8},{9,10},{11,12},{13,14},{15,16},{17,18},{19... | collective-permute-start | bytes 49160 | tf_op jit(solution)/shard_map/ppermute | solution.py:368
  5.1 5.7 %collective-permute-start = (f32[32,128]{1,0:T(8,128)S(1)}, f32[32,128]{1,0:T(8,128)S(1)}, u32[]{:S(2)}, u32[]{:S(2)}) collective-permute-start(f32[32,128]{1,0:T(8,128)S(1)} %pack.1), channel_id=1, source_target_pairs={{0,1},{1,0},{2,3},{3,2},{4,5},{5,4},{6,7},{7,6},{8,9},{9,8},{10,11... | collective-permute-start | bytes 49160 | tf_op jit(solution)/shard_map/ppermute | solution.py:368
  9.7 0.7 copy-start.4
  9.7 0.7 copy-start.5
  10.8 8.4 %collective-permute-start.4 = (f32[96,128]{1,0:T(8,128)S(1)}, f32[96,128]{1,0:T(8,128)S(1)}, u32[]{:S(2)}, u32[]{:S(2)}) collective-permute-start(f32[96,128]{1,0:T(8,128)S(1)} %pad_maximum_fusion), channel_id=1, source_target_pairs={{0,192},{32,224},{64,128},{96,160},{128,64},{160,96},{192,0},{224,... | collective-permute-start | bytes 147464 | tf_op jit(solution)/shard_map/ppermute | solution.py:368
  15.1 4.0 %collective-permute-start.3 = (f32[96,128]{1,0:T(8,128)S(1)}, f32[96,128]{1,0:T(8,128)S(1)}, u32[]{:S(2)}, u32[]{:S(2)}) collective-permute-start(f32[96,128]{1,0:T(8,128)S(1)} %pad_maximum_fusion), channel_id=1, source_target_pairs={{0,128},{32,160},{64,192},{96,224},{128,0},{160,32},{192,64},{224,... | collective-permute-start | bytes 147464 | tf_op jit(solution)/shard_map/ppermute | solution.py:368
  15.1 3.2 %collective-permute-start.2 = (f32[96,128]{1,0:T(8,128)S(1)}, f32[96,128]{1,0:T(8,128)S(1)}, u32[]{:S(2)}, u32[]{:S(2)}) collective-permute-start(f32[96,128]{1,0:T(8,128)S(1)} %pad_maximum_fusion), channel_id=1, source_target_pairs={{0,64},{32,96},{64,0},{96,32},{128,192},{160,224},{192,128},{224,1... | collective-permute-start | bytes 147464 | tf_op jit(solution)/shard_map/ppermute | solution.py:368
  19.2 4.2 %collective-permute-start.5 = (f32[384,128]{1,0:T(8,128)S(1)}, f32[384,128]{1,0:T(8,128)S(1)}, u32[]{:S(2)}, u32[]{:S(2)}) collective-permute-start(f32[384,128]{1,0:T(8,128)S(1)} %constant_dynamic-update-slice_fusion.mine), channel_id=1, source_target_pairs={{0,32},{32,0},{64,96},{96,64},{128,160},{160,128},{192,224},{224,1... | collective-permute-start | bytes 589832 | tf_op jit(solution)/shard_map/ppermute | solution.py:368
  31.7 4.9 %collective-permute-start.6 = (f32[128,128]{1,0:T(8,128)S(1)}, f32[128,128]{1,0:T(8,128)S(1)}, u32[]{:S(2)}, u32[]{:S(2)}) collective-permute-start(f32[128,128]{1,0:T(8,128)S(1)} %get-tuple-element.15), channel_id=1, source_target_pairs={{0,64},{32,96},{64,0},{96,32},{128,192},{160,224},{192,128},{224,1... | collective-permute-start | bytes 196616 | tf_op jit(solution)/shard_map/ppermute | solution.py:368
  32.0 5.1 %collective-permute-start.7 = (f32[128,128]{1,0:T(8,128)S(1)}, f32[128,128]{1,0:T(8,128)S(1)}, u32[]{:S(2)}, u32[]{:S(2)}) collective-permute-start(f32[128,128]{1,0:T(8,128)S(1)} %get-tuple-element.16), channel_id=1, source_target_pairs={{0,128},{32,160},{64,192},{96,224},{128,0},{160,32},{192,64},{224,... | collective-permute-start | bytes 196616 | tf_op jit(solution)/shard_map/ppermute | solution.py:368
  33.6 7.3 %collective-permute-start.8 = (f32[128,128]{1,0:T(8,128)S(1)}, f32[128,128]{1,0:T(8,128)S(1)}, u32[]{:S(2)}, u32[]{:S(2)}) collective-permute-start(f32[128,128]{1,0:T(8,128)S(1)} %get-tuple-element.17), channel_id=1, source_target_pairs={{0,192},{32,224},{64,128},{96,160},{128,64},{160,96},{192,0},{224,... | collective-permute-start | bytes 196616 | tf_op jit(solution)/shard_map/ppermute | solution.py:368
  35.3 5.6 %collective-permute-start.9 = (f32[128,128]{1,0:T(8,128)S(1)}, f32[128,128]{1,0:T(8,128)S(1)}, u32[]{:S(2)}, u32[]{:S(2)}) collective-permute-start(f32[128,128]{1,0:T(8,128)S(1)} %get-tuple-element.14.refs_0_), channel_id=1, source_target_pairs={{0,32},{32,0},{64,96},{96,64},{128,160},{160,128},{192,224},{224,1... | collective-permute-start | bytes 196616 | tf_op jit(solution)/shard_map/ppermute | solution.py:368
  36.5 4.4 %collective-permute-start.10 = (f32[128,128]{1,0:T(8,128)S(1)}, f32[128,128]{1,0:T(8,128)S(1)}, u32[]{:S(2)}, u32[]{:S(2)}) collective-permute-start(f32[128,128]{1,0:T(8,128)S(1)} %collective-permute-done.6.refs_1_), channel_id=1, source_target_pairs={{0,32},{32,0},{64,96},{96,64},{128,160},{160,128},{192,224},{224,1... | collective-permute-start | bytes 196616 | tf_op jit(solution)/shard_map/ppermute | solution.py:368
  37.1 4.7 %collective-permute-start.11 = (f32[128,128]{1,0:T(8,128)S(1)}, f32[128,128]{1,0:T(8,128)S(1)}, u32[]{:S(2)}, u32[]{:S(2)}) collective-permute-start(f32[128,128]{1,0:T(8,128)S(1)} %collective-permute-done.7.refs_2_), channel_id=1, source_target_pairs={{0,32},{32,0},{64,96},{96,64},{128,160},{160,128},{192,224},{224,1... | collective-permute-start | bytes 196616 | tf_op jit(solution)/shard_map/ppermute | solution.py:368
  40.9 1.3 %collective-permute-start.12 = (f32[128,128]{1,0:T(8,128)S(1)}, f32[128,128]{1,0:T(8,128)S(1)}, u32[]{:S(2)}, u32[]{:S(2)}) collective-permute-start(f32[128,128]{1,0:T(8,128)S(1)} %collective-permute-done.8.refs_3_), channel_id=1, source_target_pairs={{0,32},{32,0},{64,96},{96,64},{128,160},{160,128},{192,224},{224,1... | collective-permute-start | bytes 196616 | tf_op jit(solution)/shard_map/ppermute | solution.py:368

commit v5 on v4

--- a/solution.py
+++ b/solution.py
@@ -39,11 +39,14 @@
     return jnp.where(sub_places() == SUBX - 1, 0.0, pltpu.roll(field, SUBX - 1, 0))
 
 
-def layers_sum(field):
+def layers_sums(fields):
     lanes = lane_places()
-    above = jnp.where(lanes >= TILE[1] - GROUP, 0.0, pltpu.roll(field, TILE[1] - GROUP, 1))
-    below = jnp.where(lanes < GROUP, 0.0, pltpu.roll(field, GROUP, 1))
-    return (field + above) + (field + below)
+    above = [pltpu.roll(field, TILE[1] - GROUP, 1) for field in fields]
+    below = [pltpu.roll(field, GROUP, 1) for field in fields]
+    return [
+        (field + jnp.where(lanes >= TILE[1] - GROUP, 0.0, up)) + (field + jnp.where(lanes < GROUP, 0.0, down))
+        for field, up, down in zip(fields, above, below)
+    ]
 
 
 def rows_sum(cells):
@@ -95,21 +98,20 @@
     picks = [[half * 64 + part * LAYERS + lanes // GROUP for part in range(4)] for half in range(2)]
     bases = (2 * OWN - odd * OWN, 0, OWN + odd * OWN)
 
+    for half in range(2):
+        for part, target in enumerate((cond, store, head, zone)):
+            for col in range(WIDE):
+                block, place = divmod(col - HALO + COLS, COLS)
+                if place // HALF != half:
+                    continue
+                for row in range(ROWS):
+                    packed = raw[pl.ds(bases[block] + row * HALF + place % HALF, SUBX, stride=BLOCK), :]
+                    target[col, row + (part == 0)] = jnp.take_along_axis(
+                        packed, picks[half][part], axis=1, mode="promise_in_bounds"
+                    )
     for col in range(WIDE):
-        block, place = divmod(col - HALO + COLS, COLS)
-        conds = []
-        for row in range(ROWS):
-            packed = raw[pl.ds(bases[block] + row * HALF + place % HALF, SUBX, stride=BLOCK), :]
-            parts = [
-                jnp.take_along_axis(packed, places, axis=1, mode="promise_in_bounds")
-                for places in picks[place // HALF]
-            ]
-            conds.append(parts[0])
-            store[col, row] = parts[1]
-            head[col, row] = parts[2]
-            zone[col, row] = parts[3]
-        for row, field in enumerate([up_sub(conds[-1])] + conds + [down_sub(conds[0])]):
-            cond[col, row] = field
+        cond[col, 0] = up_sub(cond[col, ROWS])
+        cond[col, ROWS + 1] = down_sub(cond[col, 1])
 
 
 def coefficients(zone_base, cond, store, head, zone, keep, gain, source):
@@ -117,7 +119,7 @@
 
     def column(col):
         sums = rows_sum([cond[col, row] for row in range(ROWS + 2)])
-        return [layers_sum(field) for field in sums]
+        return layers_sums(sums)
 
     def emit(col, around):
         keeps, gains, sources = [], [], []
@@ -180,15 +182,15 @@
                 old, new = fields[part][(sweep + 1) % 2], fields[part][sweep % 2]
                 first, last = ranges[part]
                 if outer == 0 and sweep == 0:
-                    def copy(col, carry, new=new, base=base):
-                        for row in range(6):
-                            new[col - base, row] = source[col, row]
-                        return carry
-                    lax.fori_loop(first, last + 1, copy, 0, unroll=True)
                     continue
-
-                def column(col, old=old, base=base, sweep=sweep, outer=outer):
-                    if sweep == 0:
+                begun = outer == 0 and sweep == 1
+
+                def column(col, old=old, base=base, sweep=sweep, outer=outer, begun=begun, rim=rims[part]):
+                    if begun and col in rim:
+                        return [zeros] * 6
+                    if begun:
+                        cells = [None] + [source[col, row] for row in range(6)] + [None]
+                    elif sweep == 0:
                         cells = [state[col, row] for row in range(8)]
                     else:
                         cells = [old[col - base, row] for row in range(6)]
@@ -196,11 +198,14 @@
                             cells = [None] + cells + [None]
                         else:
                             cells = [state[col, 0]] + cells + [state[col, 7]]
-                    return [layers_sum(field) for field in rows_sum(cells)]
-
-                def emit(col, around, old=old, new=new, base=base, sweep=sweep):
+                    return layers_sums(rows_sum(cells))
+
+                def emit(col, around, old=old, new=new, base=base, sweep=sweep, begun=begun):
                     for row in range(6):
-                        here = state[col, row + 1] if sweep == 0 else old[col - base, row]
+                        if begun:
+                            here = source[col, row]
+                        else:
+                            here = state[col, row + 1] if sweep == 0 else old[col - base, row]
                         new[col - base, row] = (
                             source[col, row] + keep[col, row] * here + gain[col, row] * around[row]
                         )
@@ -292,12 +297,12 @@
     return fields
 
 
-def place_kernel(info, index, *refs):
-    pieces, (tangent, picks, parts, table) = refs[:SUBX], refs[SUBX:]
+def place_kernel(info, index, near, far, tangent, picks, parts, table):
     lanes = lane_places()
     for place in range(SUBX):
         side = place % 2
-        chunk = pieces[side * 4 + place // 2][side * PLACES : (side + 1) * PLACES, :]
+        start = (2 * (3 - place // 2) + side) * PLACES
+        chunk = (near, far)[side][start : start + PLACES, :]
         parts[pl.ds(pl.multiple_of((info[0] ^ place) * PLACES, 8), PLACES), :] = chunk
     order = (lanes % ZONES) // GROUP * 16 + lanes // ZONES * GROUP + lanes % GROUP
     entries = PLACES * LAYERS // 2
@@ -327,7 +332,7 @@
             jax.ShapeDtypeStruct((PLACES, LAYERS * ZONES), jnp.float32),
             jax.ShapeDtypeStruct((SUBY * CAP // 2, 128), jnp.float32),
         ),
-        in_specs=[pl.BlockSpec(memory_space=pltpu.SMEM)] * 2 + [pl.BlockSpec(memory_space=pltpu.VMEM)] * 8,
+        in_specs=[pl.BlockSpec(memory_space=pltpu.SMEM)] * 2 + [pl.BlockSpec(memory_space=pltpu.VMEM)] * 2,
         out_specs=(pl.BlockSpec(memory_space=pltpu.VMEM),) * 2,
         scratch_shapes=[
             pltpu.VMEM((SUBX * PLACES, 128), jnp.float32),
@@ -402,8 +407,8 @@
     )
     sends = run_main(info, mine, other)
     near = [sends[0]] + [swap(sends[k], "gx", partners(2 * k)) for k in (1, 2, 3)]
-    far = [swap(part, "gx", partners(1)) for part in near]
-    tangent, picks = run_place(info, index, near + far)
+    near = jnp.concatenate(near[::-1], axis=0)
+    tangent, picks = run_place(info, index, (near, swap(near, "gx", partners(1))))
     picks = picks.reshape(SUBY, CAP // 2, 128)
     arrived = lax.all_to_all(picks, "gy", split_axis=0, concat_axis=0, tiled=True)
     wells = run_finish(arrived.reshape(SUBY * CAP // 2, 128)).T

time: 70.6 us -> 70.2 us (level)
  starting transfers between devices: 22.4 us -> 17.4 us
  waiting for transfers between devices: 6.23 us -> 11.2 us
    ppermute x13 -> x10, starting transfers between devices: 22.4 us -> 17.4 us  [swap(): return lax.ppermute(array, axis, pairs)]
    ppermute x13 -> x10, waiting for transfers between devices: 6.23 us -> 11.2 us  [swap(): return lax.ppermute(array, axis, pairs)]
    unnamed x15 -> x18, local copies, waits for them, and re-layouts: 3.72 us -> 3.74 us
  transfers between devices with their start and end apart: 13 -> 10, of which waited for: 6 -> 7; matrix products, arithmetic and copies ran while one was open for 0% -> 0% of each run, Pallas kernels for 0% -> 0%
where the time goes in v5:
time: 70.2 us; the launch traced here: 69.8 us
  blocking collectives  24.7 us (35%)
  starting transfers between devices  17.4 us (25%)
  Pallas kernels  11.3 us (16%)
  waiting for transfers between devices  11.2 us (16%)
  local copies, waits for them, and re-layouts  3.76 us (5%)
  between operations  1.36 us (2%)
    all_to_all x1, blocking collectives, shards(): lax.all_to_all(picks, 'gy', split_axis=0, concat_axis=0, tiled=True)  24.7 us
    ppermute x10, starting transfers between devices, swap(): return lax.ppermute(array, axis, pairs)  17.4 us
    ppermute x10, waiting for transfers between devices, swap(): return lax.ppermute(array, axis, pairs)  11.2 us
    pallas_call x1, Pallas kernels, run_main(): pl.pallas_call(main_kernel, out_shape=(jax.ShapeDtypeStruct((2 * PLACES,...  8.13 us
    unnamed x18, local copies, waits for them, and re-layouts  3.74 us
    pallas_call x1, Pallas kernels, run_place(): pl.pallas_call(place_kernel, out_shape=(jax.ShapeDtypeStruct((PLACES, LAY...  2.16 us
  transfers between devices with their start and end apart: 10, of which 7 were waited for; matrix products, arithmetic and copies ran while one was open for 0% of the time, Pallas kernels for 0%

profile of v5, /device:TPU:1, one launch (start us, length us, event | category | flops | bytes accessed | tf_op | source)
XLA Modules:
  0.0 69.8 jit_solution(17606706629946167038)
XLA Ops:
  1.3 0.7 %copy-done = f32[4,16,16]{2,1,0:T(8,128)S(1)} copy-done((f32[4,16,16]{2,1,0:T(8,128)S(1)}, f32[4,16,16]{2,1,0:T(8,128)}, u32[]{:S(2)}) %copy-start) | copy-done | bytes 4120
  2.0 0.8 %copy-done.1 = f32[4,16,16]{2,1,0:T(8,128)S(1)} copy-done((f32[4,16,16]{2,1,0:T(8,128)S(1)}, f32[4,16,16]{2,1,0:T(8,128)}, u32[]{:S(2)}) %copy-start.1) | copy-done | bytes 4120
  2.8 0.8 %copy-done.2 = f32[4,16,16]{2,1,0:T(8,128)S(1)} copy-done((f32[4,16,16]{2,1,0:T(8,128)S(1)}, f32[4,16,16]{2,1,0:T(8,128)}, u32[]{:S(2)}) %copy-start.2) | copy-done | bytes 4120
  3.6 0.8 %copy-done.3 = s32[4,16,16]{2,1,0:T(8,128)S(1)} copy-done((s32[4,16,16]{2,1,0:T(8,128)S(1)}, s32[4,16,16]{2,1,0:T(8,128)}, u32[]{:S(2)}) %copy-start.3) | copy-done | bytes 4120
  4.3 0.1 pack.1
  4.4 0.7 collective-permute-start.1
  5.1 4.6 %collective-permute-start = (f32[32,128]{1,0:T(8,128)S(1)}, f32[32,128]{1,0:T(8,128)S(1)}, u32[]{:S(2)}, u32[]{:S(2)}) collective-permute-start(f32[32,128]{1,0:T(8,128)S(1)} %pack.1), channel_id=1, source_target_pairs={{0,1},{1,0},{2,3},{3,2},{4,5},{5,4},{6,7},{7,6},{8,9},{9,8},{10,11... | collective-permute-start | bytes 49160 | tf_op jit(solution)/shard_map/ppermute | solution.py:373
  9.7 0.7 copy-done.4
  10.4 0.1 bitcast_select_fusion.index
  10.4 0.1 pad_add_fusion.info
  10.5 0.0 collective-permute-done.1
  10.5 0.3 collective-permute-done
  10.8 4.3 %collective-permute-start.4 = (f32[96,128]{1,0:T(8,128)S(1)}, f32[96,128]{1,0:T(8,128)S(1)}, u32[]{:S(2)}, u32[]{:S(2)}) collective-permute-start(f32[96,128]{1,0:T(8,128)S(1)} %pad_maximum_fusion), channel_id=1, source_target_pairs={{0,192},{32,224},{64,128},{96,160},{128,64},{160,96},{192,0},{224,... | collective-permute-start | bytes 147464 | tf_op jit(solution)/shard_map/ppermute | solution.py:373
  15.1 0.0 collective-permute-start.3
  15.1 0.4 collective-permute-start.2
  15.5 2.9 %collective-permute-done.2 = f32[96,128]{1,0:T(8,128)S(1)} collective-permute-done((f32[96,128]{1,0:T(8,128)S(1)}, f32[96,128]{1,0:T(8,128)S(1)}, u32[]{:S(2)}, u32[]{:S(2)}) %collective-permute-start.2) | collective-permute-done | bytes 49184 | tf_op jit(solution)/shard_map/ppermute | solution.py:373
  18.4 0.8 %collective-permute-done.3 = f32[96,128]{1,0:T(8,128)S(1)} collective-permute-done((f32[96,128]{1,0:T(8,128)S(1)}, f32[96,128]{1,0:T(8,128)S(1)}, u32[]{:S(2)}, u32[]{:S(2)}) %collective-permute-start.3) | collective-permute-done | bytes 49184 | tf_op jit(solution)/shard_map/ppermute | solution.py:373
  19.2 0.0 collective-permute-done.4
  19.2 3.2 %collective-permute-start.5 = (f32[384,128]{1,0:T(8,128)S(1)}, f32[384,128]{1,0:T(8,128)S(1)}, u32[]{:S(2)}, u32[]{:S(2)}) collective-permute-start(f32[384,128]{1,0:T(8,128)S(1)} %constant_dynamic-update-slice_fusion.mine), channel_id=1, source_target_pairs={{0,32},{32,0},{64,96},{96,64},{128,160},{160,128},{192,224},{224,1... | collective-permute-start | bytes 589832 | tf_op jit(solution)/shard_map/ppermute | solution.py:373
  22.4 1.1 %collective-permute-done.5.other = f32[384,128]{1,0:T(8,128)S(1)} collective-permute-done((f32[384,128]{1,0:T(8,128)S(1)}, f32[384,128]{1,0:T(8,128)S(1)}, u32[]{:S(2)}, u32[]{:S(2)}) %collective-permute-start.5) | collective-permute-done | bytes 196640 | tf_op jit(solution)/shard_map/ppermute | solution.py:373
  23.4 8.1 %schwarz.1 = (f32[128,128]{1,0:T(8,128)S(1)}, f32[128,128]{1,0:T(8,128)S(1)}, f32[128,128]{1,0:T(8,128)S(1)}, f32[128,128]{1,0:T(8,128)S(1)}) custom-call(s32[3]{0:T(128)S(1)} %pad_add_fusion.info, f32[384,128]{1,0:T(8,128)S(1)} %constant_dynamic-update-slice_fusion.mine, f32[384,128]{1,0:T(8,128)S(1)} %collective-permute-done.5.other), custom_call_target="tpu_custom_call" | custom-call | tf_op jit(solution)/shard_map/schwarz/pallas_call | solution.py:274
  31.6 1.4 %collective-permute-start.6 = (f32[128,128]{1,0:T(8,128)S(1)}, f32[128,128]{1,0:T(8,128)S(1)}, u32[]{:S(2)}, u32[]{:S(2)}) collective-permute-start(f32[128,128]{1,0:T(8,128)S(1)} %get-tuple-element.14), channel_id=1, source_target_pairs={{0,192},{32,224},{64,128},{96,160},{128,64},{160,96},{192,0},{224,... | collective-permute-start | bytes 196616 | tf_op jit(solution)/shard_map/ppermute | solution.py:373
  32.9 0.6 collective-permute-start.7
  33.5 1.7 %collective-permute-start.8 = (f32[128,128]{1,0:T(8,128)S(1)}, f32[128,128]{1,0:T(8,128)S(1)}, u32[]{:S(2)}, u32[]{:S(2)}) collective-permute-start(f32[128,128]{1,0:T(8,128)S(1)} %get-tuple-element.16), channel_id=1, source_target_pairs={{0,64},{32,96},{64,0},{96,32},{128,192},{160,224},{192,128},{224,1... | collective-permute-start | bytes 196616 | tf_op jit(solution)/shard_map/ppermute | solution.py:373
  35.2 1.4 %collective-permute-done.6 = f32[128,128]{1,0:T(8,128)S(1)} collective-permute-done((f32[128,128]{1,0:T(8,128)S(1)}, f32[128,128]{1,0:T(8,128)S(1)}, u32[]{:S(2)}, u32[]{:S(2)}) %collective-permute-start.6) | collective-permute-done | bytes 65568 | tf_op jit(solution)/shard_map/ppermute | solution.py:373
  36.6 3.6 %collective-permute-done.7 = f32[128,128]{1,0:T(8,128)S(1)} collective-permute-done((f32[128,128]{1,0:T(8,128)S(1)}, f32[128,128]{1,0:T(8,128)S(1)}, u32[]{:S(2)}, u32[]{:S(2)}) %collective-permute-start.7) | collective-permute-done | bytes 65568 | tf_op jit(solution)/shard_map/ppermute | solution.py:373
  40.2 0.0 collective-permute-done.8
  40.3 0.6 collective-permute-start.9
  40.9 1.2 %collective-permute-done.9.far = f32[512,128]{1,0:T(8,128)S(1)} collective-permute-done((f32[512,128]{1,0:T(8,128)S(1)}, f32[512,128]{1,0:T(8,128)S(1)}, u32[]{:S(2)}, u32[]{:S(2)}) %collective-permute-start.9) | collective-permute-done | bytes 262176 | tf_op jit(solution)/shard_map/ppermute | solution.py:373
  42.1 2.2 %place.1 = (f32[64,1024]{1,0:T(8,128)}, f32[128,128]{1,0:T(8,128)S(1)}) custom-call(s32[3]{0:T(128)S(1)} %pad_add_fusion.info, s32[8,32]{1,0:T(8,128)S(1)} %bitcast_select_fusion.index, f32[512,128]{1,0:T(8,128)S(1)} %constant_dynamic-update-slice_fusion.4.near, f32[512,128]{1,0:T(8,128)S(1)} %collective-permute-done.9.far), custom_call_target="tpu_custom_call" | custom-call | tf_op jit(solution)/shard_map/place/pallas_call | solution.py:329
  44.2 24.7 %all_to_all.5 = f32[32,4,128]{2,1,0:T(4,128)S(1)} all-to-all(f32[32,4,128]{2,1,0:T(4,128)S(1)} %bitcast.19), channel_id=1, replica_groups=mesh['gx'=8,'gy'=32] {'gy'}, dimensions={0} | all-to-all | bytes 131072 | tf_op jit(solution)/shard_map/all_to_all | solution.py:413
  68.9 0.9 %finish.1 = f32[64,256]{1,0:T(8,128)} custom-call(f32[128,128]{1,0:T(8,128)S(1)} %bitcast.18), custom_call_target="tpu_custom_call" | custom-call | tf_op jit(solution)/shard_map/finish/pallas_call | solution.py:362
  (17 shorter events, 0.1 us)
Async XLA Ops:
  1.3 0.8 %copy-start = (f32[4,16,16]{2,1,0:T(8,128)S(1)}, f32[4,16,16]{2,1,0:T(8,128)}, u32[]{:S(2)}) copy-start(f32[4,16,16]{2,1,0:T(8,128)} %conductivity.1) | copy-start | bytes 12292
  2.0 0.8 %copy-start.1 = (f32[4,16,16]{2,1,0:T(8,128)S(1)}, f32[4,16,16]{2,1,0:T(8,128)}, u32[]{:S(2)}) copy-start(f32[4,16,16]{2,1,0:T(8,128)} %storage.1) | copy-start | bytes 12292
  2.8 0.8 %copy-start.2 = (f32[4,16,16]{2,1,0:T(8,128)S(1)}, f32[4,16,16]{2,1,0:T(8,128)}, u32[]{:S(2)}) copy-start(f32[4,16,16]{2,1,0:T(8,128)} %head.1) | copy-start | bytes 12292
  3.6 0.8 %copy-start.3 = (s32[4,16,16]{2,1,0:T(8,128)S(1)}, s32[4,16,16]{2,1,0:T(8,128)}, u32[]{:S(2)}) copy-start(s32[4,16,16]{2,1,0:T(8,128)} %zone.1) | copy-start | bytes 12292
  4.4 6.1 %collective-permute-start.1 = (f32[32,128]{1,0:T(8,128)S(1)}, f32[32,128]{1,0:T(8,128)S(1)}, u32[]{:S(2)}, u32[]{:S(2)}) collective-permute-start(f32[32,128]{1,0:T(8,128)S(1)} %pack.1), channel_id=1, source_target_pairs={{1,2},{3,4},{5,6},{7,8},{9,10},{11,12},{13,14},{15,16},{17,18},{19... | collective-permute-start | bytes 49160 | tf_op jit(solution)/shard_map/ppermute | solution.py:373
  5.1 5.7 %collective-permute-start = (f32[32,128]{1,0:T(8,128)S(1)}, f32[32,128]{1,0:T(8,128)S(1)}, u32[]{:S(2)}, u32[]{:S(2)}) collective-permute-start(f32[32,128]{1,0:T(8,128)S(1)} %pack.1), channel_id=1, source_target_pairs={{0,1},{1,0},{2,3},{3,2},{4,5},{5,4},{6,7},{7,6},{8,9},{9,8},{10,11... | collective-permute-start | bytes 49160 | tf_op jit(solution)/shard_map/ppermute | solution.py:373
  9.7 0.7 copy-start.4
  9.7 0.7 copy-start.5
  10.8 8.4 %collective-permute-start.4 = (f32[96,128]{1,0:T(8,128)S(1)}, f32[96,128]{1,0:T(8,128)S(1)}, u32[]{:S(2)}, u32[]{:S(2)}) collective-permute-start(f32[96,128]{1,0:T(8,128)S(1)} %pad_maximum_fusion), channel_id=1, source_target_pairs={{0,192},{32,224},{64,128},{96,160},{128,64},{160,96},{192,0},{224,... | collective-permute-start | bytes 147464 | tf_op jit(solution)/shard_map/ppermute | solution.py:373
  15.1 4.0 %collective-permute-start.3 = (f32[96,128]{1,0:T(8,128)S(1)}, f32[96,128]{1,0:T(8,128)S(1)}, u32[]{:S(2)}, u32[]{:S(2)}) collective-permute-start(f32[96,128]{1,0:T(8,128)S(1)} %pad_maximum_fusion), channel_id=1, source_target_pairs={{0,128},{32,160},{64,192},{96,224},{128,0},{160,32},{192,64},{224,... | collective-permute-start | bytes 147464 | tf_op jit(solution)/shard_map/ppermute | solution.py:373
  15.1 3.2 %collective-permute-start.2 = (f32[96,128]{1,0:T(8,128)S(1)}, f32[96,128]{1,0:T(8,128)S(1)}, u32[]{:S(2)}, u32[]{:S(2)}) collective-permute-start(f32[96,128]{1,0:T(8,128)S(1)} %pad_maximum_fusion), channel_id=1, source_target_pairs={{0,64},{32,96},{64,0},{96,32},{128,192},{160,224},{192,128},{224,1... | collective-permute-start | bytes 147464 | tf_op jit(solution)/shard_map/ppermute | solution.py:373
  19.2 4.2 %collective-permute-start.5 = (f32[384,128]{1,0:T(8,128)S(1)}, f32[384,128]{1,0:T(8,128)S(1)}, u32[]{:S(2)}, u32[]{:S(2)}) collective-permute-start(f32[384,128]{1,0:T(8,128)S(1)} %constant_dynamic-update-slice_fusion.mine), channel_id=1, source_target_pairs={{0,32},{32,0},{64,96},{96,64},{128,160},{160,128},{192,224},{224,1... | collective-permute-start | bytes 589832 | tf_op jit(solution)/shard_map/ppermute | solution.py:373
  31.6 5.1 %collective-permute-start.6 = (f32[128,128]{1,0:T(8,128)S(1)}, f32[128,128]{1,0:T(8,128)S(1)}, u32[]{:S(2)}, u32[]{:S(2)}) collective-permute-start(f32[128,128]{1,0:T(8,128)S(1)} %get-tuple-element.14), channel_id=1, source_target_pairs={{0,192},{32,224},{64,128},{96,160},{128,64},{160,96},{192,0},{224,... | collective-permute-start | bytes 196616 | tf_op jit(solution)/shard_map/ppermute | solution.py:373
  32.9 7.3 %collective-permute-start.7 = (f32[128,128]{1,0:T(8,128)S(1)}, f32[128,128]{1,0:T(8,128)S(1)}, u32[]{:S(2)}, u32[]{:S(2)}) collective-permute-start(f32[128,128]{1,0:T(8,128)S(1)} %get-tuple-element.15), channel_id=1, source_target_pairs={{0,128},{32,160},{64,192},{96,224},{128,0},{160,32},{192,64},{224,... | collective-permute-start | bytes 196616 | tf_op jit(solution)/shard_map/ppermute | solution.py:373
  33.5 6.7 %collective-permute-start.8 = (f32[128,128]{1,0:T(8,128)S(1)}, f32[128,128]{1,0:T(8,128)S(1)}, u32[]{:S(2)}, u32[]{:S(2)}) collective-permute-start(f32[128,128]{1,0:T(8,128)S(1)} %get-tuple-element.16), channel_id=1, source_target_pairs={{0,64},{32,96},{64,0},{96,32},{128,192},{160,224},{192,128},{224,1... | collective-permute-start | bytes 196616 | tf_op jit(solution)/shard_map/ppermute | solution.py:373
  40.3 1.8 %collective-permute-start.9 = (f32[512,128]{1,0:T(8,128)S(1)}, f32[512,128]{1,0:T(8,128)S(1)}, u32[]{:S(2)}, u32[]{:S(2)}) collective-permute-start(f32[512,128]{1,0:T(8,128)S(1)} %constant_dynamic-update-slice_fusion.4.near), channel_id=1, source_target_pairs={{0,32},{32,0},{64,96},{96,64},{128,160},{160,128},{192,224},{224,1... | collective-permute-start | bytes 786440 | tf_op jit(solution)/shard_map/ppermute | solution.py:373

commit v6 on v5

--- a/solution.py
+++ b/solution.py
@@ -93,10 +93,10 @@
     )(layers, conductivity, storage, head, zone)
 
 
-def expand(odd, raw, cond, store, head, zone):
+def expand(raw, cond, store, head, zone):
     lanes = lane_places()
     picks = [[half * 64 + part * LAYERS + lanes // GROUP for part in range(4)] for half in range(2)]
-    bases = (2 * OWN - odd * OWN, 0, OWN + odd * OWN)
+    bases = (OWN, 0, 2 * OWN)
 
     for half in range(2):
         for part, target in enumerate((cond, store, head, zone)):
@@ -140,15 +140,17 @@
     column_loop(1, WIDE - 2, column, emit)
 
 
-def collect(me, mine, other, raw):
+def collect(me, odd, mine, other, raw):
     for place in range(SUBX):
-        piece = (mine if place % 2 == 0 else other)[pl.ds((place // 2) * BLOCK, BLOCK), :]
-        raw[pl.ds(pl.multiple_of((me ^ place) * BLOCK, 8), BLOCK), :] = piece
+        for part, shift in enumerate((0, 2 * OWN - odd * OWN, OWN + odd * OWN)):
+            start = (place // 2) * BLOCK + part * OWN
+            piece = (mine if place % 2 == 0 else other)[start : start + OWN, :]
+            raw[pl.ds(pl.multiple_of((me ^ place) * BLOCK + shift, 8), OWN), :] = piece
 
 
 def main_kernel(info, mine, other, out0, out2, out4, out6, out, raw, cond, store, head, zone, keep, gain, source, state, *buffers):
-    collect(info[0], mine, other, raw)
-    expand(info[1] & 1, raw, cond, store, head, zone)
+    collect(info[0], info[1] & 1, mine, other, raw)
+    expand(raw, cond, store, head, zone)
     coefficients(info[0] * GROUP, cond, store, head, zone, keep, gain, source)
     has_left, has_right = info[1] > 0, info[2] > 0
     left_own = jnp.where(has_left, 0.5, 1.0)

time: 70.2 us -> 69.9 us (level)
  no operation moved by 1% of the time
where the time goes in v6:
time: 69.9 us; the launch traced here: 69.5 us
  blocking collectives  24.7 us (35%)
  starting transfers between devices  17.4 us (25%)
  waiting for transfers between devices  11.2 us (16%)
  Pallas kernels  11 us (16%)
  local copies, waits for them, and re-layouts  3.76 us (5%)
  between operations  1.36 us (2%)
    all_to_all x1, blocking collectives, shards(): lax.all_to_all(picks, 'gy', split_axis=0, concat_axis=0, tiled=True)  24.7 us
    ppermute x10, starting transfers between devices, swap(): return lax.ppermute(array, axis, pairs)  17.4 us
    ppermute x10, waiting for transfers between devices, swap(): return lax.ppermute(array, axis, pairs)  11.2 us
    pallas_call x1, Pallas kernels, run_main(): pl.pallas_call(main_kernel, out_shape=(jax.ShapeDtypeStruct((2 * PLACES,...  7.84 us
    unnamed x18, local copies, waits for them, and re-layouts  3.74 us
    pallas_call x1, Pallas kernels, run_place(): pl.pallas_call(place_kernel, out_shape=(jax.ShapeDtypeStruct((PLACES, LAY...  2.16 us
  transfers between devices with their start and end apart: 10, of which 7 were waited for; matrix products, arithmetic and copies ran while one was open for 0% of the time, Pallas kernels for 0%

profile of v6, /device:TPU:1, one launch (start us, length us, event | category | flops | bytes accessed | tf_op | source)
XLA Modules:
  0.0 69.5 jit_solution(754465093525453568)
XLA Ops:
  1.3 0.7 %copy-done = f32[4,16,16]{2,1,0:T(8,128)S(1)} copy-done((f32[4,16,16]{2,1,0:T(8,128)S(1)}, f32[4,16,16]{2,1,0:T(8,128)}, u32[]{:S(2)}) %copy-start) | copy-done | bytes 4120
  2.0 0.8 %copy-done.1 = f32[4,16,16]{2,1,0:T(8,128)S(1)} copy-done((f32[4,16,16]{2,1,0:T(8,128)S(1)}, f32[4,16,16]{2,1,0:T(8,128)}, u32[]{:S(2)}) %copy-start.1) | copy-done | bytes 4120
  2.8 0.8 %copy-done.2 = f32[4,16,16]{2,1,0:T(8,128)S(1)} copy-done((f32[4,16,16]{2,1,0:T(8,128)S(1)}, f32[4,16,16]{2,1,0:T(8,128)}, u32[]{:S(2)}) %copy-start.2) | copy-done | bytes 4120
  3.6 0.8 %copy-done.3 = s32[4,16,16]{2,1,0:T(8,128)S(1)} copy-done((s32[4,16,16]{2,1,0:T(8,128)S(1)}, s32[4,16,16]{2,1,0:T(8,128)}, u32[]{:S(2)}) %copy-start.3) | copy-done | bytes 4120
  4.3 0.1 pack.1
  4.4 0.7 collective-permute-start.1
  5.1 4.6 %collective-permute-start = (f32[32,128]{1,0:T(8,128)S(1)}, f32[32,128]{1,0:T(8,128)S(1)}, u32[]{:S(2)}, u32[]{:S(2)}) collective-permute-start(f32[32,128]{1,0:T(8,128)S(1)} %pack.1), channel_id=1, source_target_pairs={{0,1},{1,0},{2,3},{3,2},{4,5},{5,4},{6,7},{7,6},{8,9},{9,8},{10,11... | collective-permute-start | bytes 49160 | tf_op jit(solution)/shard_map/ppermute | solution.py:375
  9.7 0.7 copy-done.4
  10.4 0.1 bitcast_select_fusion.index
  10.4 0.1 pad_add_fusion.info
  10.5 0.0 collective-permute-done.1
  10.5 0.3 collective-permute-done
  10.8 4.3 %collective-permute-start.4 = (f32[96,128]{1,0:T(8,128)S(1)}, f32[96,128]{1,0:T(8,128)S(1)}, u32[]{:S(2)}, u32[]{:S(2)}) collective-permute-start(f32[96,128]{1,0:T(8,128)S(1)} %pad_maximum_fusion), channel_id=1, source_target_pairs={{0,192},{32,224},{64,128},{96,160},{128,64},{160,96},{192,0},{224,... | collective-permute-start | bytes 147464 | tf_op jit(solution)/shard_map/ppermute | solution.py:375
  15.1 0.0 collective-permute-start.3
  15.1 0.4 collective-permute-start.2
  15.5 2.9 %collective-permute-done.2 = f32[96,128]{1,0:T(8,128)S(1)} collective-permute-done((f32[96,128]{1,0:T(8,128)S(1)}, f32[96,128]{1,0:T(8,128)S(1)}, u32[]{:S(2)}, u32[]{:S(2)}) %collective-permute-start.2) | collective-permute-done | bytes 49184 | tf_op jit(solution)/shard_map/ppermute | solution.py:375
  18.4 0.8 %collective-permute-done.3 = f32[96,128]{1,0:T(8,128)S(1)} collective-permute-done((f32[96,128]{1,0:T(8,128)S(1)}, f32[96,128]{1,0:T(8,128)S(1)}, u32[]{:S(2)}, u32[]{:S(2)}) %collective-permute-start.3) | collective-permute-done | bytes 49184 | tf_op jit(solution)/shard_map/ppermute | solution.py:375
  19.2 0.0 collective-permute-done.4
  19.2 3.2 %collective-permute-start.5 = (f32[384,128]{1,0:T(8,128)S(1)}, f32[384,128]{1,0:T(8,128)S(1)}, u32[]{:S(2)}, u32[]{:S(2)}) collective-permute-start(f32[384,128]{1,0:T(8,128)S(1)} %constant_dynamic-update-slice_fusion.mine), channel_id=1, source_target_pairs={{0,32},{32,0},{64,96},{96,64},{128,160},{160,128},{192,224},{224,1... | collective-permute-start | bytes 589832 | tf_op jit(solution)/shard_map/ppermute | solution.py:375
  22.4 1.1 %collective-permute-done.5.other = f32[384,128]{1,0:T(8,128)S(1)} collective-permute-done((f32[384,128]{1,0:T(8,128)S(1)}, f32[384,128]{1,0:T(8,128)S(1)}, u32[]{:S(2)}, u32[]{:S(2)}) %collective-permute-start.5) | collective-permute-done | bytes 196640 | tf_op jit(solution)/shard_map/ppermute | solution.py:375
  23.4 7.8 %schwarz.1 = (f32[128,128]{1,0:T(8,128)S(1)}, f32[128,128]{1,0:T(8,128)S(1)}, f32[128,128]{1,0:T(8,128)S(1)}, f32[128,128]{1,0:T(8,128)S(1)}) custom-call(s32[3]{0:T(128)S(1)} %pad_add_fusion.info, f32[384,128]{1,0:T(8,128)S(1)} %constant_dynamic-update-slice_fusion.mine, f32[384,128]{1,0:T(8,128)S(1)} %collective-permute-done.5.other), custom_call_target="tpu_custom_call" | custom-call | tf_op jit(solution)/shard_map/schwarz/pallas_call | solution.py:276
  31.3 1.4 %collective-permute-start.6 = (f32[128,128]{1,0:T(8,128)S(1)}, f32[128,128]{1,0:T(8,128)S(1)}, u32[]{:S(2)}, u32[]{:S(2)}) collective-permute-start(f32[128,128]{1,0:T(8,128)S(1)} %get-tuple-element.14), channel_id=1, source_target_pairs={{0,192},{32,224},{64,128},{96,160},{128,64},{160,96},{192,0},{224,... | collective-permute-start | bytes 196616 | tf_op jit(solution)/shard_map/ppermute | solution.py:375
  32.7 0.6 collective-permute-start.7
  33.2 1.7 %collective-permute-start.8 = (f32[128,128]{1,0:T(8,128)S(1)}, f32[128,128]{1,0:T(8,128)S(1)}, u32[]{:S(2)}, u32[]{:S(2)}) collective-permute-start(f32[128,128]{1,0:T(8,128)S(1)} %get-tuple-element.16), channel_id=1, source_target_pairs={{0,64},{32,96},{64,0},{96,32},{128,192},{160,224},{192,128},{224,1... | collective-permute-start | bytes 196616 | tf_op jit(solution)/shard_map/ppermute | solution.py:375
  34.9 1.4 %collective-permute-done.6 = f32[128,128]{1,0:T(8,128)S(1)} collective-permute-done((f32[128,128]{1,0:T(8,128)S(1)}, f32[128,128]{1,0:T(8,128)S(1)}, u32[]{:S(2)}, u32[]{:S(2)}) %collective-permute-start.6) | collective-permute-done | bytes 65568 | tf_op jit(solution)/shard_map/ppermute | solution.py:375
  36.4 3.6 %collective-permute-done.7 = f32[128,128]{1,0:T(8,128)S(1)} collective-permute-done((f32[128,128]{1,0:T(8,128)S(1)}, f32[128,128]{1,0:T(8,128)S(1)}, u32[]{:S(2)}, u32[]{:S(2)}) %collective-permute-start.7) | collective-permute-done | bytes 65568 | tf_op jit(solution)/shard_map/ppermute | solution.py:375
  40.0 0.0 collective-permute-done.8
  40.0 0.6 collective-permute-start.9
  40.6 1.2 %collective-permute-done.9.far = f32[512,128]{1,0:T(8,128)S(1)} collective-permute-done((f32[512,128]{1,0:T(8,128)S(1)}, f32[512,128]{1,0:T(8,128)S(1)}, u32[]{:S(2)}, u32[]{:S(2)}) %collective-permute-start.9) | collective-permute-done | bytes 262176 | tf_op jit(solution)/shard_map/ppermute | solution.py:375
  41.8 2.2 %place.1 = (f32[64,1024]{1,0:T(8,128)}, f32[128,128]{1,0:T(8,128)S(1)}) custom-call(s32[3]{0:T(128)S(1)} %pad_add_fusion.info, s32[8,32]{1,0:T(8,128)S(1)} %bitcast_select_fusion.index, f32[512,128]{1,0:T(8,128)S(1)} %constant_dynamic-update-slice_fusion.4.near, f32[512,128]{1,0:T(8,128)S(1)} %collective-permute-done.9.far), custom_call_target="tpu_custom_call" | custom-call | tf_op jit(solution)/shard_map/place/pallas_call | solution.py:331
  43.9 24.7 %all_to_all.5 = f32[32,4,128]{2,1,0:T(4,128)S(1)} all-to-all(f32[32,4,128]{2,1,0:T(4,128)S(1)} %bitcast.19), channel_id=1, replica_groups=mesh['gx'=8,'gy'=32] {'gy'}, dimensions={0} | all-to-all | bytes 131072 | tf_op jit(solution)/shard_map/all_to_all | solution.py:415
  68.6 0.9 %finish.1 = f32[64,256]{1,0:T(8,128)} custom-call(f32[128,128]{1,0:T(8,128)S(1)} %bitcast.18), custom_call_target="tpu_custom_call" | custom-call | tf_op jit(solution)/shard_map/finish/pallas_call | solution.py:364
  (17 shorter events, 0.1 us)
Async XLA Ops:
  1.3 0.8 %copy-start = (f32[4,16,16]{2,1,0:T(8,128)S(1)}, f32[4,16,16]{2,1,0:T(8,128)}, u32[]{:S(2)}) copy-start(f32[4,16,16]{2,1,0:T(8,128)} %conductivity.1) | copy-start | bytes 12292
  2.0 0.8 %copy-start.1 = (f32[4,16,16]{2,1,0:T(8,128)S(1)}, f32[4,16,16]{2,1,0:T(8,128)}, u32[]{:S(2)}) copy-start(f32[4,16,16]{2,1,0:T(8,128)} %storage.1) | copy-start | bytes 12292
  2.8 0.8 %copy-start.2 = (f32[4,16,16]{2,1,0:T(8,128)S(1)}, f32[4,16,16]{2,1,0:T(8,128)}, u32[]{:S(2)}) copy-start(f32[4,16,16]{2,1,0:T(8,128)} %head.1) | copy-start | bytes 12292
  3.6 0.8 %copy-start.3 = (s32[4,16,16]{2,1,0:T(8,128)S(1)}, s32[4,16,16]{2,1,0:T(8,128)}, u32[]{:S(2)}) copy-start(s32[4,16,16]{2,1,0:T(8,128)} %zone.1) | copy-start | bytes 12292
  4.4 6.1 %collective-permute-start.1 = (f32[32,128]{1,0:T(8,128)S(1)}, f32[32,128]{1,0:T(8,128)S(1)}, u32[]{:S(2)}, u32[]{:S(2)}) collective-permute-start(f32[32,128]{1,0:T(8,128)S(1)} %pack.1), channel_id=1, source_target_pairs={{1,2},{3,4},{5,6},{7,8},{9,10},{11,12},{13,14},{15,16},{17,18},{19... | collective-permute-start | bytes 49160 | tf_op jit(solution)/shard_map/ppermute | solution.py:375
  5.1 5.7 %collective-permute-start = (f32[32,128]{1,0:T(8,128)S(1)}, f32[32,128]{1,0:T(8,128)S(1)}, u32[]{:S(2)}, u32[]{:S(2)}) collective-permute-start(f32[32,128]{1,0:T(8,128)S(1)} %pack.1), channel_id=1, source_target_pairs={{0,1},{1,0},{2,3},{3,2},{4,5},{5,4},{6,7},{7,6},{8,9},{9,8},{10,11... | collective-permute-start | bytes 49160 | tf_op jit(solution)/shard_map/ppermute | solution.py:375
  9.7 0.7 copy-start.4
  9.7 0.7 copy-start.5
  10.8 8.4 %collective-permute-start.4 = (f32[96,128]{1,0:T(8,128)S(1)}, f32[96,128]{1,0:T(8,128)S(1)}, u32[]{:S(2)}, u32[]{:S(2)}) collective-permute-start(f32[96,128]{1,0:T(8,128)S(1)} %pad_maximum_fusion), channel_id=1, source_target_pairs={{0,192},{32,224},{64,128},{96,160},{128,64},{160,96},{192,0},{224,... | collective-permute-start | bytes 147464 | tf_op jit(solution)/shard_map/ppermute | solution.py:375
  15.1 4.0 %collective-permute-start.3 = (f32[96,128]{1,0:T(8,128)S(1)}, f32[96,128]{1,0:T(8,128)S(1)}, u32[]{:S(2)}, u32[]{:S(2)}) collective-permute-start(f32[96,128]{1,0:T(8,128)S(1)} %pad_maximum_fusion), channel_id=1, source_target_pairs={{0,128},{32,160},{64,192},{96,224},{128,0},{160,32},{192,64},{224,... | collective-permute-start | bytes 147464 | tf_op jit(solution)/shard_map/ppermute | solution.py:375
  15.1 3.2 %collective-permute-start.2 = (f32[96,128]{1,0:T(8,128)S(1)}, f32[96,128]{1,0:T(8,128)S(1)}, u32[]{:S(2)}, u32[]{:S(2)}) collective-permute-start(f32[96,128]{1,0:T(8,128)S(1)} %pad_maximum_fusion), channel_id=1, source_target_pairs={{0,64},{32,96},{64,0},{96,32},{128,192},{160,224},{192,128},{224,1... | collective-permute-start | bytes 147464 | tf_op jit(solution)/shard_map/ppermute | solution.py:375
  19.2 4.2 %collective-permute-start.5 = (f32[384,128]{1,0:T(8,128)S(1)}, f32[384,128]{1,0:T(8,128)S(1)}, u32[]{:S(2)}, u32[]{:S(2)}) collective-permute-start(f32[384,128]{1,0:T(8,128)S(1)} %constant_dynamic-update-slice_fusion.mine), channel_id=1, source_target_pairs={{0,32},{32,0},{64,96},{96,64},{128,160},{160,128},{192,224},{224,1... | collective-permute-start | bytes 589832 | tf_op jit(solution)/shard_map/ppermute | solution.py:375
  31.3 5.1 %collective-permute-start.6 = (f32[128,128]{1,0:T(8,128)S(1)}, f32[128,128]{1,0:T(8,128)S(1)}, u32[]{:S(2)}, u32[]{:S(2)}) collective-permute-start(f32[128,128]{1,0:T(8,128)S(1)} %get-tuple-element.14), channel_id=1, source_target_pairs={{0,192},{32,224},{64,128},{96,160},{128,64},{160,96},{192,0},{224,... | collective-permute-start | bytes 196616 | tf_op jit(solution)/shard_map/ppermute | solution.py:375
  32.7 7.3 %collective-permute-start.7 = (f32[128,128]{1,0:T(8,128)S(1)}, f32[128,128]{1,0:T(8,128)S(1)}, u32[]{:S(2)}, u32[]{:S(2)}) collective-permute-start(f32[128,128]{1,0:T(8,128)S(1)} %get-tuple-element.15), channel_id=1, source_target_pairs={{0,128},{32,160},{64,192},{96,224},{128,0},{160,32},{192,64},{224,... | collective-permute-start | bytes 196616 | tf_op jit(solution)/shard_map/ppermute | solution.py:375
  33.2 6.7 %collective-permute-start.8 = (f32[128,128]{1,0:T(8,128)S(1)}, f32[128,128]{1,0:T(8,128)S(1)}, u32[]{:S(2)}, u32[]{:S(2)}) collective-permute-start(f32[128,128]{1,0:T(8,128)S(1)} %get-tuple-element.16), channel_id=1, source_target_pairs={{0,64},{32,96},{64,0},{96,32},{128,192},{160,224},{192,128},{224,1... | collective-permute-start | bytes 196616 | tf_op jit(solution)/shard_map/ppermute | solution.py:375
  40.0 1.8 %collective-permute-start.9 = (f32[512,128]{1,0:T(8,128)S(1)}, f32[512,128]{1,0:T(8,128)S(1)}, u32[]{:S(2)}, u32[]{:S(2)}) collective-permute-start(f32[512,128]{1,0:T(8,128)S(1)} %constant_dynamic-update-slice_fusion.4.near), channel_id=1, source_target_pairs={{0,32},{32,0},{64,96},{96,64},{128,160},{160,128},{192,224},{224,1... | collective-permute-start | bytes 786440 | tf_op jit(solution)/shard_map/ppermute | solution.py:375
